TPU v7x, 32 devices: a whole 2x2x4 slice. The times are simulated.
32 devices in a mesh: rhs: 8 (over z, x), clus: 4 (over y, core).
Axes of the slice: x: 2, y: 2, z: 4, core: 2. Of those that a mesh axis runs over, the one named last changes fastest.
Arguments:
- incident: bfloat16 [832, 32768], P('rhs', 'clus'), may hold values from -6 to 6
- v_factors: bfloat16 [20, 2048, 128], P('clus', 'rhs'), may hold values from -0.125 to 0.125
- u_factors: bfloat16 [40, 2048, 128], P('clus', 'rhs'), may hold values from -0.5 to 0.5
- block_source: int32 [20], P('clus'), may hold values from 0 to 3
- block_rank: int32 [20], P('clus'), may hold values from 16 to 128
- block_slot: int32 [20], P('clus'), may hold values from 0 to 39, as said below
- slot_target: int32 [40], P('clus'), may hold values from 0 to 3
Outputs:
- scattered: bfloat16 [832, 32768], P('rhs', 'clus')
Inputs may be any that keep to these rules, and one draw needn't show every extreme that they name: `block_slot`: every value is a slot number, all 20 values are distinct, and slot v belongs to index v // 10 of clus. The 5 blocks of one index of clus name at most 3 slots of any one index, and in every draw some index sends exactly 3 to one index and some index of clus receives exactly 10 blocks. Which slots stay empty varies.
All inputs are finite; a program needn't handle non-finite values.
Results may differ from a plain program's by a relative error of at most 0.0049.
Values may be sent and summed in bfloat16 or wider, within the bound.
No kernel may reach another device: no remote copies, remote signals or barrier semaphores. Data moves between devices by JAX's collectives and lax.ppermute only.
A program may use at most 64 MiB of HBM per device.

v0:
```python
import jax
import jax.numpy as jnp
from jax import lax
from jax.sharding import PartitionSpec as P


def local(incident, v_factors, u_factors, block_source, block_rank, block_slot, slot_target):
    columns = incident.shape[0]
    blocks = v_factors.shape[0]
    rank_max = v_factors.shape[2]
    capacity = u_factors.shape[0]
    devices = lax.axis_size("clus")
    cluster_len = v_factors.shape[1] * lax.axis_size("rhs")
    local_clusters = incident.shape[1] // cluster_len
    per_peer = max(1, (2 * blocks + devices - 1) // devices)
    sources = jnp.take(incident.reshape(columns, local_clusters, cluster_len), block_source, axis=1)
    compressed = jnp.einsum(
        "cbr,brk->bck",
        sources,
        lax.all_gather(v_factors, "rhs", axis=1, tiled=True),
        preferred_element_type=jnp.float32,
    )
    rank_index = lax.broadcasted_iota(jnp.int32, (blocks, 1, rank_max), 2)
    compressed = jnp.where(rank_index < block_rank[:, None, None], compressed, 0.0).astype(
        jnp.bfloat16
    )
    target_dev = block_slot // capacity
    target_pos = block_slot % capacity
    later_index = lax.broadcasted_iota(jnp.int32, (blocks, blocks), 0)
    earlier_index = lax.broadcasted_iota(jnp.int32, (blocks, blocks), 1)
    same_target = target_dev[None, :] == target_dev[:, None]
    before = jnp.sum((same_target & (earlier_index < later_index)).astype(jnp.int32), axis=1)
    position = target_dev * per_peer + before
    places = lax.broadcasted_iota(jnp.int32, (blocks, devices * per_peer), 1)
    placed = position[:, None] == places
    outgoing = jnp.einsum(
        "bp,bck->pck", placed.astype(jnp.bfloat16), compressed, preferred_element_type=jnp.float32
    ).astype(jnp.bfloat16)
    labels = jnp.sum(jnp.where(placed, target_pos[:, None] + 1, 0), axis=0) - 1
    arrived, arrived_labels = (
        lax.all_to_all(outgoing, "clus", split_axis=0, concat_axis=0, tiled=True),
        lax.all_to_all(labels, "clus", split_axis=0, concat_axis=0, tiled=True),
    )
    slot_ids = lax.broadcasted_iota(jnp.int32, (devices * per_peer, capacity), 1)
    landing = (arrived_labels[:, None] == slot_ids).astype(jnp.bfloat16)
    slot_rows = jnp.einsum(
        "pj,pck->jck", landing, arrived, preferred_element_type=jnp.float32
    ).astype(jnp.bfloat16)
    cluster_ids = lax.broadcasted_iota(jnp.int32, (capacity, local_clusters), 1)
    owners = (slot_target[:, None] == cluster_ids).astype(jnp.float32)
    products = jnp.einsum(
        "jck,jrk->jcr",
        slot_rows,
        lax.all_gather(u_factors, "rhs", axis=1, tiled=True),
        preferred_element_type=jnp.float32,
    )
    summed = jnp.einsum("jt,jcr->ctr", owners, products, precision=lax.Precision.HIGHEST)
    return summed.reshape(columns, local_clusters * cluster_len).astype(jnp.bfloat16)


def solution(mesh):
    placed = (
        P("rhs", "clus"),
        P("clus", "rhs", None),
        P("clus", "rhs", None),
        P("clus"),
        P("clus"),
        P("clus"),
        P("clus"),
    )
    return jax.shard_map(
        local, mesh=mesh, in_specs=placed, out_specs=P("rhs", "clus"), check_vma=False
    )
```

profile of v0, /device:TPU:0, one launch (start us, length us, event | category | flops | bytes accessed | tf_op | source)
XLA Modules:
  0.0 182.1 jit_solution(14479420949571712537)
XLA Ops:
  6.5 0.0 all-gather.3.cloned.1.call-start
  6.5 0.7 all-gather.3.cloned.1.call-update
  7.3 0.0 all-gather.5.cloned.1.call-start
  7.3 0.7 all-gather.5.cloned.1.call-update
  8.0 0.7 fusion.30
  8.7 0.2 convert_reduce_fusion
  8.9 0.1 select_reduce_fusion
  9.0 0.6 sub.11
  9.6 4.2 %all-to-all-start = ((s32[4,3,1]{1,2,0:T(1,128)}), s32[4,3,1]{1,2,0:T(1,128)S(1)}, u32[]{:S(2)}, u32[]{:S(2)}) async-start(s32[4,3,1]{1,2,0:T(1,128)} %bitcast), calls=%async_computation | async-start | bytes 4096 | tf_op jit(solution)/shard_map/all_to_all | solution.py:42
  13.8 1.6 copy.39
  15.4 0.0 copy-done.1
  15.4 0.0 copy-start.2
  15.4 2.2 %gather_fusion = bf16[5,104,2048]{2,1,0:T(8,128)(2,1)} fusion(bf16[104,4,2048]{2,0,1:T(8,128)(2,1)S(1)} %bitcast.27, s32[1024]{0:T(1024)S(1)} %pad_clamp_fusion), kind=kCustom, calls=%fused_computation | custom fusion | bytes 4259860 | tf_op jit(solution)/shard_map/jit(_take)/gather | solution.py:16
  17.6 0.0 copy-done.2
  17.6 0.1 iota_compare_fusion.1
  17.7 49.2 %all-gather.3.cloned.1.call-done = bf16[5,2048,128]{2,1,0:T(8,128)(2,1)} async-done(((bf16[5,256,128]{2,1,0:T(8,128)(2,1)}), bf16[5,2048,128]{2,1,0:T(8,128)(2,1)}) %all-gather.3.cloned.1.call-update) | async-done | bytes 2621456 | tf_op jit(solution)/shard_map/all_gather | solution.py:20
  66.9 3.3 %fusion.12 = bf16[5,104,128]{2,1,0:T(8,128)(2,1)S(1)} fusion(bf16[5,2048,128]{2,1,0:T(8,128)(2,1)} %all-gather.3.cloned.1.call-done, bf16[5,104,2048]{2,1,0:T(8,128)(2,1)} %gather_fusion, pred[5]{0:T(512)(128)(4,1)S(1)} %compare_and_fusion, pred[5,128]{1,0:T(8,128)(4,1)S(1)} %iota_compare_fusion.1), kind=kOutput, calls=%fused_computation.12 | convolution fusion | flops 273827840 | bytes 4885125 | tf_op jit(solution)/shard_map/cbr,brk->bck/dot_general | solution.py:17
  70.3 0.4 convolution_convert_fusion
  70.7 0.8 copy.22
  71.5 0.0 all-to-all-done
  71.5 3.5 %all-to-all-start.1 = ((bf16[12,104,128]{2,1,0:T(8,128)(2,1)}), bf16[12,104,128]{2,1,0:T(8,128)(2,1)S(1)}, u32[]{:S(2)}, u32[]{:S(2)}) async-start(bf16[12,104,128]{2,1,0:T(8,128)(2,1)} %copy.22), calls=%async_computation.1 | async-start | bytes 638976 | tf_op jit(solution)/shard_map/all_to_all | solution.py:41
  75.0 0.5 broadcast.81
  75.5 0.6 reduce.3
  76.1 0.1 eq.46
  76.2 5.4 %all-to-all-done.1 = bf16[12,104,128]{2,1,0:T(8,128)(2,1)S(1)} async-done(((bf16[12,104,128]{2,1,0:T(8,128)(2,1)}), bf16[12,104,128]{2,1,0:T(8,128)(2,1)S(1)}, u32[]{:S(2)}, u32[]{:S(2)}) %all-to-all-start.1) | async-done | bytes 319520 | tf_op jit(solution)/shard_map/all_to_all | solution.py:41
  81.6 0.3 convolution_convert_fusion.1
  81.9 0.0 copy-start
  81.9 72.1 %all-gather.5.cloned.1.call-done = bf16[10,2048,128]{2,1,0:T(8,128)(2,1)} async-done(((bf16[10,256,128]{2,1,0:T(8,128)(2,1)}), bf16[10,2048,128]{2,1,0:T(8,128)(2,1)}) %all-gather.5.cloned.1.call-update) | async-done | bytes 5242896 | tf_op jit(solution)/shard_map/all_gather | solution.py:54
  154.0 5.8 %fusion.17 = f32[10,104,2048]{2,1,0:T(8,128)S(1)} fusion(bf16[10,2048,128]{2,1,0:T(8,128)(2,1)} %all-gather.5.cloned.1.call-done, bf16[10,104,128]{2,0,1:T(8,128)(2,1)S(1)} %convolution_convert_fusion.1), kind=kOutput, calls=%fused_computation.15 | convolution fusion | flops 545259520 | bytes 14028800 | tf_op jit(solution)/shard_map/jck,jrk->jcr/dot_general | solution.py:51
  159.8 0.0 copy-done
  159.8 13.1 %fusion.2 = bf16[104,2048,4]{1,2,0:T(4,128)(2,1)S(1)} fusion(f32[10,104,2048]{2,1,0:T(8,128)S(1)} %fusion.17, s32[10]{0:T(128)S(1)} %copy-done), kind=kOutput, calls=%fused_computation.3 | convolution fusion | flops 103088168 | bytes 10223656 | tf_op jit(solution)/shard_map/jt,jcr->ctr/dot_general | solution.py:57
  172.9 2.3 %copy.27 = bf16[13,8,4,2048]{3,1,2,0:T(8,128)(2,1)} copy(bf16[13,8,4,2048]{3,2,1,0:T(4,128)(2,1)S(1)} %bitcast.28) | data formatting | bytes 3407872
  (6 shorter events, 0.0 us)
Async XLA Ops:
  6.5 8.8 %copy-start.1 = (s32[5]{0:T(128)S(1)}, s32[5]{0:T(128)}, u32[]{:S(2)}) copy-start(s32[5]{0:T(128)} %param.10) | copy-start | bytes 64
  6.5 60.4 %all-gather.3.cloned.1.call-start = ((), (), s32[]{:S(2)}) async-start(), calls=%async_computation.2 | async-start | bytes 2949120 | tf_op jit(solution)/shard_map/all_gather | solution.py:20
  7.3 146.7 %all-gather.5.cloned.1.call-start = ((), (), s32[]{:S(2)}) async-start(), calls=%async_computation.3 | async-start | bytes 5898240 | tf_op jit(solution)/shard_map/all_gather | solution.py:54
  9.6 61.9 %all-to-all-start = ((s32[4,3,1]{1,2,0:T(1,128)}), s32[4,3,1]{1,2,0:T(1,128)S(1)}, u32[]{:S(2)}, u32[]{:S(2)}) async-start(s32[4,3,1]{1,2,0:T(1,128)} %bitcast), calls=%async_computation | async-start | bytes 4096 | tf_op jit(solution)/shard_map/all_to_all | solution.py:42
  15.4 2.2 %copy-start.2 = (s32[5]{0:T(128)S(1)}, s32[5]{0:T(128)}, u32[]{:S(2)}) copy-start(s32[5]{0:T(128)} %param.11) | copy-start | bytes 64
  71.5 10.1 %all-to-all-start.1 = ((bf16[12,104,128]{2,1,0:T(8,128)(2,1)}), bf16[12,104,128]{2,1,0:T(8,128)(2,1)S(1)}, u32[]{:S(2)}, u32[]{:S(2)}) async-start(bf16[12,104,128]{2,1,0:T(8,128)(2,1)} %copy.22), calls=%async_computation.1 | async-start | bytes 638976 | tf_op jit(solution)/shard_map/all_to_all | solution.py:41
  81.9 77.9 %copy-start = (s32[10]{0:T(128)S(1)}, s32[10]{0:T(128)}, u32[]{:S(2)}) copy-start(s32[10]{0:T(128)} %param.13) | copy-start | bytes 124
Sparse Core Ops, SparseCore 0:
  9.5 57.3 all-gather.2
  69.1 84.8 all-gather.4
where the time goes:
time: 182 us
  waiting for transfers between devices  128 us (70%)
  matrix products  22.9 us (13%)
  between operations  13.5 us (7%)
  local copies, waits for them, and re-layouts  8.1 us (4%)
  starting transfers between devices  7.73 us (4%)
    all_gather x1, waiting for transfers between devices, local(): lax.all_gather(u_factors, 'rhs', axis=1, tiled=True)  72.1 us
    all_gather x1, waiting for transfers between devices, local(): lax.all_gather(v_factors, 'rhs', axis=1, tiled=True)  49.2 us
    dot_general x1, matrix products, local(): jnp.einsum('jt,jcr->ctr', owners, products, precision=lax.Precision.HIGHEST)  13.1 us
    dot_general x1, matrix products, local(): jnp.einsum('jck,jrk->jcr', slot_rows, lax.all_gather(u_factors, 'rhs', ax...  5.76 us
    all_to_all x1, waiting for transfers between devices, local(): lax.all_to_all(outgoing, 'clus', split_axis=0, concat_axis=0, tiled=True)  5.42 us
    all_to_all x1, starting transfers between devices, local(): lax.all_to_all(labels, 'clus', split_axis=0, concat_axis=0, tiled=True)  4.24 us
  transfers between devices with their start and end apart: 4, of which 3 were waited for; matrix products, arithmetic and copies ran while one was open for 6% of the time, Pallas kernels for 0%

commit v1 on v0

--- a/solution.py
+++ b/solution.py
@@ -1,10 +1,179 @@
+import functools
+
 import jax
 import jax.numpy as jnp
 from jax import lax
+from jax.experimental import pallas as pl
+from jax.experimental.pallas import tpu as pltpu
 from jax.sharding import PartitionSpec as P
 
-
-def local(incident, v_factors, u_factors, block_source, block_rank, block_slot, slot_target):
+VMEM = pl.BlockSpec(memory_space=pltpu.VMEM)
+SMEM = pl.BlockSpec(memory_space=pltpu.SMEM)
+LIMIT = 32 * 1024 * 1024
+
+
+def call(body, out_shape, in_specs, name, flops=0, moved=0, scratch=()):
+    out_specs = [VMEM] * len(out_shape) if isinstance(out_shape, list) else VMEM
+    return pl.pallas_call(
+        body,
+        out_shape=out_shape,
+        in_specs=in_specs,
+        out_specs=out_specs,
+        scratch_shapes=list(scratch),
+        compiler_params=pltpu.CompilerParams(vmem_limit_bytes=LIMIT),
+        cost_estimate=pl.CostEstimate(flops=flops, bytes_accessed=moved, transcendentals=0),
+        name=name,
+    )
+
+
+def pack_body(seg, pos_ref, x_ref, out_ref):
+    half = 1 - pos_ref[0]
+    for piece in range(out_ref.shape[1] // seg):
+        start = pl.multiple_of((2 * piece + half) * seg, seg)
+        out_ref[:, piece * seg : (piece + 1) * seg] = x_ref[:, pl.ds(start, seg)]
+
+
+def compress_body(seg, outer, pos_ref, source_ref, x_ref, xn_ref, *refs):
+    shards, out_ref = refs[:-1], refs[-1]
+    half, mine = pos_ref[0], pos_ref[1]
+    for block in range(out_ref.shape[0]):
+        source = source_ref[block]
+        own = jnp.zeros(out_ref.shape[2:], jnp.float32)
+        other = jnp.zeros(out_ref.shape[2:], jnp.float32)
+        for shift, shard in enumerate(shards):
+            place = lax.rem(mine - shift + outer, outer)
+            here = pl.multiple_of(((source * outer + place) * 2 + half) * seg, seg)
+            there = pl.multiple_of((source * outer + place) * seg, seg)
+            rows = shard[block]
+            own += jnp.dot(x_ref[:, pl.ds(here, seg)], rows, preferred_element_type=jnp.float32)
+            other += jnp.dot(xn_ref[:, pl.ds(there, seg)], rows, preferred_element_type=jnp.float32)
+        out_ref[block, half] = own
+        out_ref[block, 1 - half] = other
+
+
+def expand_body(seg, pos_ref, index_ref, target_ref, comp_ref, u_ref, own_ref, other_ref, acc):
+    half = pos_ref[0]
+    acc[...] = jnp.zeros_like(acc)
+    for slot in range(u_ref.shape[0]):
+        block = index_ref[slot]
+
+        @pl.when(block >= 0)
+        def _():
+            target = target_ref[slot]
+            rows = u_ref[slot]
+            for side in range(2):
+                acc[target, side] += lax.dot_general(
+                    comp_ref[block, side],
+                    rows,
+                    (((1,), (1,)), ((), ())),
+                    preferred_element_type=jnp.float32,
+                )
+
+    for target in range(acc.shape[0]):
+        span = slice(target * seg, (target + 1) * seg)
+        own_ref[:, span] = acc[target, half].astype(own_ref.dtype)
+        other_ref[:, span] = acc[target, 1 - half].astype(other_ref.dtype)
+
+
+def join_body(seg, outer, clusters, pos_ref, *refs):
+    out_ref = refs[-1]
+    half, mine = pos_ref[0], pos_ref[1]
+    for shift in range(outer):
+        place = lax.rem(mine - shift + outer, outer)
+        for target in range(clusters):
+            span = slice(target * seg, (target + 1) * seg)
+            base = (target * outer + place) * 2
+            here = pl.multiple_of((base + half) * seg, seg)
+            there = pl.multiple_of((base + 1 - half) * seg, seg)
+            out_ref[:, pl.ds(here, seg)] = refs[shift][:, span]
+            out_ref[:, pl.ds(there, seg)] = refs[outer + shift][:, span]
+
+
+def after(value, *first):
+    return lax.optimization_barrier((value, *first))[0]
+
+
+def paired(incident, v_factors, u_factors, block_source, block_rank, block_slot, slot_target):
+    columns, width = incident.shape
+    blocks, seg, rank_max = v_factors.shape
+    capacity = u_factors.shape[0]
+    places, owners = lax.axis_size("rhs"), lax.axis_size("clus")
+    outer = places // 2
+    clusters = width // (seg * places)
+    me, owner = lax.axis_index("rhs"), lax.axis_index("clus")
+    position = jnp.stack([me % 2, me // 2]).astype(jnp.int32)
+
+    across = [(p, p ^ 1) for p in range(places)]
+
+    def along(array, shift):
+        return lax.ppermute(
+            array,
+            "rhs",
+            [(p, (p // 2 + shift) % outer * 2 + p % 2) for p in range(places)],
+        )
+
+    def to_owner(array, shift):
+        return lax.ppermute(array, "clus", [(p, (p + shift) % owners) for p in range(owners)])
+
+    v_shards = [v_factors] + [along(v_factors, s) for s in range(1, outer)]
+    packed = call(
+        functools.partial(pack_body, seg),
+        jax.ShapeDtypeStruct((columns, width // 2), incident.dtype),
+        [SMEM, VMEM],
+        "pack",
+        moved=3 * columns * width,
+    )(position, incident)
+    x_other = lax.ppermute(packed, "rhs", across)
+    slots = jnp.concatenate([block_slot] + [to_owner(block_slot, s) for s in range(1, owners)])
+    u_shards = [u_factors] + [along(after(u_factors, v_shards[s]), s) for s in range(1, outer)]
+
+    partial = call(
+        functools.partial(compress_body, seg, outer),
+        jax.ShapeDtypeStruct((blocks, 2, columns, rank_max), jnp.float32),
+        [SMEM, SMEM] + [VMEM] * (2 + outer),
+        "compress",
+        flops=4 * blocks * columns * seg * outer * rank_max,
+        moved=3 * columns * width + 2 * outer * v_factors.size,
+    )(position, block_source, incident, x_other, *v_shards)
+    rank_index = lax.broadcasted_iota(jnp.int32, (blocks, 1, 1, rank_max), 3)
+    compressed = jnp.where(
+        rank_index < block_rank[:, None, None, None],
+        partial + lax.ppermute(partial, "rhs", across),
+        0.0,
+    ).astype(jnp.bfloat16)
+    gathered = jnp.concatenate(
+        [compressed] + [to_owner(compressed, s) for s in range(1, owners)], axis=0
+    )
+    wanted = owner * capacity + lax.broadcasted_iota(jnp.int32, (capacity, slots.shape[0]), 0)
+    order = lax.broadcasted_iota(jnp.int32, (capacity, slots.shape[0]), 1)
+    feeding = jnp.max(jnp.where(wanted == slots[None, :], order, -1), axis=1)
+
+    chunk = jax.ShapeDtypeStruct((columns, clusters * seg), jnp.bfloat16)
+    own_parts, other_parts = [], []
+    for shard in u_shards:
+        own, other = call(
+            functools.partial(expand_body, seg),
+            [chunk, chunk],
+            [SMEM, SMEM, SMEM, VMEM, VMEM],
+            "expand",
+            flops=4 * capacity * columns * seg * rank_max,
+            moved=2 * shard.size + 2 * gathered.size + 4 * columns * clusters * seg,
+            scratch=[pltpu.VMEM((clusters, 2, columns, seg), jnp.float32)],
+        )(position, feeding, slot_target, gathered, shard)
+        own_parts.append(own)
+        other_parts.append(lax.ppermute(other, "rhs", across))
+    return call(
+        functools.partial(join_body, seg, outer, clusters),
+        jax.ShapeDtypeStruct((columns, width), jnp.bfloat16),
+        [SMEM] + [VMEM] * (2 * outer),
+        "join",
+        moved=4 * columns * width,
+    )(position, *own_parts, *other_parts)
+
+
+def gathered_plan(
+    incident, v_factors, u_factors, block_source, block_rank, block_slot, slot_target
+):
     columns = incident.shape[0]
     blocks = v_factors.shape[0]
     rank_max = v_factors.shape[2]
@@ -58,6 +227,11 @@
     return summed.reshape(columns, local_clusters * cluster_len).astype(jnp.bfloat16)
 
 
+def local(incident, v_factors, *rest):
+    plan = paired if v_factors.shape[1] % 128 == 0 else gathered_plan
+    return plan(incident, v_factors, *rest)
+
+
 def solution(mesh):
     placed = (
         P("rhs", "clus"),

time: 182 us -> 129 us (0.71)
  the two profiles are of different devices: /device:TPU:0 before, /device:TPU:29 now
where the time goes in v1:
time: 129 us
  waiting for transfers between devices  94.4 us (73%)
  starting transfers between devices  18.1 us (14%)
  Pallas kernels  13.8 us (11%)
  local copies, waits for them, and re-layouts  1.48 us (1%)
    ppermute x6, waiting for transfers between devices, along(): lax.ppermute(array, 'rhs', [(p, (p // 2 + shift) % outer * 2 + p % 2) for...  60.3 us
    ppermute x6, waiting for transfers between devices, to_owner(): lax.ppermute(array, 'clus', [(p, (p + shift) % owners) for p in range(own...  13.8 us
    ppermute x1, waiting for transfers between devices, paired(): lax.ppermute(partial, 'rhs', across)  11.4 us
    pallas_call x4, Pallas kernels, paired(): call(functools.partial(expand_body, seg), [chunk, chunk], [SMEM, SMEM, SM...  9.85 us
    ppermute x4, waiting for transfers between devices, paired(): other_parts.append(lax.ppermute(other, 'rhs', across))  8.93 us
    ppermute x6, starting transfers between devices, to_owner(): lax.ppermute(array, 'clus', [(p, (p + shift) % owners) for p in range(own...  8.89 us
    ppermute x6, starting transfers between devices, along(): lax.ppermute(array, 'rhs', [(p, (p // 2 + shift) % outer * 2 + p % 2) for...  5.41 us
  transfers between devices with their start and end apart: 18, of which 12 were waited for; matrix products, arithmetic and copies ran while one was open for 0% of the time, Pallas kernels for 8%

profile of v1, /device:TPU:29, one launch (start us, length us, event | category | flops | bytes accessed | tf_op | source)
XLA Modules:
  0.0 128.5 jit_solution(15149034781635232256)
XLA Ops:
  0.1 1.5 %copy-done = bf16[104,8192]{1,0:T(8,128)(2,1)S(1)} copy-done((bf16[104,8192]{1,0:T(8,128)(2,1)S(1)}, bf16[104,8192]{1,0:T(8,128)(2,1)}, u32[]{:S(2)}) %copy-start) | copy-done | bytes 1703960
  1.5 0.7 pack.1
  2.2 1.3 collective-permute-start.3
  3.5 1.3 %collective-permute-start.5 = (bf16[5,256,128]{2,1,0:T(8,128)(2,1)S(1)}, bf16[5,256,128]{2,1,0:T(8,128)(2,1)S(1)}, u32[]{:S(2)}, u32[]{:S(2)}) collective-permute-start(bf16[5,256,128]{2,1,0:T(8,128)(2,1)S(1)} %copy-done.2), channel_id=1, source_target_pairs={{0,16},{4,20},{8,24},{12,28},{16,0},{20,4},{24,8},{28,12},{1,17},{... | collective-permute-start | bytes 983048 | tf_op jit(solution)/shard_map/ppermute | solution.py:109
  5.0 6.7 %collective-permute-done.4.refs_1_ = bf16[5,256,128]{2,1,0:T(8,128)(2,1)S(1)} collective-permute-done((bf16[5,256,128]{2,1,0:T(8,128)(2,1)S(1)}, bf16[5,256,128]{2,1,0:T(8,128)(2,1)S(1)}, u32[]{:S(2)}, u32[]{:S(2)}) %collective-permute-start.4) | collective-permute-done | bytes 327712 | tf_op jit(solution)/shard_map/ppermute | solution.py:109
  11.8 21.0 %collective-permute-done.5.refs_2_ = bf16[5,256,128]{2,1,0:T(8,128)(2,1)S(1)} collective-permute-done((bf16[5,256,128]{2,1,0:T(8,128)(2,1)S(1)}, bf16[5,256,128]{2,1,0:T(8,128)(2,1)S(1)}, u32[]{:S(2)}, u32[]{:S(2)}) %collective-permute-start.5) | collective-permute-done | bytes 327712 | tf_op jit(solution)/shard_map/ppermute | solution.py:109
  32.7 1.3 %compress.1 = f32[5,2,104,128]{3,2,1,0:T(8,128)S(1)} custom-call(s32[2]{0:T(128)S(1)} %pad_add_fusion.pos_ref, s32[5]{0:T(128)S(1)} %copy-done.4, bf16[104,8192]{1,0:T(8,128)(2,1)S(1)} %copy-done, bf16[104,4096]{1,0:T(8,128)(2,1)S(1)} %collective-permute-done.3.xn_ref, bf16[5,256,128]{2,1,0:T(8,128)(2,1)S(1)} %copy-done.2, ...), custom_call_target="tpu_custom_call" | custom-call | flops 272629760 | bytes 3866624 | tf_op jit(solution)/shard_map/compress/pallas_call | solution.py:130
  34.4 11.4 %collective-permute-done.7 = f32[5,2,104,128]{3,2,1,0:T(8,128)S(1)} collective-permute-done((f32[5,2,104,128]{3,2,1,0:T(8,128)S(1)}, f32[5,2,104,128]{3,2,1,0:T(8,128)S(1)}, u32[]{:S(2)}, u32[]{:S(2)}) %collective-permute-start.7) | collective-permute-done | bytes 532512 | tf_op jit(solution)/shard_map/ppermute | solution.py:141
  45.9 2.8 %collective-permute-start.10 = (bf16[5,2,104,128]{3,2,1,0:T(8,128)(2,1)S(1)}, bf16[5,2,104,128]{3,2,1,0:T(8,128)(2,1)S(1)}, u32[]{:S(2)}, u32[]{:S(2)}) collective-permute-start(bf16[5,2,104,128]{3,2,1,0:T(8,128)(2,1)S(1)} %select_convert_fusion), channel_id=1, source_target_pairs={{0,3},{1,0},{2,1},{3,2},{4,7},{5,4},{6,5},{7,6},{8,11},{9,8},{10,9... | collective-permute-start | bytes 798728 | tf_op jit(solution)/shard_map/ppermute | solution.py:116
  48.8 2.4 %collective-permute-start.12 = (bf16[10,256,128]{2,1,0:T(8,128)(2,1)S(1)}, bf16[10,256,128]{2,1,0:T(8,128)(2,1)S(1)}, u32[]{:S(2)}, u32[]{:S(2)}) collective-permute-start(bf16[10,256,128]{2,1,0:T(8,128)(2,1)S(1)} %copy-done.1), channel_id=1, source_target_pairs={{0,16},{4,20},{8,24},{12,28},{16,0},{20,4},{24,8},{28,12},{1,17},{... | collective-permute-start | bytes 1966088 | tf_op jit(solution)/shard_map/ppermute | solution.py:109
  51.2 1.5 %collective-permute-start.13 = (bf16[10,256,128]{2,1,0:T(8,128)(2,1)S(1)}, bf16[10,256,128]{2,1,0:T(8,128)(2,1)S(1)}, u32[]{:S(2)}, u32[]{:S(2)}) collective-permute-start(bf16[10,256,128]{2,1,0:T(8,128)(2,1)S(1)} %copy-done.1), channel_id=1, source_target_pairs={{0,24},{4,28},{8,0},{12,4},{16,8},{20,12},{24,16},{28,20},{1,25},{... | collective-permute-start | bytes 1966088 | tf_op jit(solution)/shard_map/ppermute | solution.py:109
  52.7 1.2 collective-permute-start
  53.9 0.7 collective-permute-done
  54.6 1.0 collective-permute-start.1
  55.7 1.7 %collective-permute-done.1 = s32[5]{0:T(128)S(1)} collective-permute-done((s32[5]{0:T(128)S(1)}, s32[5]{0:T(128)S(1)}, u32[]{:S(2)}, u32[]{:S(2)}) %collective-permute-start.1) | collective-permute-done | bytes 52 | tf_op jit(solution)/shard_map/ppermute | solution.py:116
  57.3 2.8 %collective-permute-start.2 = (s32[5]{0:T(128)S(1)}, s32[5]{0:T(128)S(1)}, u32[]{:S(2)}, u32[]{:S(2)}) collective-permute-start(s32[5]{0:T(128)S(1)} %copy-done.5), channel_id=1, source_target_pairs={{0,3},{1,0},{2,1},{3,2},{4,7},{5,4},{6,5},{7,6},{8,11},{9,8},{10,9... | collective-permute-start | bytes 68 | tf_op jit(solution)/shard_map/ppermute | solution.py:116
  60.1 1.9 %collective-permute-done.2 = s32[5]{0:T(128)S(1)} collective-permute-done((s32[5]{0:T(128)S(1)}, s32[5]{0:T(128)S(1)}, u32[]{:S(2)}, u32[]{:S(2)}) %collective-permute-start.2) | collective-permute-done | bytes 52 | tf_op jit(solution)/shard_map/ppermute | solution.py:116
  61.9 1.0 collective-permute-start.9
  63.2 2.9 %collective-permute-done.8 = bf16[5,2,104,128]{3,2,1,0:T(8,128)(2,1)S(1)} collective-permute-done((bf16[5,2,104,128]{3,2,1,0:T(8,128)(2,1)S(1)}, bf16[5,2,104,128]{3,2,1,0:T(8,128)(2,1)S(1)}, u32[]{:S(2)}, u32[]{:S(2)}) %collective-permute-start.8) | collective-permute-done | bytes 266272 | tf_op jit(solution)/shard_map/ppermute | solution.py:116
  66.1 6.7 %collective-permute-done.9 = bf16[5,2,104,128]{3,2,1,0:T(8,128)(2,1)S(1)} collective-permute-done((bf16[5,2,104,128]{3,2,1,0:T(8,128)(2,1)S(1)}, bf16[5,2,104,128]{3,2,1,0:T(8,128)(2,1)S(1)}, u32[]{:S(2)}, u32[]{:S(2)}) %collective-permute-start.9) | collective-permute-done | bytes 266272 | tf_op jit(solution)/shard_map/ppermute | solution.py:116
  72.9 2.5 %expand.5 = (bf16[104,1024]{1,0:T(8,128)(2,1)S(1)}, bf16[104,1024]{1,0:T(8,128)(2,1)S(1)}) custom-call(s32[2]{0:T(128)S(1)} %pad_add_fusion.pos_ref, s32[10]{0:T(128)S(1)} %select_reduce_fusion.index_ref, s32[10]{0:T(128)S(1)} %copy-done.3, bf16[20,2,104,128]{3,2,1,0:T(8,128)(2,1)S(1)} %pad_maximum_fusion.comp_ref, ...), custom_call_target="tpu_custom_call" | custom-call | flops 136314880 | bytes 2146304 | tf_op jit(solution)/shard_map/expand/pallas_call | solution.py:154
  75.4 0.3 collective-permute-start.15
  75.7 32.6 %collective-permute-done.12.u_ref = bf16[10,256,128]{2,1,0:T(8,128)(2,1)S(1)} collective-permute-done((bf16[10,256,128]{2,1,0:T(8,128)(2,1)S(1)}, bf16[10,256,128]{2,1,0:T(8,128)(2,1)S(1)}, u32[]{:S(2)}, u32[]{:S(2)}) %collective-permute-start.12) | collective-permute-done | bytes 655392 | tf_op jit(solution)/shard_map/ppermute | solution.py:109
  108.4 2.5 %expand.6 = (bf16[104,1024]{1,0:T(8,128)(2,1)S(1)}, bf16[104,1024]{1,0:T(8,128)(2,1)S(1)}) custom-call(s32[2]{0:T(128)S(1)} %pad_add_fusion.pos_ref, s32[10]{0:T(128)S(1)} %select_reduce_fusion.index_ref, s32[10]{0:T(128)S(1)} %copy-done.3, bf16[20,2,104,128]{3,2,1,0:T(8,128)(2,1)S(1)} %pad_maximum_fusion.comp_ref, ...), custom_call_target="tpu_custom_call" | custom-call | flops 136314880 | bytes 2146304 | tf_op jit(solution)/shard_map/expand/pallas_call | solution.py:154
  110.8 0.3 collective-permute-start.16
  111.2 2.5 %expand.4 = (bf16[104,1024]{1,0:T(8,128)(2,1)S(1)}, bf16[104,1024]{1,0:T(8,128)(2,1)S(1)}) custom-call(s32[2]{0:T(128)S(1)} %pad_add_fusion.pos_ref, s32[10]{0:T(128)S(1)} %select_reduce_fusion.index_ref, s32[10]{0:T(128)S(1)} %copy-done.3, bf16[20,2,104,128]{3,2,1,0:T(8,128)(2,1)S(1)} %pad_maximum_fusion.comp_ref, bf16[10,256,128]{2,1,0:T(8,128)(2,1)S(1)} %copy-done.1), custom_call_target="tpu_custom_call" | custom-call | flops 136314880 | bytes 2146304 | tf_op jit(solution)/shard_map/expand/pallas_call | solution.py:154
  113.6 2.5 %expand.7 = (bf16[104,1024]{1,0:T(8,128)(2,1)S(1)}, bf16[104,1024]{1,0:T(8,128)(2,1)S(1)}) custom-call(s32[2]{0:T(128)S(1)} %pad_add_fusion.pos_ref, s32[10]{0:T(128)S(1)} %select_reduce_fusion.index_ref, s32[10]{0:T(128)S(1)} %copy-done.3, bf16[20,2,104,128]{3,2,1,0:T(8,128)(2,1)S(1)} %pad_maximum_fusion.comp_ref, ...), custom_call_target="tpu_custom_call" | custom-call | flops 136314880 | bytes 2146304 | tf_op jit(solution)/shard_map/expand/pallas_call | solution.py:154
  116.1 1.3 collective-permute-start.17
  117.6 0.4 collective-permute-done.16.refs_6_
  118.1 5.4 %collective-permute-done.17.refs_7_ = bf16[104,1024]{1,0:T(8,128)(2,1)S(1)} collective-permute-done((bf16[104,1024]{1,0:T(8,128)(2,1)S(1)}, bf16[104,1024]{1,0:T(8,128)(2,1)S(1)}, u32[]{:S(2)}, u32[]{:S(2)}) %collective-permute-start.17) | collective-permute-done | bytes 213024 | tf_op jit(solution)/shard_map/ppermute | solution.py:164
  123.5 3.1 %collective-permute-done.14.refs_4_ = bf16[104,1024]{1,0:T(8,128)(2,1)S(1)} collective-permute-done((bf16[104,1024]{1,0:T(8,128)(2,1)S(1)}, bf16[104,1024]{1,0:T(8,128)(2,1)S(1)}, u32[]{:S(2)}, u32[]{:S(2)}) %collective-permute-start.14) | collective-permute-done | bytes 213024 | tf_op jit(solution)/shard_map/ppermute | solution.py:164
  126.6 1.9 %join.1 = bf16[104,8192]{1,0:T(8,128)(2,1)} custom-call(s32[2]{0:T(128)S(1)} %pad_add_fusion.pos_ref, bf16[104,1024]{1,0:T(8,128)(2,1)S(1)} %get-tuple-element.16.refs_0_, bf16[104,1024]{1,0:T(8,128)(2,1)S(1)} %get-tuple-element.18.refs_1_, bf16[104,1024]{1,0:T(8,128)(2,1)S(1)} %get-tuple-element.20.refs_2_, ...), custom_call_target="tpu_custom_call" | custom-call | bytes 3407872 | tf_op jit(solution)/shard_map/join/pallas_call | solution.py:165
  (32 shorter events, 1.4 us)
Async XLA Ops:
  0.1 1.5 %copy-start = (bf16[104,8192]{1,0:T(8,128)(2,1)S(1)}, bf16[104,8192]{1,0:T(8,128)(2,1)}, u32[]{:S(2)}) copy-start(bf16[104,8192]{1,0:T(8,128)(2,1)} %x_ref.3) | copy-start | bytes 5111812
  1.5 2.0 %copy-start.2 = (bf16[5,256,128]{2,1,0:T(8,128)(2,1)S(1)}, bf16[5,256,128]{2,1,0:T(8,128)(2,1)}, u32[]{:S(2)}) copy-start(bf16[5,256,128]{2,1,0:T(8,128)(2,1)} %refs_0_.1) | copy-start | bytes 983044
  1.5 31.2 %copy-start.4 = (s32[5]{0:T(128)S(1)}, s32[5]{0:T(128)}, u32[]{:S(2)}) copy-start(s32[5]{0:T(128)} %source_ref.1) | copy-start | bytes 64
  2.2 32.2 %copy-start.6 = (s32[5]{0:T(128)S(1)}, s32[5]{0:T(128)}, u32[]{:S(2)}) copy-start(s32[5]{0:T(128)} %param.11) | copy-start | bytes 64
  2.2 30.5 %collective-permute-start.3 = (bf16[104,4096]{1,0:T(8,128)(2,1)S(1)}, bf16[104,4096]{1,0:T(8,128)(2,1)S(1)}, u32[]{:S(2)}, u32[]{:S(2)}) collective-permute-start(bf16[104,4096]{1,0:T(8,128)(2,1)S(1)} %pack.1), channel_id=1, source_target_pairs={{0,4},{4,0},{8,12},{12,8},{16,20},{20,16},{24,28},{28,24},{1,5},{5... | collective-permute-start | bytes 2555912 | tf_op jit(solution)/shard_map/ppermute | solution.py:126
  3.5 8.3 %collective-permute-start.4 = (bf16[5,256,128]{2,1,0:T(8,128)(2,1)S(1)}, bf16[5,256,128]{2,1,0:T(8,128)(2,1)S(1)}, u32[]{:S(2)}, u32[]{:S(2)}) collective-permute-start(bf16[5,256,128]{2,1,0:T(8,128)(2,1)S(1)} %copy-done.2), channel_id=1, source_target_pairs={{0,8},{4,12},{8,16},{12,20},{16,24},{20,28},{24,0},{28,4},{1,9},{5... | collective-permute-start | bytes 983048 | tf_op jit(solution)/shard_map/ppermute | solution.py:109
  3.5 29.2 %collective-permute-start.5 = (bf16[5,256,128]{2,1,0:T(8,128)(2,1)S(1)}, bf16[5,256,128]{2,1,0:T(8,128)(2,1)S(1)}, u32[]{:S(2)}, u32[]{:S(2)}) collective-permute-start(bf16[5,256,128]{2,1,0:T(8,128)(2,1)S(1)} %copy-done.2), channel_id=1, source_target_pairs={{0,16},{4,20},{8,24},{12,28},{16,0},{20,4},{24,8},{28,12},{1,17},{... | collective-permute-start | bytes 983048 | tf_op jit(solution)/shard_map/ppermute | solution.py:109
  4.8 27.9 %collective-permute-start.6 = (bf16[5,256,128]{2,1,0:T(8,128)(2,1)S(1)}, bf16[5,256,128]{2,1,0:T(8,128)(2,1)S(1)}, u32[]{:S(2)}, u32[]{:S(2)}) collective-permute-start(bf16[5,256,128]{2,1,0:T(8,128)(2,1)S(1)} %copy-done.2), channel_id=1, source_target_pairs={{0,24},{4,28},{8,0},{12,4},{16,8},{20,12},{24,16},{28,20},{1,25},{... | collective-permute-start | bytes 983048 | tf_op jit(solution)/shard_map/ppermute | solution.py:109
  34.0 14.7 %copy-start.1 = (bf16[10,256,128]{2,1,0:T(8,128)(2,1)S(1)}, bf16[10,256,128]{2,1,0:T(8,128)(2,1)}, u32[]{:S(2)}) copy-start(bf16[10,256,128]{2,1,0:T(8,128)(2,1)} %u_ref.1) | copy-start | bytes 1966084
  34.0 18.6 %copy-start.5 = (s32[5]{0:T(128)S(1)}, s32[5]{0:T(128)}, u32[]{:S(2)}) copy-start(s32[5]{0:T(128)} %param.12) | copy-start | bytes 64
  34.1 11.8 %collective-permute-start.7 = (f32[5,2,104,128]{3,2,1,0:T(8,128)S(1)}, f32[5,2,104,128]{3,2,1,0:T(8,128)S(1)}, u32[]{:S(2)}, u32[]{:S(2)}) collective-permute-start(f32[5,2,104,128]{3,2,1,0:T(8,128)S(1)} %compress.1), channel_id=1, source_target_pairs={{0,4},{4,0},{8,12},{12,8},{16,20},{20,16},{24,28},{28,24},{1,5},{5... | collective-permute-start | bytes 1597448 | tf_op jit(solution)/shard_map/ppermute | solution.py:141
  45.9 16.0 %collective-permute-start.10 = (bf16[5,2,104,128]{3,2,1,0:T(8,128)(2,1)S(1)}, bf16[5,2,104,128]{3,2,1,0:T(8,128)(2,1)S(1)}, u32[]{:S(2)}, u32[]{:S(2)}) collective-permute-start(bf16[5,2,104,128]{3,2,1,0:T(8,128)(2,1)S(1)} %select_convert_fusion), channel_id=1, source_target_pairs={{0,3},{1,0},{2,1},{3,2},{4,7},{5,4},{6,5},{7,6},{8,11},{9,8},{10,9... | collective-permute-start | bytes 798728 | tf_op jit(solution)/shard_map/ppermute | solution.py:116
  48.8 24.1 %collective-permute-start.11 = (bf16[10,256,128]{2,1,0:T(8,128)(2,1)S(1)}, bf16[10,256,128]{2,1,0:T(8,128)(2,1)S(1)}, u32[]{:S(2)}, u32[]{:S(2)}) collective-permute-start(bf16[10,256,128]{2,1,0:T(8,128)(2,1)S(1)} %copy-done.1), channel_id=1, source_target_pairs={{0,8},{4,12},{8,16},{12,20},{16,24},{20,28},{24,0},{28,4},{1,9},{5... | collective-permute-start | bytes 1966088 | tf_op jit(solution)/shard_map/ppermute | solution.py:109
  48.8 59.6 %collective-permute-start.12 = (bf16[10,256,128]{2,1,0:T(8,128)(2,1)S(1)}, bf16[10,256,128]{2,1,0:T(8,128)(2,1)S(1)}, u32[]{:S(2)}, u32[]{:S(2)}) collective-permute-start(bf16[10,256,128]{2,1,0:T(8,128)(2,1)S(1)} %copy-done.1), channel_id=1, source_target_pairs={{0,16},{4,20},{8,24},{12,28},{16,0},{20,4},{24,8},{28,12},{1,17},{... | collective-permute-start | bytes 1966088 | tf_op jit(solution)/shard_map/ppermute | solution.py:109
  51.2 62.4 %collective-permute-start.13 = (bf16[10,256,128]{2,1,0:T(8,128)(2,1)S(1)}, bf16[10,256,128]{2,1,0:T(8,128)(2,1)S(1)}, u32[]{:S(2)}, u32[]{:S(2)}) collective-permute-start(bf16[10,256,128]{2,1,0:T(8,128)(2,1)S(1)} %copy-done.1), channel_id=1, source_target_pairs={{0,24},{4,28},{8,0},{12,4},{16,8},{20,12},{24,16},{28,20},{1,25},{... | collective-permute-start | bytes 1966088 | tf_op jit(solution)/shard_map/ppermute | solution.py:109
  52.7 2.0 %collective-permute-start = (s32[5]{0:T(128)S(1)}, s32[5]{0:T(128)S(1)}, u32[]{:S(2)}, u32[]{:S(2)}) collective-permute-start(s32[5]{0:T(128)S(1)} %copy-done.5), channel_id=1, source_target_pairs={{0,1},{1,2},{2,3},{3,0},{4,5},{5,6},{6,7},{7,4},{8,9},{9,10},{10,1... | collective-permute-start | bytes 68 | tf_op jit(solution)/shard_map/ppermute | solution.py:116
  54.6 2.7 %collective-permute-start.1 = (s32[5]{0:T(128)S(1)}, s32[5]{0:T(128)S(1)}, u32[]{:S(2)}, u32[]{:S(2)}) collective-permute-start(s32[5]{0:T(128)S(1)} %copy-done.5), channel_id=1, source_target_pairs={{0,2},{1,3},{2,0},{3,1},{4,6},{5,7},{6,4},{7,5},{8,10},{9,11},{10,... | collective-permute-start | bytes 68 | tf_op jit(solution)/shard_map/ppermute | solution.py:116
  57.3 4.6 %collective-permute-start.2 = (s32[5]{0:T(128)S(1)}, s32[5]{0:T(128)S(1)}, u32[]{:S(2)}, u32[]{:S(2)}) collective-permute-start(s32[5]{0:T(128)S(1)} %copy-done.5), channel_id=1, source_target_pairs={{0,3},{1,0},{2,1},{3,2},{4,7},{5,4},{6,5},{7,6},{8,11},{9,8},{10,9... | collective-permute-start | bytes 68 | tf_op jit(solution)/shard_map/ppermute | solution.py:116
  61.9 4.2 %collective-permute-start.8 = (bf16[5,2,104,128]{3,2,1,0:T(8,128)(2,1)S(1)}, bf16[5,2,104,128]{3,2,1,0:T(8,128)(2,1)S(1)}, u32[]{:S(2)}, u32[]{:S(2)}) collective-permute-start(bf16[5,2,104,128]{3,2,1,0:T(8,128)(2,1)S(1)} %select_convert_fusion), channel_id=1, source_target_pairs={{0,1},{1,2},{2,3},{3,0},{4,5},{5,6},{6,7},{7,4},{8,9},{9,10},{10,1... | collective-permute-start | bytes 798728 | tf_op jit(solution)/shard_map/ppermute | solution.py:116
  61.9 10.8 %collective-permute-start.9 = (bf16[5,2,104,128]{3,2,1,0:T(8,128)(2,1)S(1)}, bf16[5,2,104,128]{3,2,1,0:T(8,128)(2,1)S(1)}, u32[]{:S(2)}, u32[]{:S(2)}) collective-permute-start(bf16[5,2,104,128]{3,2,1,0:T(8,128)(2,1)S(1)} %select_convert_fusion), channel_id=1, source_target_pairs={{0,2},{1,3},{2,0},{3,1},{4,6},{5,7},{6,4},{7,5},{8,10},{9,11},{10,... | collective-permute-start | bytes 798728 | tf_op jit(solution)/shard_map/ppermute | solution.py:116
  63.2 9.7 %copy-start.3 = (s32[10]{0:T(128)S(1)}, s32[10]{0:T(128)}, u32[]{:S(2)}) copy-start(s32[10]{0:T(128)} %target_ref.7) | copy-start | bytes 124
  75.4 42.2 %collective-permute-start.15 = (bf16[104,1024]{1,0:T(8,128)(2,1)S(1)}, bf16[104,1024]{1,0:T(8,128)(2,1)S(1)}, u32[]{:S(2)}, u32[]{:S(2)}) collective-permute-start(bf16[104,1024]{1,0:T(8,128)(2,1)S(1)} %get-tuple-element.24), channel_id=1, source_target_pairs={{0,4},{4,0},{8,12},{12,8},{16,20},{20,16},{24,28},{28,24},{1,5},{5... | collective-permute-start | bytes 638984 | tf_op jit(solution)/shard_map/ppermute | solution.py:164
  110.8 7.3 %collective-permute-start.16 = (bf16[104,1024]{1,0:T(8,128)(2,1)S(1)}, bf16[104,1024]{1,0:T(8,128)(2,1)S(1)}, u32[]{:S(2)}, u32[]{:S(2)}) collective-permute-start(bf16[104,1024]{1,0:T(8,128)(2,1)S(1)} %get-tuple-element.25), channel_id=1, source_target_pairs={{0,4},{4,0},{8,12},{12,8},{16,20},{20,16},{24,28},{28,24},{1,5},{5... | collective-permute-start | bytes 638984 | tf_op jit(solution)/shard_map/ppermute | solution.py:164
  116.1 7.4 %collective-permute-start.17 = (bf16[104,1024]{1,0:T(8,128)(2,1)S(1)}, bf16[104,1024]{1,0:T(8,128)(2,1)S(1)}, u32[]{:S(2)}, u32[]{:S(2)}) collective-permute-start(bf16[104,1024]{1,0:T(8,128)(2,1)S(1)} %get-tuple-element.26), channel_id=1, source_target_pairs={{0,4},{4,0},{8,12},{12,8},{16,20},{20,16},{24,28},{28,24},{1,5},{5... | collective-permute-start | bytes 638984 | tf_op jit(solution)/shard_map/ppermute | solution.py:164
  117.4 9.2 %collective-permute-start.14 = (bf16[104,1024]{1,0:T(8,128)(2,1)S(1)}, bf16[104,1024]{1,0:T(8,128)(2,1)S(1)}, u32[]{:S(2)}, u32[]{:S(2)}) collective-permute-start(bf16[104,1024]{1,0:T(8,128)(2,1)S(1)} %get-tuple-element.23), channel_id=1, source_target_pairs={{0,4},{4,0},{8,12},{12,8},{16,20},{20,16},{24,28},{28,24},{1,5},{5... | collective-permute-start | bytes 638984 | tf_op jit(solution)/shard_map/ppermute | solution.py:164

commit v2 on v0

--- a/solution.py
+++ b/solution.py
@@ -1,10 +1,257 @@
+import functools
+
 import jax
 import jax.numpy as jnp
 from jax import lax
+from jax.experimental import pallas as pl
+from jax.experimental.pallas import tpu as pltpu
 from jax.sharding import PartitionSpec as P
 
-
-def local(incident, v_factors, u_factors, block_source, block_rank, block_slot, slot_target):
+VMEM = pl.BlockSpec(memory_space=pltpu.VMEM)
+SMEM = pl.BlockSpec(memory_space=pltpu.SMEM)
+LIMIT = 32 * 1024 * 1024
+
+
+def call(body, out_shape, in_specs, name, flops=0, moved=0, scratch=()):
+    out_specs = [VMEM] * len(out_shape) if isinstance(out_shape, list) else VMEM
+    return pl.pallas_call(
+        body,
+        out_shape=out_shape,
+        in_specs=in_specs,
+        out_specs=out_specs,
+        scratch_shapes=list(scratch),
+        compiler_params=pltpu.CompilerParams(vmem_limit_bytes=LIMIT),
+        cost_estimate=pl.CostEstimate(flops=flops, bytes_accessed=moved, transcendentals=0),
+        name=name,
+    )
+
+
+def pack_body(seg, pos_ref, x_ref, out_ref):
+    half = 1 - pos_ref[0]
+    for piece in range(out_ref.shape[1] // seg):
+        start = pl.multiple_of((2 * piece + half) * seg, seg)
+        out_ref[:, piece * seg : (piece + 1) * seg] = x_ref[:, pl.ds(start, seg)]
+
+
+def compress_body(seg, pos_ref, source_ref, x_ref, xn_ref, v0, v1, v2, v3, v4, out_ref, send_ref):
+    half, mine = pos_ref[0], pos_ref[1]
+    columns = x_ref.shape[0]
+    out_ref[...] = jnp.zeros_like(out_ref)
+
+    def run(shards):
+        for block in range(out_ref.shape[0]):
+            source = source_ref[block]
+            own = other = 0.0
+            for step, shard in enumerate(shards):
+                piece = source * PLACES + jnp.bitwise_xor(mine, step)
+                here = pl.multiple_of((piece * 2 + half) * seg, seg)
+                there = pl.multiple_of(piece * seg, seg)
+                rows = shard[block]
+                own += jnp.dot(x_ref[:, pl.ds(here, seg)], rows, preferred_element_type=jnp.float32)
+                other += jnp.dot(
+                    xn_ref[:, pl.ds(there, seg)], rows, preferred_element_type=jnp.float32
+                )
+            out_ref[block, half, :columns] = own
+            out_ref[block, 1 - half, :columns] = other
+
+    inner = (mine == 1) | (mine == 2)
+
+    @pl.when(inner)
+    def _():
+        run((v0, v1, v2, v3))
+
+    @pl.when(jnp.logical_not(inner))
+    def _():
+        run((v0, v1, v2, v4))
+
+    send_ref[...] = out_ref[...].astype(send_ref.dtype)
+
+
+def land_body(index_ref, target_ref, comp_ref, rows_ref):
+    clusters, rank_max = rows_ref.shape[0], comp_ref.shape[3]
+    for slot in range(rows_ref.shape[3] // rank_max):
+        block, target = index_ref[slot], target_ref[slot]
+        found = comp_ref[jnp.maximum(block, 0)]
+        for cluster in range(clusters):
+            wanted = (block >= 0) & (target == cluster)
+            kept = jnp.where(wanted, found, jnp.zeros_like(found))
+            rows_ref[cluster, :, :, slot * rank_max : (slot + 1) * rank_max] = kept
+
+
+def expand_body(seg, columns, choices, pos_ref, rows_ref, *refs):
+    own_ref, other_ref, acc = refs[-3:]
+    half, mine = pos_ref[0], pos_ref[1]
+    clusters, sides, padded, depth = rows_ref.shape
+
+    def run(choice):
+        slots = [refs[index][slot] for index in choice for slot in range(refs[index].shape[0])]
+        factor = jnp.concatenate(slots, axis=1)
+        product = lax.dot_general(
+            rows_ref[...].reshape(clusters * sides * padded, depth),
+            factor,
+            (((1,), (1,)), ((), ())),
+            preferred_element_type=jnp.float32,
+        )
+        acc[...] = product.reshape(clusters, sides, padded, seg)
+
+    if len(choices) == 1:
+        run(choices[0])
+    else:
+        inner = (mine == 1) | (mine == 2)
+
+        @pl.when(inner)
+        def _():
+            run(choices[0])
+
+        @pl.when(jnp.logical_not(inner))
+        def _():
+            run(choices[1])
+
+    for target in range(clusters):
+        span = slice(target * seg, (target + 1) * seg)
+        own_ref[:, span] = acc[target, half, :columns].astype(own_ref.dtype)
+        other_ref[:, span] = acc[target, 1 - half, :columns].astype(other_ref.dtype)
+
+
+def join_body(seg, clusters, pos_ref, *refs):
+    out_ref = refs[-1]
+    half, mine = pos_ref[0], pos_ref[1]
+    for step in range(PLACES):
+        place = jnp.bitwise_xor(mine, step)
+        for target in range(clusters):
+            span = slice(target * seg, (target + 1) * seg)
+            base = (target * PLACES + place) * 2
+            here = pl.multiple_of((base + half) * seg, seg)
+            there = pl.multiple_of((base + 1 - half) * seg, seg)
+            out_ref[:, pl.ds(here, seg)] = refs[step][:, span]
+            out_ref[:, pl.ds(there, seg)] = refs[PLACES + step][:, span]
+
+
+def after(value, *first):
+    return lax.optimization_barrier((value, *first))[0]
+
+
+PLACES = 4
+
+
+def paired(incident, v_factors, u_factors, block_source, block_rank, block_slot, slot_target):
+    columns, width = incident.shape
+    padded = -(-columns // 16) * 16
+    blocks, seg, rank_max = v_factors.shape
+    capacity = u_factors.shape[0]
+    owners = lax.axis_size("clus")
+    clusters = width // (seg * 2 * PLACES)
+    me, owner = lax.axis_index("rhs"), lax.axis_index("clus")
+    position = jnp.stack([me % 2, me // 2]).astype(jnp.int32)
+
+    def move(array, pairs):
+        return lax.ppermute(array, "rhs", [(2 * a + i, 2 * b + i) for a, b in pairs for i in (0, 1)])
+
+    def across(array):
+        return lax.ppermute(array, "rhs", [(p, p ^ 1) for p in range(2 * PLACES)])
+
+    far = [(p, p ^ 2) for p in range(PLACES)]
+    near = [(p, p ^ 1) for p in range(PLACES)]
+    middle = [(1, 2), (2, 1)]
+    early = capacity // 2
+    ends = [(1, 0), (2, 3)]
+
+    def spread(array):
+        stages, stage = [], 1
+        while stage < owners:
+            stages, stage = [stage] + stages, 2 * stage
+        for stage in stages:
+            other = lax.ppermute(array, "clus", [(p, p ^ stage) for p in range(owners)])
+            array = jnp.concatenate([array, other], axis=0)
+        return array
+
+    v_far, v_near, v_middle = (
+        move(v_factors, far),
+        move(v_factors, near),
+        move(v_factors, middle),
+    )
+    packed = call(
+        functools.partial(pack_body, seg),
+        jax.ShapeDtypeStruct((columns, width // 2), incident.dtype),
+        [SMEM, VMEM],
+        "pack",
+        moved=3 * columns * width,
+    )(position, incident)
+    x_other = across(packed)
+    slots = spread(block_slot)
+    v_far, slots = lax.optimization_barrier((v_far, slots))
+    v_ends = move(v_far, ends)
+    u_first = after(u_factors, v_far)
+    u_far = [move(u_first[part], far) for part in (slice(0, early), slice(early, capacity))]
+    u_near, u_middle = move(u_first, near), move(u_first, middle)
+    u_ends = [move(part, ends) for part in u_far]
+
+    partial, sent = call(
+        functools.partial(compress_body, seg),
+        [
+            jax.ShapeDtypeStruct((blocks, 2, padded, rank_max), jnp.float32),
+            jax.ShapeDtypeStruct((blocks, 2, padded, rank_max), jnp.bfloat16),
+        ],
+        [SMEM, SMEM] + [VMEM] * 7,
+        "compress",
+        flops=4 * blocks * columns * seg * PLACES * rank_max,
+        moved=3 * columns * width + 2 * PLACES * v_factors.size,
+    )(position, block_source, incident, x_other, v_factors, v_near, v_far, v_middle, v_ends)
+    rank_index = lax.broadcasted_iota(jnp.int32, (blocks, 1, 1, rank_max), 3)
+    compressed = jnp.where(
+        rank_index < block_rank[:, None, None, None],
+        partial + across(sent).astype(jnp.float32),
+        0.0,
+    ).astype(jnp.bfloat16)
+    gathered = spread(after(compressed, u_far[0]))
+    wanted = owner * capacity + lax.broadcasted_iota(jnp.int32, (capacity, slots.shape[0]), 0)
+    order = lax.broadcasted_iota(jnp.int32, (capacity, slots.shape[0]), 1)
+    feeding = jnp.max(jnp.where(wanted == slots[None, :], order, -1), axis=1)
+    slot_rows = call(
+        land_body,
+        jax.ShapeDtypeStruct((clusters, 2, padded, capacity * rank_max), jnp.bfloat16),
+        [SMEM, SMEM, VMEM],
+        "land",
+        moved=2 * gathered.size * (1 + clusters),
+    )(feeding, slot_target, after(gathered, u_far[1]))
+
+    chunk = jax.ShapeDtypeStruct((columns, clusters * seg), jnp.bfloat16)
+    own_parts, other_parts = [None] * PLACES, [None] * PLACES
+    arrivals = {
+        0: ([u_factors], [[0]]),
+        2: (u_far, [[0, 1]]),
+        1: ([u_near], [[0]]),
+        3: ([u_middle, *u_ends], [[0], [1, 2]]),
+    }
+    finished = []
+    for step, (shards, choices) in arrivals.items():
+        if finished:
+            slot_rows = after(slot_rows, own_parts[finished[-1]])
+        if len(finished) > 1:
+            slot_rows = after(slot_rows, other_parts[finished[-2]])
+        own, other = call(
+            functools.partial(expand_body, seg, columns, choices),
+            [chunk, chunk],
+            [SMEM, VMEM] + [VMEM] * len(shards),
+            "expand",
+            flops=4 * clusters * capacity * columns * seg * rank_max,
+            moved=2 * u_factors.size + 2 * slot_rows.size + 4 * columns * clusters * seg,
+            scratch=[pltpu.VMEM((clusters, 2, padded, seg), jnp.float32)],
+        )(position, slot_rows, *shards)
+        own_parts[step], other_parts[step] = own, across(other)
+        finished.append(step)
+    return call(
+        functools.partial(join_body, seg, clusters),
+        jax.ShapeDtypeStruct((columns, width), jnp.bfloat16),
+        [SMEM] + [VMEM] * (2 * PLACES),
+        "join",
+        moved=4 * columns * width,
+    )(position, *own_parts, *other_parts)
+
+
+def gathered_plan(
+    incident, v_factors, u_factors, block_source, block_rank, block_slot, slot_target
+):
     columns = incident.shape[0]
     blocks = v_factors.shape[0]
     rank_max = v_factors.shape[2]
@@ -58,6 +305,16 @@
     return summed.reshape(columns, local_clusters * cluster_len).astype(jnp.bfloat16)
 
 
+def local(incident, v_factors, *rest):
+    owners = lax.axis_size("clus")
+    fits = (
+        lax.axis_size("rhs") == 2 * PLACES
+        and v_factors.shape[1] % 128 == 0
+        and owners & (owners - 1) == 0
+    )
+    return (paired if fits else gathered_plan)(incident, v_factors, *rest)
+
+
 def solution(mesh):
     placed = (
         P("rhs", "clus"),

time: 182 us -> 112 us (0.62)
  waiting for transfers between devices: 128 us -> 68 us
  matrix products: 22.9 us -> 0 us
  starting transfers between devices: 7.73 us -> 30.1 us
  between operations: 13.5 us -> 0.22 us
  Pallas kernels: 0 us -> 10.5 us
  local copies, waits for them, and re-layouts: 8.1 us -> 1.52 us
    all_gather x2 -> x0, waiting for transfers between devices: 121 us -> none  [the longest x1 72.1 us: local(): lax.all_gather(u_factors, 'rhs', axis=1, tiled=True)]
    ppermute x0 -> x20, waiting for transfers between devices: none -> 68 us  [the longest x10 44.8 us: move(): lax.ppermute(array, 'rhs', [(2 * a + i, 2 * b + i) for a, b in pairs for...]
    ppermute x0 -> x20, starting transfers between devices: none -> 30.1 us  [the longest x10 18.2 us: move(): lax.ppermute(array, 'rhs', [(2 * a + i, 2 * b + i) for a, b in pairs for...]
    dot_general x5 -> x0, matrix products: 22.9 us -> none  [the longest x1 13.1 us: local(): jnp.einsum('jt,jcr->ctr', owners, products, precision=lax.Precision.HIGHEST)]
    pallas_call x0 -> x8, Pallas kernels: none -> 10.5 us  [the longest x4 5.57 us: paired(): call(functools.partial(expand_body, seg, columns, choices), [chunk, chunk...]
    all_to_all x2 -> x0, starting transfers between devices: 7.69 us -> none  [the longest x1 4.24 us: local(): lax.all_to_all(labels, 'clus', split_axis=0, concat_axis=0, tiled=True)]
    all_to_all x2 -> x0, waiting for transfers between devices: 5.43 us -> none  [the longest x1 5.42 us: local(): lax.all_to_all(outgoing, 'clus', split_axis=0, concat_axis=0, tiled=True)]
    gather x1 -> x0, local copies, waits for them, and re-layouts: 2.21 us -> none  [local(): jnp.take(incident.reshape(columns, local_clusters, cluster_len), block_so...]
  transfers between devices with their start and end apart: 4 -> 20, of which waited for: 3 -> 14; matrix products, arithmetic and copies ran while one was open for 6% -> 1% of each run, Pallas kernels for 0% -> 5%
where the time goes in v2:
time: 112 us; the launch traced here: 111 us
  waiting for transfers between devices  68 us (61%)
  starting transfers between devices  30.1 us (27%)
  Pallas kernels  10.5 us (9%)
  local copies, waits for them, and re-layouts  1.52 us (1%)
    ppermute x10, waiting for transfers between devices, move(): lax.ppermute(array, 'rhs', [(2 * a + i, 2 * b + i) for a, b in pairs for...  44.8 us
    ppermute x10, starting transfers between devices, move(): lax.ppermute(array, 'rhs', [(2 * a + i, 2 * b + i) for a, b in pairs for...  18.2 us
    ppermute x6, waiting for transfers between devices, across(): return lax.ppermute(array, 'rhs', [(p, p ^ 1) for p in range(2 * PLACES)])  14.8 us
    ppermute x6, starting transfers between devices, across(): return lax.ppermute(array, 'rhs', [(p, p ^ 1) for p in range(2 * PLACES)])  8.77 us
    ppermute x4, waiting for transfers between devices, spread(): other = lax.ppermute(array, 'clus', [(p, p ^ stage) for p in range(owners)])  8.37 us
    pallas_call x4, Pallas kernels, paired(): call(functools.partial(expand_body, seg, columns, choices), [chunk, chunk...  5.57 us
    ppermute x4, starting transfers between devices, spread(): other = lax.ppermute(array, 'clus', [(p, p ^ stage) for p in range(owners)])  3.18 us
  transfers between devices with their start and end apart: 20, of which 14 were waited for; matrix products, arithmetic and copies ran while one was open for 1% of the time, Pallas kernels for 5%

profile of v2, /device:TPU:0, one launch (start us, length us, event | category | flops | bytes accessed | tf_op | source)
XLA Modules:
  0.0 111.1 jit_solution(1081020692991726827)
XLA Ops:
  0.1 1.5 %copy-done = bf16[104,8192]{1,0:T(8,128)(2,1)S(1)} copy-done((bf16[104,8192]{1,0:T(8,128)(2,1)S(1)}, bf16[104,8192]{1,0:T(8,128)(2,1)}, u32[]{:S(2)}) %copy-start) | copy-done | bytes 1703960
  2.2 3.0 %collective-permute-start.3 = (bf16[104,4096]{1,0:T(8,128)(2,1)S(1)}, bf16[104,4096]{1,0:T(8,128)(2,1)S(1)}, u32[]{:S(2)}, u32[]{:S(2)}) collective-permute-start(bf16[104,4096]{1,0:T(8,128)(2,1)S(1)} %pack.1), channel_id=1, source_target_pairs={{0,4},{4,0},{8,12},{12,8},{16,20},{20,16},{24,28},{28,24},{1,5},{5... | collective-permute-start | bytes 2555912 | tf_op jit(solution)/shard_map/ppermute | solution.py:151
  5.2 2.6 %collective-permute-start = (bf16[5,256,128]{2,1,0:T(8,128)(2,1)S(1)}, bf16[5,256,128]{2,1,0:T(8,128)(2,1)S(1)}, u32[]{:S(2)}, u32[]{:S(2)}) collective-permute-start(bf16[5,256,128]{2,1,0:T(8,128)(2,1)S(1)} %copy-done.2), channel_id=1, source_target_pairs={{0,16},{4,20},{8,24},{12,28},{16,0},{20,4},{24,8},{28,12},{1,17},{... | collective-permute-start | bytes 983048 | tf_op jit(solution)/shard_map/ppermute | solution.py:148
  7.8 1.6 %collective-permute-start.4 = (bf16[5,256,128]{2,1,0:T(8,128)(2,1)S(1)}, bf16[5,256,128]{2,1,0:T(8,128)(2,1)S(1)}, u32[]{:S(2)}, u32[]{:S(2)}) collective-permute-start(bf16[5,256,128]{2,1,0:T(8,128)(2,1)S(1)} %copy-done.2), channel_id=1, source_target_pairs={{0,8},{4,12},{8,0},{12,4},{16,24},{20,28},{24,16},{28,20},{1,9},{5... | collective-permute-start | bytes 983048 | tf_op jit(solution)/shard_map/ppermute | solution.py:148
  10.1 1.6 %collective-permute-start.1 = (s32[5]{0:T(128)S(1)}, s32[5]{0:T(128)S(1)}, u32[]{:S(2)}, u32[]{:S(2)}) collective-permute-start(s32[5]{0:T(128)S(1)} %copy-done.5), channel_id=1, source_target_pairs={{0,2},{1,3},{2,0},{3,1},{4,6},{5,7},{6,4},{7,5},{8,10},{9,11},{10,... | collective-permute-start | bytes 68 | tf_op jit(solution)/shard_map/ppermute | solution.py:164
  11.6 2.0 %collective-permute-done.1 = s32[5]{0:T(128)S(1)} collective-permute-done((s32[5]{0:T(128)S(1)}, s32[5]{0:T(128)S(1)}, u32[]{:S(2)}, u32[]{:S(2)}) %collective-permute-start.1) | collective-permute-done | bytes 52 | tf_op jit(solution)/shard_map/ppermute | solution.py:164
  13.8 1.1 collective-permute-done.2
  14.9 8.6 %collective-permute-done.v2 = bf16[5,256,128]{2,1,0:T(8,128)(2,1)S(1)} collective-permute-done((bf16[5,256,128]{2,1,0:T(8,128)(2,1)S(1)}, bf16[5,256,128]{2,1,0:T(8,128)(2,1)S(1)}, u32[]{:S(2)}, u32[]{:S(2)}) %collective-permute-start) | collective-permute-done | bytes 327712 | tf_op jit(solution)/shard_map/ppermute | solution.py:148
  23.5 1.3 %collective-permute-start.6 = (bf16[5,256,128]{2,1,0:T(8,128)(2,1)S(1)}, bf16[5,256,128]{2,1,0:T(8,128)(2,1)S(1)}, u32[]{:S(2)}, u32[]{:S(2)}) collective-permute-start(bf16[5,256,128]{2,1,0:T(8,128)(2,1)S(1)} %collective-permute-done.v2), channel_id=1, source_target_pairs={{8,0},{12,4},{16,24},{20,28},{9,1},{13,5},{17,25},{21,29},{10,2},{... | collective-permute-start | bytes 983048 | tf_op jit(solution)/shard_map/ppermute | solution.py:148
  24.8 8.0 %collective-permute-done.6.v4 = bf16[5,256,128]{2,1,0:T(8,128)(2,1)S(1)} collective-permute-done((bf16[5,256,128]{2,1,0:T(8,128)(2,1)S(1)}, bf16[5,256,128]{2,1,0:T(8,128)(2,1)S(1)}, u32[]{:S(2)}, u32[]{:S(2)}) %collective-permute-start.6) | collective-permute-done | bytes 327712 | tf_op jit(solution)/shard_map/ppermute | solution.py:148
  32.8 1.4 %compress.1 = (f32[5,2,112,128]{3,2,1,0:T(8,128)S(1)}, bf16[5,2,112,128]{3,2,1,0:T(8,128)(2,1)S(1)}) custom-call(s32[2]{0:T(128)S(1)} %pad_add_fusion.pos_ref, s32[5]{0:T(128)S(1)} %copy-done.3, bf16[104,8192]{1,0:T(8,128)(2,1)S(1)} %copy-done, bf16[104,4096]{1,0:T(8,128)(2,1)S(1)} %collective-permute-done.3.xn_ref, bf16[5,256,128]{2,1,0:T(8,128)(2,1)S(1)} %copy-done.2, ...), custom_call_target="tpu_custom_call" | custom-call | flops 272629760 | bytes 3866624 | tf_op jit(solution)/shard_map/compress/pallas_call | solution.py:189
  34.8 2.6 %collective-permute-start.8 = (bf16[5,256,128]{2,1,0:T(8,128)(2,1)S(1)}, bf16[5,256,128]{2,1,0:T(8,128)(2,1)S(1)}, u32[]{:S(2)}, u32[]{:S(2)}) collective-permute-start(bf16[5,256,128]{2,1,0:T(8,128)(2,1)S(1)} %get-tuple-element.46), channel_id=1, source_target_pairs={{0,16},{4,20},{8,24},{12,28},{16,0},{20,4},{24,8},{28,12},{1,17},{... | collective-permute-start | bytes 983048 | tf_op jit(solution)/shard_map/ppermute | solution.py:148
  37.6 3.3 %collective-permute-done.7 = bf16[5,2,112,128]{3,2,1,0:T(8,128)(2,1)S(1)} collective-permute-done((bf16[5,2,112,128]{3,2,1,0:T(8,128)(2,1)S(1)}, bf16[5,2,112,128]{3,2,1,0:T(8,128)(2,1)S(1)}, u32[]{:S(2)}, u32[]{:S(2)}) %collective-permute-start.7) | collective-permute-done | bytes 286752 | tf_op jit(solution)/shard_map/ppermute | solution.py:151
  41.0 10.2 %collective-permute-done.8.refs_0_ = bf16[5,256,128]{2,1,0:T(8,128)(2,1)S(1)} collective-permute-done((bf16[5,256,128]{2,1,0:T(8,128)(2,1)S(1)}, bf16[5,256,128]{2,1,0:T(8,128)(2,1)S(1)}, u32[]{:S(2)}, u32[]{:S(2)}) %collective-permute-start.8) | collective-permute-done | bytes 327712 | tf_op jit(solution)/shard_map/ppermute | solution.py:148
  51.2 1.5 %collective-permute-start.9 = (bf16[5,2,112,128]{3,2,1,0:T(8,128)(2,1)S(1)}, bf16[5,2,112,128]{3,2,1,0:T(8,128)(2,1)S(1)}, u32[]{:S(2)}, u32[]{:S(2)}) collective-permute-start(bf16[5,2,112,128]{3,2,1,0:T(8,128)(2,1)S(1)} %select_convert_fusion), channel_id=1, source_target_pairs={{0,2},{1,3},{2,0},{3,1},{4,6},{5,7},{6,4},{7,5},{8,10},{9,11},{10,... | collective-permute-start | bytes 860168 | tf_op jit(solution)/shard_map/ppermute | solution.py:164
  52.7 5.2 %collective-permute-done.9 = bf16[5,2,112,128]{3,2,1,0:T(8,128)(2,1)S(1)} collective-permute-done((bf16[5,2,112,128]{3,2,1,0:T(8,128)(2,1)S(1)}, bf16[5,2,112,128]{3,2,1,0:T(8,128)(2,1)S(1)}, u32[]{:S(2)}, u32[]{:S(2)}) %collective-permute-start.9) | collective-permute-done | bytes 286752 | tf_op jit(solution)/shard_map/ppermute | solution.py:164
  58.2 6.1 %collective-permute-start.13 = (bf16[10,256,128]{2,1,0:T(8,128)(2,1)S(1)}, bf16[10,256,128]{2,1,0:T(8,128)(2,1)S(1)}, u32[]{:S(2)}, u32[]{:S(2)}) collective-permute-start(bf16[10,256,128]{2,1,0:T(8,128)(2,1)S(1)} %copy-done.1), channel_id=1, source_target_pairs={{0,8},{4,12},{8,0},{12,4},{16,24},{20,28},{24,16},{28,20},{1,9},{5... | collective-permute-start | bytes 1966088 | tf_op jit(solution)/shard_map/ppermute | solution.py:148
  65.3 11.4 %collective-permute-done.11.refs_1_ = bf16[5,256,128]{2,1,0:T(8,128)(2,1)S(1)} collective-permute-done((bf16[5,256,128]{2,1,0:T(8,128)(2,1)S(1)}, bf16[5,256,128]{2,1,0:T(8,128)(2,1)S(1)}, u32[]{:S(2)}, u32[]{:S(2)}) %collective-permute-start.11) | collective-permute-done | bytes 327712 | tf_op jit(solution)/shard_map/ppermute | solution.py:148
  77.6 1.4 %expand.4 = (bf16[104,1024]{1,0:T(8,128)(2,1)S(1)}, bf16[104,1024]{1,0:T(8,128)(2,1)S(1)}) custom-call(s32[2]{0:T(128)S(1)} %pad_add_fusion.pos_ref, bf16[4,2,112,1280]{3,2,1,0:T(8,128)(2,1)S(1)} %land.1.rows_ref, bf16[10,256,128]{2,1,0:T(8,128)(2,1)S(1)} %copy-done.1), custom_call_target="tpu_custom_call" | custom-call | flops 545259520 | bytes 3375104 | tf_op jit(solution)/shard_map/expand/pallas_call | solution.py:232
  79.0 1.6 %collective-permute-start.12 = (bf16[104,1024]{1,0:T(8,128)(2,1)S(1)}, bf16[104,1024]{1,0:T(8,128)(2,1)S(1)}, u32[]{:S(2)}, u32[]{:S(2)}) collective-permute-start(bf16[104,1024]{1,0:T(8,128)(2,1)S(1)} %get-tuple-element.36), channel_id=1, source_target_pairs={{0,4},{4,0},{8,12},{12,8},{16,20},{20,16},{24,28},{28,24},{1,5},{5... | collective-permute-start | bytes 638984 | tf_op jit(solution)/shard_map/ppermute | solution.py:151
  80.5 1.3 %collective-permute-start.16 = (bf16[5,256,128]{2,1,0:T(8,128)(2,1)S(1)}, bf16[5,256,128]{2,1,0:T(8,128)(2,1)S(1)}, u32[]{:S(2)}, u32[]{:S(2)}) collective-permute-start(bf16[5,256,128]{2,1,0:T(8,128)(2,1)S(1)} %collective-permute-done.8.refs_0_), channel_id=1, source_target_pairs={{8,0},{12,4},{16,24},{20,28},{9,1},{13,5},{17,25},{21,29},{10,2},{... | collective-permute-start | bytes 983048 | tf_op jit(solution)/shard_map/ppermute | solution.py:148
  81.8 1.3 %collective-permute-start.17 = (bf16[5,256,128]{2,1,0:T(8,128)(2,1)S(1)}, bf16[5,256,128]{2,1,0:T(8,128)(2,1)S(1)}, u32[]{:S(2)}, u32[]{:S(2)}) collective-permute-start(bf16[5,256,128]{2,1,0:T(8,128)(2,1)S(1)} %collective-permute-done.11.refs_1_), channel_id=1, source_target_pairs={{8,0},{12,4},{16,24},{20,28},{9,1},{13,5},{17,25},{21,29},{10,2},{... | collective-permute-start | bytes 983048 | tf_op jit(solution)/shard_map/ppermute | solution.py:148
  83.1 1.4 %expand.5 = (bf16[104,1024]{1,0:T(8,128)(2,1)S(1)}, bf16[104,1024]{1,0:T(8,128)(2,1)S(1)}) custom-call(s32[2]{0:T(128)S(1)} %pad_add_fusion.pos_ref, bf16[4,2,112,1280]{3,2,1,0:T(8,128)(2,1)S(1)} %land.1.rows_ref, bf16[5,256,128]{2,1,0:T(8,128)(2,1)S(1)} %collective-permute-done.8.refs_0_, bf16[5,256,128]{2,1,0:T(8,128)(2,1)S(1)} %collective-permute-done.11.refs_1_), custom_call_target="tpu_custom_call" | custom-call | flops 545259520 | bytes 3375104 | tf_op jit(solution)/shard_map/expand/pallas_call | solution.py:232
  85.4 1.5 %collective-permute-start.14 = (bf16[104,1024]{1,0:T(8,128)(2,1)S(1)}, bf16[104,1024]{1,0:T(8,128)(2,1)S(1)}, u32[]{:S(2)}, u32[]{:S(2)}) collective-permute-start(bf16[104,1024]{1,0:T(8,128)(2,1)S(1)} %get-tuple-element.40), channel_id=1, source_target_pairs={{0,4},{4,0},{8,12},{12,8},{16,20},{20,16},{24,28},{28,24},{1,5},{5... | collective-permute-start | bytes 638984 | tf_op jit(solution)/shard_map/ppermute | solution.py:151
  86.9 1.4 %expand.6 = (bf16[104,1024]{1,0:T(8,128)(2,1)S(1)}, bf16[104,1024]{1,0:T(8,128)(2,1)S(1)}) custom-call(s32[2]{0:T(128)S(1)} %pad_add_fusion.pos_ref, bf16[4,2,112,1280]{3,2,1,0:T(8,128)(2,1)S(1)} %land.1.rows_ref, bf16[10,256,128]{2,1,0:T(8,128)(2,1)S(1)} %collective-permute-done.13.refs_0_), custom_call_target="tpu_custom_call" | custom-call | flops 545259520 | bytes 3375104 | tf_op jit(solution)/shard_map/expand/pallas_call | solution.py:232
  88.3 2.9 %collective-permute-done.14.refs_6_ = bf16[104,1024]{1,0:T(8,128)(2,1)S(1)} collective-permute-done((bf16[104,1024]{1,0:T(8,128)(2,1)S(1)}, bf16[104,1024]{1,0:T(8,128)(2,1)S(1)}, u32[]{:S(2)}, u32[]{:S(2)}) %collective-permute-start.14) | collective-permute-done | bytes 213024 | tf_op jit(solution)/shard_map/ppermute | solution.py:151
  91.2 1.8 %collective-permute-done.16.refs_1_ = bf16[5,256,128]{2,1,0:T(8,128)(2,1)S(1)} collective-permute-done((bf16[5,256,128]{2,1,0:T(8,128)(2,1)S(1)}, bf16[5,256,128]{2,1,0:T(8,128)(2,1)S(1)}, u32[]{:S(2)}, u32[]{:S(2)}) %collective-permute-start.16) | collective-permute-done | bytes 327712 | tf_op jit(solution)/shard_map/ppermute | solution.py:148
  93.1 4.9 %collective-permute-done.17.refs_2_ = bf16[5,256,128]{2,1,0:T(8,128)(2,1)S(1)} collective-permute-done((bf16[5,256,128]{2,1,0:T(8,128)(2,1)S(1)}, bf16[5,256,128]{2,1,0:T(8,128)(2,1)S(1)}, u32[]{:S(2)}, u32[]{:S(2)}) %collective-permute-start.17) | collective-permute-done | bytes 327712 | tf_op jit(solution)/shard_map/ppermute | solution.py:148
  98.0 1.4 %expand.7 = (bf16[104,1024]{1,0:T(8,128)(2,1)S(1)}, bf16[104,1024]{1,0:T(8,128)(2,1)S(1)}) custom-call(s32[2]{0:T(128)S(1)} %pad_add_fusion.pos_ref, bf16[4,2,112,1280]{3,2,1,0:T(8,128)(2,1)S(1)} %land.1.rows_ref, bf16[10,256,128]{2,1,0:T(8,128)(2,1)S(1)} %collective-permute-done.15.refs_0_, bf16[5,256,128]{2,1,0:T(8,128)(2,1)S(1)} %collective-permute-done.16.refs_1_, ...), custom_call_target="tpu_custom_call" | custom-call | flops 545259520 | bytes 3375104 | tf_op jit(solution)/shard_map/expand/pallas_call | solution.py:232
  101.5 5.4 %collective-permute-done.19.refs_7_ = bf16[104,1024]{1,0:T(8,128)(2,1)S(1)} collective-permute-done((bf16[104,1024]{1,0:T(8,128)(2,1)S(1)}, bf16[104,1024]{1,0:T(8,128)(2,1)S(1)}, u32[]{:S(2)}, u32[]{:S(2)}) %collective-permute-start.19) | collective-permute-done | bytes 213024 | tf_op jit(solution)/shard_map/ppermute | solution.py:151
  106.9 2.3 %collective-permute-done.18.refs_5_ = bf16[104,1024]{1,0:T(8,128)(2,1)S(1)} collective-permute-done((bf16[104,1024]{1,0:T(8,128)(2,1)S(1)}, bf16[104,1024]{1,0:T(8,128)(2,1)S(1)}, u32[]{:S(2)}, u32[]{:S(2)}) %collective-permute-start.18) | collective-permute-done | bytes 213024 | tf_op jit(solution)/shard_map/ppermute | solution.py:151
  109.1 1.9 %join.1 = bf16[104,8192]{1,0:T(8,128)(2,1)} custom-call(s32[2]{0:T(128)S(1)} %pad_add_fusion.pos_ref, bf16[104,1024]{1,0:T(8,128)(2,1)S(1)} %get-tuple-element.32.refs_0_, bf16[104,1024]{1,0:T(8,128)(2,1)S(1)} %get-tuple-element.38.refs_1_, bf16[104,1024]{1,0:T(8,128)(2,1)S(1)} %get-tuple-element.34.refs_2_, ...), custom_call_target="tpu_custom_call" | custom-call | bytes 3407872 | tf_op jit(solution)/shard_map/join/pallas_call | solution.py:243
  (40 shorter events, 7.5 us)
Async XLA Ops:
  0.1 1.5 %copy-start = (bf16[104,8192]{1,0:T(8,128)(2,1)S(1)}, bf16[104,8192]{1,0:T(8,128)(2,1)}, u32[]{:S(2)}) copy-start(bf16[104,8192]{1,0:T(8,128)(2,1)} %x_ref.3) | copy-start | bytes 5111812
  1.5 3.7 %copy-start.2 = (bf16[5,256,128]{2,1,0:T(8,128)(2,1)S(1)}, bf16[5,256,128]{2,1,0:T(8,128)(2,1)}, u32[]{:S(2)}) copy-start(bf16[5,256,128]{2,1,0:T(8,128)(2,1)} %v0.1) | copy-start | bytes 983044
  1.5 8.5 %copy-start.5 = (s32[5]{0:T(128)S(1)}, s32[5]{0:T(128)}, u32[]{:S(2)}) copy-start(s32[5]{0:T(128)} %param.12) | copy-start | bytes 64
  1.5 31.3 %copy-start.3 = (s32[5]{0:T(128)S(1)}, s32[5]{0:T(128)}, u32[]{:S(2)}) copy-start(s32[5]{0:T(128)} %source_ref.1) | copy-start | bytes 64
  2.2 30.6 %collective-permute-start.3 = (bf16[104,4096]{1,0:T(8,128)(2,1)S(1)}, bf16[104,4096]{1,0:T(8,128)(2,1)S(1)}, u32[]{:S(2)}, u32[]{:S(2)}) collective-permute-start(bf16[104,4096]{1,0:T(8,128)(2,1)S(1)} %pack.1), channel_id=1, source_target_pairs={{0,4},{4,0},{8,12},{12,8},{16,20},{20,16},{24,28},{28,24},{1,5},{5... | collective-permute-start | bytes 2555912 | tf_op jit(solution)/shard_map/ppermute | solution.py:151
  5.2 18.3 %collective-permute-start = (bf16[5,256,128]{2,1,0:T(8,128)(2,1)S(1)}, bf16[5,256,128]{2,1,0:T(8,128)(2,1)S(1)}, u32[]{:S(2)}, u32[]{:S(2)}) collective-permute-start(bf16[5,256,128]{2,1,0:T(8,128)(2,1)S(1)} %copy-done.2), channel_id=1, source_target_pairs={{0,16},{4,20},{8,24},{12,28},{16,0},{20,4},{24,8},{28,12},{1,17},{... | collective-permute-start | bytes 983048 | tf_op jit(solution)/shard_map/ppermute | solution.py:148
  7.8 17.0 %collective-permute-start.4 = (bf16[5,256,128]{2,1,0:T(8,128)(2,1)S(1)}, bf16[5,256,128]{2,1,0:T(8,128)(2,1)S(1)}, u32[]{:S(2)}, u32[]{:S(2)}) collective-permute-start(bf16[5,256,128]{2,1,0:T(8,128)(2,1)S(1)} %copy-done.2), channel_id=1, source_target_pairs={{0,8},{4,12},{8,0},{12,4},{16,24},{20,28},{24,16},{28,20},{1,9},{5... | collective-permute-start | bytes 983048 | tf_op jit(solution)/shard_map/ppermute | solution.py:148
  9.4 15.4 %collective-permute-start.5 = (bf16[5,256,128]{2,1,0:T(8,128)(2,1)S(1)}, bf16[5,256,128]{2,1,0:T(8,128)(2,1)S(1)}, u32[]{:S(2)}, u32[]{:S(2)}) collective-permute-start(bf16[5,256,128]{2,1,0:T(8,128)(2,1)S(1)} %copy-done.2), channel_id=1, source_target_pairs={{8,16},{12,20},{16,8},{20,12},{9,17},{13,21},{17,9},{21,13},{10,18... | collective-permute-start | bytes 983048 | tf_op jit(solution)/shard_map/ppermute | solution.py:148
  10.1 3.6 %collective-permute-start.1 = (s32[5]{0:T(128)S(1)}, s32[5]{0:T(128)S(1)}, u32[]{:S(2)}, u32[]{:S(2)}) collective-permute-start(s32[5]{0:T(128)S(1)} %copy-done.5), channel_id=1, source_target_pairs={{0,2},{1,3},{2,0},{3,1},{4,6},{5,7},{6,4},{7,5},{8,10},{9,11},{10,... | collective-permute-start | bytes 68 | tf_op jit(solution)/shard_map/ppermute | solution.py:164
  13.7 1.1 %collective-permute-start.2 = (s32[10]{0:T(128)S(1)}, s32[10]{0:T(128)S(1)}, u32[]{:S(2)}, u32[]{:S(2)}) collective-permute-start(s32[10]{0:T(128)S(1)} %pad_add_fusion.1), channel_id=1, source_target_pairs={{0,1},{1,0},{2,3},{3,2},{4,5},{5,4},{6,7},{7,6},{8,9},{9,8},{10,11... | collective-permute-start | bytes 128 | tf_op jit(solution)/shard_map/ppermute | solution.py:164
  14.9 19.9 %copy-start.1 = (bf16[10,256,128]{2,1,0:T(8,128)(2,1)S(1)}, bf16[10,256,128]{2,1,0:T(8,128)(2,1)}, u32[]{:S(2)}) copy-start(bf16[10,256,128]{2,1,0:T(8,128)(2,1)} %refs_0_.1) | copy-start | bytes 1966084
  23.5 9.3 %collective-permute-start.6 = (bf16[5,256,128]{2,1,0:T(8,128)(2,1)S(1)}, bf16[5,256,128]{2,1,0:T(8,128)(2,1)S(1)}, u32[]{:S(2)}, u32[]{:S(2)}) collective-permute-start(bf16[5,256,128]{2,1,0:T(8,128)(2,1)S(1)} %collective-permute-done.v2), channel_id=1, source_target_pairs={{8,0},{12,4},{16,24},{20,28},{9,1},{13,5},{17,25},{21,29},{10,2},{... | collective-permute-start | bytes 983048 | tf_op jit(solution)/shard_map/ppermute | solution.py:148
  34.2 3.3 %copy-start.6 = (s32[5]{0:T(128)S(1)}, s32[5]{0:T(128)}, u32[]{:S(2)}) copy-start(s32[5]{0:T(128)} %param.11) | copy-start | bytes 64
  34.2 6.7 %collective-permute-start.7 = (bf16[5,2,112,128]{3,2,1,0:T(8,128)(2,1)S(1)}, bf16[5,2,112,128]{3,2,1,0:T(8,128)(2,1)S(1)}, u32[]{:S(2)}, u32[]{:S(2)}) collective-permute-start(bf16[5,2,112,128]{3,2,1,0:T(8,128)(2,1)S(1)} %get-tuple-element.28), channel_id=1, source_target_pairs={{0,4},{4,0},{8,12},{12,8},{16,20},{20,16},{24,28},{28,24},{1,5},{5... | collective-permute-start | bytes 860168 | tf_op jit(solution)/shard_map/ppermute | solution.py:151
  34.8 16.3 %collective-permute-start.8 = (bf16[5,256,128]{2,1,0:T(8,128)(2,1)S(1)}, bf16[5,256,128]{2,1,0:T(8,128)(2,1)S(1)}, u32[]{:S(2)}, u32[]{:S(2)}) collective-permute-start(bf16[5,256,128]{2,1,0:T(8,128)(2,1)S(1)} %get-tuple-element.46), channel_id=1, source_target_pairs={{0,16},{4,20},{8,24},{12,28},{16,0},{20,4},{24,8},{28,12},{1,17},{... | collective-permute-start | bytes 983048 | tf_op jit(solution)/shard_map/ppermute | solution.py:148
  51.2 6.8 %collective-permute-start.9 = (bf16[5,2,112,128]{3,2,1,0:T(8,128)(2,1)S(1)}, bf16[5,2,112,128]{3,2,1,0:T(8,128)(2,1)S(1)}, u32[]{:S(2)}, u32[]{:S(2)}) collective-permute-start(bf16[5,2,112,128]{3,2,1,0:T(8,128)(2,1)S(1)} %select_convert_fusion), channel_id=1, source_target_pairs={{0,2},{1,3},{2,0},{3,1},{4,6},{5,7},{6,4},{7,5},{8,10},{9,11},{10,... | collective-permute-start | bytes 860168 | tf_op jit(solution)/shard_map/ppermute | solution.py:164
  58.0 7.1 %collective-permute-start.10 = (bf16[10,2,112,128]{3,2,1,0:T(8,128)(2,1)S(1)}, bf16[10,2,112,128]{3,2,1,0:T(8,128)(2,1)S(1)}, u32[]{:S(2)}, u32[]{:S(2)}) collective-permute-start(bf16[10,2,112,128]{3,2,1,0:T(8,128)(2,1)S(1)} %pad_maximum_fusion.1), channel_id=1, source_target_pairs={{0,1},{1,0},{2,3},{3,2},{4,5},{5,4},{6,7},{7,6},{8,9},{9,8},{10,11... | collective-permute-start | bytes 1720328 | tf_op jit(solution)/shard_map/ppermute | solution.py:164
  58.1 18.6 %collective-permute-start.11 = (bf16[5,256,128]{2,1,0:T(8,128)(2,1)S(1)}, bf16[5,256,128]{2,1,0:T(8,128)(2,1)S(1)}, u32[]{:S(2)}, u32[]{:S(2)}) collective-permute-start(bf16[5,256,128]{2,1,0:T(8,128)(2,1)S(1)} %get-tuple-element.45), channel_id=1, source_target_pairs={{0,16},{4,20},{8,24},{12,28},{16,0},{20,4},{24,8},{28,12},{1,17},{... | collective-permute-start | bytes 983048 | tf_op jit(solution)/shard_map/ppermute | solution.py:148
  58.2 28.7 %collective-permute-start.13 = (bf16[10,256,128]{2,1,0:T(8,128)(2,1)S(1)}, bf16[10,256,128]{2,1,0:T(8,128)(2,1)S(1)}, u32[]{:S(2)}, u32[]{:S(2)}) collective-permute-start(bf16[10,256,128]{2,1,0:T(8,128)(2,1)S(1)} %copy-done.1), channel_id=1, source_target_pairs={{0,8},{4,12},{8,0},{12,4},{16,24},{20,28},{24,16},{28,20},{1,9},{5... | collective-permute-start | bytes 1966088 | tf_op jit(solution)/shard_map/ppermute | solution.py:148
  64.2 33.7 %collective-permute-start.15 = (bf16[10,256,128]{2,1,0:T(8,128)(2,1)S(1)}, bf16[10,256,128]{2,1,0:T(8,128)(2,1)S(1)}, u32[]{:S(2)}, u32[]{:S(2)}) collective-permute-start(bf16[10,256,128]{2,1,0:T(8,128)(2,1)S(1)} %copy-done.1), channel_id=1, source_target_pairs={{8,16},{12,20},{16,8},{20,12},{9,17},{13,21},{17,9},{21,13},{10,18... | collective-permute-start | bytes 1966088 | tf_op jit(solution)/shard_map/ppermute | solution.py:148
  65.1 11.5 %copy-start.4 = (s32[10]{0:T(128)S(1)}, s32[10]{0:T(128)}, u32[]{:S(2)}) copy-start(s32[10]{0:T(128)} %target_ref.1) | copy-start | bytes 124
  79.0 6.4 %collective-permute-start.12 = (bf16[104,1024]{1,0:T(8,128)(2,1)S(1)}, bf16[104,1024]{1,0:T(8,128)(2,1)S(1)}, u32[]{:S(2)}, u32[]{:S(2)}) collective-permute-start(bf16[104,1024]{1,0:T(8,128)(2,1)S(1)} %get-tuple-element.36), channel_id=1, source_target_pairs={{0,4},{4,0},{8,12},{12,8},{16,20},{20,16},{24,28},{28,24},{1,5},{5... | collective-permute-start | bytes 638984 | tf_op jit(solution)/shard_map/ppermute | solution.py:151
  80.5 12.5 %collective-permute-start.16 = (bf16[5,256,128]{2,1,0:T(8,128)(2,1)S(1)}, bf16[5,256,128]{2,1,0:T(8,128)(2,1)S(1)}, u32[]{:S(2)}, u32[]{:S(2)}) collective-permute-start(bf16[5,256,128]{2,1,0:T(8,128)(2,1)S(1)} %collective-permute-done.8.refs_0_), channel_id=1, source_target_pairs={{8,0},{12,4},{16,24},{20,28},{9,1},{13,5},{17,25},{21,29},{10,2},{... | collective-permute-start | bytes 983048 | tf_op jit(solution)/shard_map/ppermute | solution.py:148
  81.8 16.1 %collective-permute-start.17 = (bf16[5,256,128]{2,1,0:T(8,128)(2,1)S(1)}, bf16[5,256,128]{2,1,0:T(8,128)(2,1)S(1)}, u32[]{:S(2)}, u32[]{:S(2)}) collective-permute-start(bf16[5,256,128]{2,1,0:T(8,128)(2,1)S(1)} %collective-permute-done.11.refs_1_), channel_id=1, source_target_pairs={{8,0},{12,4},{16,24},{20,28},{9,1},{13,5},{17,25},{21,29},{10,2},{... | collective-permute-start | bytes 983048 | tf_op jit(solution)/shard_map/ppermute | solution.py:148
  85.4 5.8 %collective-permute-start.14 = (bf16[104,1024]{1,0:T(8,128)(2,1)S(1)}, bf16[104,1024]{1,0:T(8,128)(2,1)S(1)}, u32[]{:S(2)}, u32[]{:S(2)}) collective-permute-start(bf16[104,1024]{1,0:T(8,128)(2,1)S(1)} %get-tuple-element.40), channel_id=1, source_target_pairs={{0,4},{4,0},{8,12},{12,8},{16,20},{20,16},{24,28},{28,24},{1,5},{5... | collective-permute-start | bytes 638984 | tf_op jit(solution)/shard_map/ppermute | solution.py:151
  99.4 7.5 %collective-permute-start.19 = (bf16[104,1024]{1,0:T(8,128)(2,1)S(1)}, bf16[104,1024]{1,0:T(8,128)(2,1)S(1)}, u32[]{:S(2)}, u32[]{:S(2)}) collective-permute-start(bf16[104,1024]{1,0:T(8,128)(2,1)S(1)} %get-tuple-element.44), channel_id=1, source_target_pairs={{0,4},{4,0},{8,12},{12,8},{16,20},{20,16},{24,28},{28,24},{1,5},{5... | collective-permute-start | bytes 638984 | tf_op jit(solution)/shard_map/ppermute | solution.py:151
  100.4 8.8 %collective-permute-start.18 = (bf16[104,1024]{1,0:T(8,128)(2,1)S(1)}, bf16[104,1024]{1,0:T(8,128)(2,1)S(1)}, u32[]{:S(2)}, u32[]{:S(2)}) collective-permute-start(bf16[104,1024]{1,0:T(8,128)(2,1)S(1)} %get-tuple-element.43), channel_id=1, source_target_pairs={{0,4},{4,0},{8,12},{12,8},{16,20},{20,16},{24,28},{28,24},{1,5},{5... | collective-permute-start | bytes 638984 | tf_op jit(solution)/shard_map/ppermute | solution.py:151

commit v3 on v2

--- a/solution.py
+++ b/solution.py
@@ -156,14 +156,11 @@
     early = capacity // 2
     ends = [(1, 0), (2, 3)]
 
-    def spread(array):
-        stages, stage = [], 1
-        while stage < owners:
-            stages, stage = [stage] + stages, 2 * stage
-        for stage in stages:
-            other = lax.ppermute(array, "clus", [(p, p ^ stage) for p in range(owners)])
-            array = jnp.concatenate([array, other], axis=0)
-        return array
+    stages = [1 << bit for bit in reversed(range((owners - 1).bit_length()))]
+
+    def double(array, stage):
+        other = lax.ppermute(array, "clus", [(p, p ^ stage) for p in range(owners)])
+        return jnp.concatenate([array, other], axis=0)
 
     v_far, v_near, v_middle = (
         move(v_factors, far),
@@ -178,12 +175,13 @@
         moved=3 * columns * width,
     )(position, incident)
     x_other = across(packed)
-    slots = spread(block_slot)
+    slots = block_slot
+    for stage in stages:
+        slots = double(slots, stage)
     v_far, slots = lax.optimization_barrier((v_far, slots))
     v_ends = move(v_far, ends)
     u_first = after(u_factors, v_far)
     u_far = [move(u_first[part], far) for part in (slice(0, early), slice(early, capacity))]
-    u_near, u_middle = move(u_first, near), move(u_first, middle)
     u_ends = [move(part, ends) for part in u_far]
 
     partial, sent = call(
@@ -197,13 +195,25 @@
         flops=4 * blocks * columns * seg * PLACES * rank_max,
         moved=3 * columns * width + 2 * PLACES * v_factors.size,
     )(position, block_source, incident, x_other, v_factors, v_near, v_far, v_middle, v_ends)
-    rank_index = lax.broadcasted_iota(jnp.int32, (blocks, 1, 1, rank_max), 3)
-    compressed = jnp.where(
-        rank_index < block_rank[:, None, None, None],
-        partial + across(sent).astype(jnp.float32),
-        0.0,
-    ).astype(jnp.bfloat16)
-    gathered = spread(after(compressed, u_far[0]))
+    received = across(sent)
+    u_next = after(u_factors, received)
+    u_near, u_middle = move(u_next, near), move(u_next, middle)
+
+    def chain(_, unused):
+        rank_index = lax.broadcasted_iota(jnp.int32, (blocks, 1, 1, rank_max), 3)
+        rows = jnp.where(
+            rank_index < block_rank[:, None, None, None],
+            partial + received.astype(jnp.float32),
+            0.0,
+        ).astype(jnp.bfloat16)
+        for stage in stages:
+            rows = double(rows, stage)
+        return rows
+
+    rounds = 1 + jnp.minimum(me, 0)
+    gathered = lax.fori_loop(
+        0, rounds, chain, jnp.zeros((owners * blocks, 2, padded, rank_max), jnp.bfloat16)
+    )
     wanted = owner * capacity + lax.broadcasted_iota(jnp.int32, (capacity, slots.shape[0]), 0)
     order = lax.broadcasted_iota(jnp.int32, (capacity, slots.shape[0]), 1)
     feeding = jnp.max(jnp.where(wanted == slots[None, :], order, -1), axis=1)
@@ -213,7 +223,7 @@
         [SMEM, SMEM, VMEM],
         "land",
         moved=2 * gathered.size * (1 + clusters),
-    )(feeding, slot_target, after(gathered, u_far[1]))
+    )(feeding, slot_target, after(gathered, u_far[0]))
 
     chunk = jax.ShapeDtypeStruct((columns, clusters * seg), jnp.bfloat16)
     own_parts, other_parts = [None] * PLACES, [None] * PLACES
@@ -229,6 +239,8 @@
             slot_rows = after(slot_rows, own_parts[finished[-1]])
         if len(finished) > 1:
             slot_rows = after(slot_rows, other_parts[finished[-2]])
+        if len(finished) == PLACES - 1:
+            slot_rows = after(slot_rows, other_parts[finished[-1]])
         own, other = call(
             functools.partial(expand_body, seg, columns, choices),
             [chunk, chunk],
@@ -310,6 +322,7 @@
     fits = (
         lax.axis_size("rhs") == 2 * PLACES
         and v_factors.shape[1] % 128 == 0
+        and owners > 1
         and owners & (owners - 1) == 0
     )
     return (paired if fits else gathered_plan)(incident, v_factors, *rest)

time: 112 us -> 98.6 us (0.88)
  waiting for transfers between devices: 68 us -> 46.3 us
  other arithmetic: 0.74 us -> 4.66 us
  local copies, waits for them, and re-layouts: 1.52 us -> 3.39 us
  starting transfers between devices: 30.1 us -> 31.9 us
  Pallas kernels: 10.5 us -> 12 us
    ppermute x10, waiting for transfers between devices: 44.8 us -> 16.7 us  [move(): lax.ppermute(array, 'rhs', [(2 * a + i, 2 * b + i) for a, b in pairs for...]
    ppermute x4, waiting for transfers between devices: 8.37 us -> 11.7 us  [double(): other = lax.ppermute(array, 'clus', [(p, p ^ stage) for p in range(owners)])]
    ppermute x6, waiting for transfers between devices: 14.8 us -> 17.9 us  [across(): return lax.ppermute(array, 'rhs', [(p, p ^ 1) for p in range(2 * PLACES)])]
    ppermute x10, starting transfers between devices: 18.2 us -> 21.2 us  [move(): lax.ppermute(array, 'rhs', [(2 * a + i, 2 * b + i) for a, b in pairs for...]
    concatenate x4, other arithmetic: 0.32 us -> 3.18 us  [double(): return jnp.concatenate([array, other], axis=0)]
    ppermute x6, starting transfers between devices: 8.77 us -> 7.48 us  [across(): return lax.ppermute(array, 'rhs', [(p, p ^ 1) for p in range(2 * PLACES)])]
    broadcast_in_dim x0 -> x1, local copies, waits for them, and re-layouts: none -> 1.15 us  [paired(): jnp.zeros((owners * blocks, 2, padded, rank_max), jnp.bfloat16)]
  transfers between devices with their start and end apart: 20 -> 20, of which waited for: 14 -> 13; matrix products, arithmetic and copies ran while one was open for 1% -> 7% of each run, Pallas kernels for 5% -> 8%
where the time goes in v3:
time: 98.6 us; the launch traced here: 98.3 us
  waiting for transfers between devices  46.3 us (47%)
  starting transfers between devices  31.9 us (32%)
  Pallas kernels  12 us (12%)
  other arithmetic  4.66 us (5%)
  local copies, waits for them, and re-layouts  3.39 us (3%)
    ppermute x10, starting transfers between devices, move(): lax.ppermute(array, 'rhs', [(2 * a + i, 2 * b + i) for a, b in pairs for...  21.2 us
    ppermute x6, waiting for transfers between devices, across(): return lax.ppermute(array, 'rhs', [(p, p ^ 1) for p in range(2 * PLACES)])  17.9 us
    ppermute x10, waiting for transfers between devices, move(): lax.ppermute(array, 'rhs', [(2 * a + i, 2 * b + i) for a, b in pairs for...  16.7 us
    ppermute x4, waiting for transfers between devices, double(): other = lax.ppermute(array, 'clus', [(p, p ^ stage) for p in range(owners)])  11.7 us
    ppermute x6, starting transfers between devices, across(): return lax.ppermute(array, 'rhs', [(p, p ^ 1) for p in range(2 * PLACES)])  7.48 us
    pallas_call x4, Pallas kernels, paired(): call(functools.partial(expand_body, seg, columns, choices), [chunk, chunk...  5.56 us
    concatenate x4, other arithmetic, double(): return jnp.concatenate([array, other], axis=0)  3.18 us
    ppermute x4, starting transfers between devices, double(): other = lax.ppermute(array, 'clus', [(p, p ^ stage) for p in range(owners)])  3.18 us
  transfers between devices with their start and end apart: 20, of which 13 were waited for; matrix products, arithmetic and copies ran while one was open for 7% of the time, Pallas kernels for 8%

profile of v3, /device:TPU:0, one launch (start us, length us, event | category | flops | bytes accessed | tf_op | source)
XLA Modules:
  0.0 98.3 jit_solution(9939192670548075058)
XLA Ops:
  0.1 1.5 %copy-done = bf16[104,8192]{1,0:T(8,128)(2,1)S(1)} copy-done((bf16[104,8192]{1,0:T(8,128)(2,1)S(1)}, bf16[104,8192]{1,0:T(8,128)(2,1)}, u32[]{:S(2)}) %copy-start) | copy-done | bytes 1703960
  2.2 3.0 %collective-permute-start.5 = (bf16[104,4096]{1,0:T(8,128)(2,1)S(1)}, bf16[104,4096]{1,0:T(8,128)(2,1)S(1)}, u32[]{:S(2)}, u32[]{:S(2)}) collective-permute-start(bf16[104,4096]{1,0:T(8,128)(2,1)S(1)} %pack.1), channel_id=1, source_target_pairs={{0,4},{4,0},{8,12},{12,8},{16,20},{20,16},{24,28},{28,24},{1,5},{5... | collective-permute-start | bytes 2555912 | tf_op jit(solution)/shard_map/ppermute | solution.py:151
  5.2 2.6 %collective-permute-start.2 = (bf16[5,256,128]{2,1,0:T(8,128)(2,1)S(1)}, bf16[5,256,128]{2,1,0:T(8,128)(2,1)S(1)}, u32[]{:S(2)}, u32[]{:S(2)}) collective-permute-start(bf16[5,256,128]{2,1,0:T(8,128)(2,1)S(1)} %copy-done.2), channel_id=1, source_target_pairs={{0,16},{4,20},{8,24},{12,28},{16,0},{20,4},{24,8},{28,12},{1,17},{... | collective-permute-start | bytes 983048 | tf_op jit(solution)/shard_map/ppermute | solution.py:148
  7.8 1.6 %collective-permute-start.6 = (bf16[5,256,128]{2,1,0:T(8,128)(2,1)S(1)}, bf16[5,256,128]{2,1,0:T(8,128)(2,1)S(1)}, u32[]{:S(2)}, u32[]{:S(2)}) collective-permute-start(bf16[5,256,128]{2,1,0:T(8,128)(2,1)S(1)} %copy-done.2), channel_id=1, source_target_pairs={{0,8},{4,12},{8,0},{12,4},{16,24},{20,28},{24,16},{28,20},{1,9},{5... | collective-permute-start | bytes 983048 | tf_op jit(solution)/shard_map/ppermute | solution.py:148
  10.1 1.6 %collective-permute-start.3 = (s32[5]{0:T(128)S(1)}, s32[5]{0:T(128)S(1)}, u32[]{:S(2)}, u32[]{:S(2)}) collective-permute-start(s32[5]{0:T(128)S(1)} %copy-done.5), channel_id=1, source_target_pairs={{0,2},{1,3},{2,0},{3,1},{4,6},{5,7},{6,4},{7,5},{8,10},{9,11},{10,... | collective-permute-start | bytes 68 | tf_op jit(solution)/shard_map/ppermute | solution.py:162
  11.7 2.0 %collective-permute-done.3 = s32[5]{0:T(128)S(1)} collective-permute-done((s32[5]{0:T(128)S(1)}, s32[5]{0:T(128)S(1)}, u32[]{:S(2)}, u32[]{:S(2)}) %collective-permute-start.3) | collective-permute-done | bytes 52 | tf_op jit(solution)/shard_map/ppermute | solution.py:162
  15.0 8.6 %collective-permute-done.2.v2 = bf16[5,256,128]{2,1,0:T(8,128)(2,1)S(1)} collective-permute-done((bf16[5,256,128]{2,1,0:T(8,128)(2,1)S(1)}, bf16[5,256,128]{2,1,0:T(8,128)(2,1)S(1)}, u32[]{:S(2)}, u32[]{:S(2)}) %collective-permute-start.2) | collective-permute-done | bytes 327712 | tf_op jit(solution)/shard_map/ppermute | solution.py:148
  25.6 3.6 %collective-permute-start.10 = (bf16[5,256,128]{2,1,0:T(8,128)(2,1)S(1)}, bf16[5,256,128]{2,1,0:T(8,128)(2,1)S(1)}, u32[]{:S(2)}, u32[]{:S(2)}) collective-permute-start(bf16[5,256,128]{2,1,0:T(8,128)(2,1)S(1)} %get-tuple-element.93), channel_id=1, source_target_pairs={{0,16},{4,20},{8,24},{12,28},{16,0},{20,4},{24,8},{28,12},{1,17},{... | collective-permute-start | bytes 983048 | tf_op jit(solution)/shard_map/ppermute | solution.py:148
  29.2 3.6 %collective-permute-done.8.v4 = bf16[5,256,128]{2,1,0:T(8,128)(2,1)S(1)} collective-permute-done((bf16[5,256,128]{2,1,0:T(8,128)(2,1)S(1)}, bf16[5,256,128]{2,1,0:T(8,128)(2,1)S(1)}, u32[]{:S(2)}, u32[]{:S(2)}) %collective-permute-start.8) | collective-permute-done | bytes 327712 | tf_op jit(solution)/shard_map/ppermute | solution.py:148
  32.8 2.2 %compress.1 = (f32[5,2,112,128]{3,2,1,0:T(8,128)}, bf16[5,2,112,128]{3,2,1,0:T(8,128)(2,1)S(1)}) custom-call(s32[2]{0:T(128)S(1)} %pad_add_fusion.pos_ref, s32[5]{0:T(128)S(1)} %copy-done.3, bf16[104,8192]{1,0:T(8,128)(2,1)S(1)} %copy-done, bf16[104,4096]{1,0:T(8,128)(2,1)S(1)} %collective-permute-done.5.xn_ref, bf16[5,256,128]{2,1,0:T(8,128)(2,1)S(1)} %copy-done.2, ...), custom_call_target="tpu_custom_call" | custom-call | flops 272629760 | bytes 3866624 | tf_op jit(solution)/shard_map/compress/pallas_call | solution.py:187
  35.5 3.6 %collective-permute-start.11 = (bf16[5,256,128]{2,1,0:T(8,128)(2,1)}, bf16[5,256,128]{2,1,0:T(8,128)(2,1)S(1)}, u32[]{:S(2)}, u32[]{:S(2)}) collective-permute-start(bf16[5,256,128]{2,1,0:T(8,128)(2,1)} %get-tuple-element.92), channel_id=1, source_target_pairs={{0,16},{4,20},{8,24},{12,28},{16,0},{20,4},{24,8},{28,12},{1,17},{... | collective-permute-start | bytes 983048 | tf_op jit(solution)/shard_map/ppermute | solution.py:148
  39.3 2.3 %collective-permute-done.9 = bf16[5,2,112,128]{3,2,1,0:T(8,128)(2,1)S(1)} collective-permute-done((bf16[5,2,112,128]{3,2,1,0:T(8,128)(2,1)S(1)}, bf16[5,2,112,128]{3,2,1,0:T(8,128)(2,1)S(1)}, u32[]{:S(2)}, u32[]{:S(2)}) %collective-permute-start.9) | collective-permute-done | bytes 286752 | tf_op jit(solution)/shard_map/ppermute | solution.py:151
  41.6 4.7 %collective-permute-start.13 = (bf16[10,256,128]{2,1,0:T(8,128)(2,1)S(1)}, bf16[10,256,128]{2,1,0:T(8,128)(2,1)S(1)}, u32[]{:S(2)}, u32[]{:S(2)}) collective-permute-start(bf16[10,256,128]{2,1,0:T(8,128)(2,1)S(1)} %copy-done.1), channel_id=1, source_target_pairs={{0,8},{4,12},{8,0},{12,4},{16,24},{20,28},{24,16},{28,20},{1,9},{5... | collective-permute-start | bytes 1966088 | tf_op jit(solution)/shard_map/ppermute | solution.py:148
  47.0 4.1 %collective-permute-done.10.refs_0_ = bf16[5,256,128]{2,1,0:T(8,128)(2,1)S(1)} collective-permute-done((bf16[5,256,128]{2,1,0:T(8,128)(2,1)S(1)}, bf16[5,256,128]{2,1,0:T(8,128)(2,1)S(1)}, u32[]{:S(2)}, u32[]{:S(2)}) %collective-permute-start.10) | collective-permute-done | bytes 327712 | tf_op jit(solution)/shard_map/ppermute | solution.py:148
  52.2 14.5 %while.10 = (s32[]{:T(128)}, bf16[20,2,112,128]{3,2,1,0:T(8,128)(2,1)}, s32[]{:T(128)}, s32[5]{0:T(128)S(1)}, bf16[5,2,112,128]{3,2,1,0:T(8,128)(2,1)S(1)}, /*index=5*/f32[5,2,112,128]{3,2,1,0:T(8,128)}, s32[]{:T(128)}) while((s32[]{:T(128)}, bf16[20,2,112,128]{3,2,1,0:T(8,128)(2,1)}, s32[]{:T(128)}, s32[5]{0:T(128)S(1)}, ...), condition=%wide.region_2.3_spmd, body=%wide.region_1.2_spmd.sunk | while | flops 2007682 | bytes 8029617 | solution.py:214
  53.4 1.6 %collective-permute-start = (bf16[5,2,112,128]{3,2,1,0:T(8,128)(2,1)S(1)}, bf16[5,2,112,128]{3,2,1,0:T(8,128)(2,1)S(1)}, u32[]{:S(2)}, u32[]{:S(2)}) collective-permute-start(bf16[5,2,112,128]{3,2,1,0:T(8,128)(2,1)S(1)} %select_convert_fusion.2), channel_id=1, source_target_pairs={{0,2},{1,3},{2,0},{3,1},{4,6},{5,7},{6,4},{7,5},{8,10},{9,11},{10,... | collective-permute-start | bytes 860168 | tf_op jit(solution)/shard_map/while/body/ppermute | solution.py:162
  55.0 6.3 %collective-permute-done = bf16[5,2,112,128]{3,2,1,0:T(8,128)(2,1)S(1)} collective-permute-done((bf16[5,2,112,128]{3,2,1,0:T(8,128)(2,1)S(1)}, bf16[5,2,112,128]{3,2,1,0:T(8,128)(2,1)S(1)}, u32[]{:S(2)}, u32[]{:S(2)}) %collective-permute-start) | collective-permute-done | bytes 286752 | tf_op jit(solution)/shard_map/while/body/ppermute | solution.py:162
  62.2 2.3 %collective-permute-done.1 = bf16[10,2,112,128]{3,2,1,0:T(8,128)(2,1)} collective-permute-done((bf16[10,2,112,128]{3,2,1,0:T(8,128)(2,1)}, bf16[10,2,112,128]{3,2,1,0:T(8,128)(2,1)}, u32[]{:S(2)}, u32[]{:S(2)}) %collective-permute-start.1) | collective-permute-done | bytes 573472 | tf_op jit(solution)/shard_map/while/body/ppermute | solution.py:162
  64.5 2.2 %pad_maximum_fusion.5 = bf16[20,2,112,128]{3,2,1,0:T(8,128)(2,1)} fusion(bf16[10,2,112,128]{3,2,1,0:T(8,128)(2,1)} %collective-permute-done.1, bf16[5,2,112,128]{3,2,1,0:T(8,128)(2,1)S(1)} %collective-permute-done, bf16[5,2,112,128]{3,2,1,0:T(8,128)(2,1)S(1)} %select_convert_fusion.2), kind=kLoop, calls=%fused_computation.clone.1 | loop fusion | flops 1146880 | bytes 2293760 | tf_op jit(solution)/shard_map/while/body/concatenate | solution.py:163
  66.7 1.6 %land.1.rows_ref = bf16[4,2,112,1280]{3,2,1,0:T(8,128)(2,1)S(1)} custom-call(s32[10]{0:T(128)S(1)} %select_reduce_fusion.index_ref, s32[10]{0:T(128)S(1)} %copy-done.4, bf16[20,2,112,128]{3,2,1,0:T(8,128)(2,1)} %get-tuple-element.64.comp_ref), custom_call_target="tpu_custom_call" | custom-call | bytes 5734400 | tf_op jit(solution)/shard_map/land/pallas_call | solution.py:220
  68.3 1.4 %expand.4 = (bf16[104,1024]{1,0:T(8,128)(2,1)S(1)}, bf16[104,1024]{1,0:T(8,128)(2,1)S(1)}) custom-call(s32[2]{0:T(128)S(1)} %pad_add_fusion.pos_ref, bf16[4,2,112,1280]{3,2,1,0:T(8,128)(2,1)S(1)} %land.1.rows_ref, bf16[10,256,128]{2,1,0:T(8,128)(2,1)S(1)} %copy-done.1), custom_call_target="tpu_custom_call" | custom-call | flops 545259520 | bytes 3375104 | tf_op jit(solution)/shard_map/expand/pallas_call | solution.py:244
  69.8 1.3 %collective-permute-start.17 = (bf16[5,256,128]{2,1,0:T(8,128)(2,1)S(1)}, bf16[5,256,128]{2,1,0:T(8,128)(2,1)S(1)}, u32[]{:S(2)}, u32[]{:S(2)}) collective-permute-start(bf16[5,256,128]{2,1,0:T(8,128)(2,1)S(1)} %collective-permute-done.10.refs_0_), channel_id=1, source_target_pairs={{8,0},{12,4},{16,24},{20,28},{9,1},{13,5},{17,25},{21,29},{10,2},{... | collective-permute-start | bytes 983048 | tf_op jit(solution)/shard_map/ppermute | solution.py:148
  72.4 1.4 %expand.5 = (bf16[104,1024]{1,0:T(8,128)(2,1)S(1)}, bf16[104,1024]{1,0:T(8,128)(2,1)S(1)}) custom-call(s32[2]{0:T(128)S(1)} %pad_add_fusion.pos_ref, bf16[4,2,112,1280]{3,2,1,0:T(8,128)(2,1)S(1)} %land.1.rows_ref, bf16[5,256,128]{2,1,0:T(8,128)(2,1)S(1)} %collective-permute-done.10.refs_0_, bf16[5,256,128]{2,1,0:T(8,128)(2,1)S(1)} %collective-permute-done.11.refs_1_), custom_call_target="tpu_custom_call" | custom-call | flops 545259520 | bytes 3375104 | tf_op jit(solution)/shard_map/expand/pallas_call | solution.py:244
  73.8 3.3 %collective-permute-done.12.refs_4_ = bf16[104,1024]{1,0:T(8,128)(2,1)S(1)} collective-permute-done((bf16[104,1024]{1,0:T(8,128)(2,1)S(1)}, bf16[104,1024]{1,0:T(8,128)(2,1)S(1)}, u32[]{:S(2)}, u32[]{:S(2)}) %collective-permute-start.12) | collective-permute-done | bytes 213024 | tf_op jit(solution)/shard_map/ppermute | solution.py:151
  77.4 1.4 %expand.6 = (bf16[104,1024]{1,0:T(8,128)(2,1)S(1)}, bf16[104,1024]{1,0:T(8,128)(2,1)S(1)}) custom-call(s32[2]{0:T(128)S(1)} %pad_add_fusion.pos_ref, bf16[4,2,112,1280]{3,2,1,0:T(8,128)(2,1)S(1)} %land.1.rows_ref, bf16[10,256,128]{2,1,0:T(8,128)(2,1)S(1)} %collective-permute-done.13.refs_0_), custom_call_target="tpu_custom_call" | custom-call | flops 545259520 | bytes 3375104 | tf_op jit(solution)/shard_map/expand/pallas_call | solution.py:244
  78.7 1.8 %collective-permute-start.15 = (bf16[104,1024]{1,0:T(8,128)(2,1)S(1)}, bf16[104,1024]{1,0:T(8,128)(2,1)S(1)}, u32[]{:S(2)}, u32[]{:S(2)}) collective-permute-start(bf16[104,1024]{1,0:T(8,128)(2,1)S(1)} %get-tuple-element.76), channel_id=1, source_target_pairs={{0,4},{4,0},{8,12},{12,8},{16,20},{20,16},{24,28},{28,24},{1,5},{5... | collective-permute-start | bytes 638984 | tf_op jit(solution)/shard_map/ppermute | solution.py:151
  80.6 4.7 %collective-permute-done.14.refs_6_ = bf16[104,1024]{1,0:T(8,128)(2,1)S(1)} collective-permute-done((bf16[104,1024]{1,0:T(8,128)(2,1)S(1)}, bf16[104,1024]{1,0:T(8,128)(2,1)S(1)}, u32[]{:S(2)}, u32[]{:S(2)}) %collective-permute-start.14) | collective-permute-done | bytes 213024 | tf_op jit(solution)/shard_map/ppermute | solution.py:151
  85.3 2.8 %collective-permute-done.15.refs_5_ = bf16[104,1024]{1,0:T(8,128)(2,1)S(1)} collective-permute-done((bf16[104,1024]{1,0:T(8,128)(2,1)S(1)}, bf16[104,1024]{1,0:T(8,128)(2,1)S(1)}, u32[]{:S(2)}, u32[]{:S(2)}) %collective-permute-start.15) | collective-permute-done | bytes 213024 | tf_op jit(solution)/shard_map/ppermute | solution.py:151
  88.5 1.4 %expand.7 = (bf16[104,1024]{1,0:T(8,128)(2,1)S(1)}, bf16[104,1024]{1,0:T(8,128)(2,1)S(1)}) custom-call(s32[2]{0:T(128)S(1)} %pad_add_fusion.pos_ref, bf16[4,2,112,1280]{3,2,1,0:T(8,128)(2,1)S(1)} %land.1.rows_ref, bf16[10,256,128]{2,1,0:T(8,128)(2,1)S(1)} %collective-permute-done.16.refs_0_, bf16[5,256,128]{2,1,0:T(8,128)(2,1)S(1)} %collective-permute-done.17.refs_1_, ...), custom_call_target="tpu_custom_call" | custom-call | flops 545259520 | bytes 3375104 | tf_op jit(solution)/shard_map/expand/pallas_call | solution.py:244
  89.9 1.8 %collective-permute-start.19 = (bf16[104,1024]{1,0:T(8,128)(2,1)S(1)}, bf16[104,1024]{1,0:T(8,128)(2,1)S(1)}, u32[]{:S(2)}, u32[]{:S(2)}) collective-permute-start(bf16[104,1024]{1,0:T(8,128)(2,1)S(1)} %get-tuple-element.79), channel_id=1, source_target_pairs={{0,4},{4,0},{8,12},{12,8},{16,20},{20,16},{24,28},{28,24},{1,5},{5... | collective-permute-start | bytes 638984 | tf_op jit(solution)/shard_map/ppermute | solution.py:151
  91.6 4.7 %collective-permute-done.19.refs_7_ = bf16[104,1024]{1,0:T(8,128)(2,1)S(1)} collective-permute-done((bf16[104,1024]{1,0:T(8,128)(2,1)S(1)}, bf16[104,1024]{1,0:T(8,128)(2,1)S(1)}, u32[]{:S(2)}, u32[]{:S(2)}) %collective-permute-start.19) | collective-permute-done | bytes 213024 | tf_op jit(solution)/shard_map/ppermute | solution.py:151
  96.4 1.9 %join.1 = bf16[104,8192]{1,0:T(8,128)(2,1)} custom-call(s32[2]{0:T(128)S(1)} %pad_add_fusion.pos_ref, bf16[104,1024]{1,0:T(8,128)(2,1)S(1)} %get-tuple-element.65.refs_0_, bf16[104,1024]{1,0:T(8,128)(2,1)S(1)} %get-tuple-element.72.refs_1_, bf16[104,1024]{1,0:T(8,128)(2,1)S(1)} %get-tuple-element.67.refs_2_, ...), custom_call_target="tpu_custom_call" | custom-call | bytes 3407872 | tf_op jit(solution)/shard_map/join/pallas_call | solution.py:255
  (42 shorter events, 11.4 us)
Async XLA Ops:
  0.1 1.5 %copy-start = (bf16[104,8192]{1,0:T(8,128)(2,1)S(1)}, bf16[104,8192]{1,0:T(8,128)(2,1)}, u32[]{:S(2)}) copy-start(bf16[104,8192]{1,0:T(8,128)(2,1)} %x_ref.3) | copy-start | bytes 5111812
  1.5 3.7 %copy-start.2 = (bf16[5,256,128]{2,1,0:T(8,128)(2,1)S(1)}, bf16[5,256,128]{2,1,0:T(8,128)(2,1)}, u32[]{:S(2)}) copy-start(bf16[5,256,128]{2,1,0:T(8,128)(2,1)} %v0.1) | copy-start | bytes 983044
  1.5 8.5 %copy-start.5 = (s32[5]{0:T(128)S(1)}, s32[5]{0:T(128)}, u32[]{:S(2)}) copy-start(s32[5]{0:T(128)} %param.14) | copy-start | bytes 64
  1.5 23.3 %copy-start.1 = (bf16[10,256,128]{2,1,0:T(8,128)(2,1)S(1)}, bf16[10,256,128]{2,1,0:T(8,128)(2,1)}, u32[]{:S(2)}) copy-start(bf16[10,256,128]{2,1,0:T(8,128)(2,1)} %refs_0_.1) | copy-start | bytes 1966084
  2.2 30.6 %copy-start.3 = (s32[5]{0:T(128)S(1)}, s32[5]{0:T(128)}, u32[]{:S(2)}) copy-start(s32[5]{0:T(128)} %source_ref.1) | copy-start | bytes 64
  2.2 30.6 %collective-permute-start.5 = (bf16[104,4096]{1,0:T(8,128)(2,1)S(1)}, bf16[104,4096]{1,0:T(8,128)(2,1)S(1)}, u32[]{:S(2)}, u32[]{:S(2)}) collective-permute-start(bf16[104,4096]{1,0:T(8,128)(2,1)S(1)} %pack.1), channel_id=1, source_target_pairs={{0,4},{4,0},{8,12},{12,8},{16,20},{20,16},{24,28},{28,24},{1,5},{5... | collective-permute-start | bytes 2555912 | tf_op jit(solution)/shard_map/ppermute | solution.py:151
  5.2 18.3 %collective-permute-start.2 = (bf16[5,256,128]{2,1,0:T(8,128)(2,1)S(1)}, bf16[5,256,128]{2,1,0:T(8,128)(2,1)S(1)}, u32[]{:S(2)}, u32[]{:S(2)}) collective-permute-start(bf16[5,256,128]{2,1,0:T(8,128)(2,1)S(1)} %copy-done.2), channel_id=1, source_target_pairs={{0,16},{4,20},{8,24},{12,28},{16,0},{20,4},{24,8},{28,12},{1,17},{... | collective-permute-start | bytes 983048 | tf_op jit(solution)/shard_map/ppermute | solution.py:148
  7.8 21.3 %collective-permute-start.6 = (bf16[5,256,128]{2,1,0:T(8,128)(2,1)S(1)}, bf16[5,256,128]{2,1,0:T(8,128)(2,1)S(1)}, u32[]{:S(2)}, u32[]{:S(2)}) collective-permute-start(bf16[5,256,128]{2,1,0:T(8,128)(2,1)S(1)} %copy-done.2), channel_id=1, source_target_pairs={{0,8},{4,12},{8,0},{12,4},{16,24},{20,28},{24,16},{28,20},{1,9},{5... | collective-permute-start | bytes 983048 | tf_op jit(solution)/shard_map/ppermute | solution.py:148
  9.4 19.8 %collective-permute-start.7 = (bf16[5,256,128]{2,1,0:T(8,128)(2,1)S(1)}, bf16[5,256,128]{2,1,0:T(8,128)(2,1)S(1)}, u32[]{:S(2)}, u32[]{:S(2)}) collective-permute-start(bf16[5,256,128]{2,1,0:T(8,128)(2,1)S(1)} %copy-done.2), channel_id=1, source_target_pairs={{8,16},{12,20},{16,8},{20,12},{9,17},{13,21},{17,9},{21,13},{10,18... | collective-permute-start | bytes 983048 | tf_op jit(solution)/shard_map/ppermute | solution.py:148
  10.1 3.6 %collective-permute-start.3 = (s32[5]{0:T(128)S(1)}, s32[5]{0:T(128)S(1)}, u32[]{:S(2)}, u32[]{:S(2)}) collective-permute-start(s32[5]{0:T(128)S(1)} %copy-done.5), channel_id=1, source_target_pairs={{0,2},{1,3},{2,0},{3,1},{4,6},{5,7},{6,4},{7,5},{8,10},{9,11},{10,... | collective-permute-start | bytes 68 | tf_op jit(solution)/shard_map/ppermute | solution.py:162
  13.8 1.1 %collective-permute-start.4 = (s32[10]{0:T(128)S(1)}, s32[10]{0:T(128)S(1)}, u32[]{:S(2)}, u32[]{:S(2)}) collective-permute-start(s32[10]{0:T(128)S(1)} %pad_add_fusion.1), channel_id=1, source_target_pairs={{0,1},{1,0},{2,3},{3,2},{4,5},{5,4},{6,7},{7,6},{8,9},{9,8},{10,11... | collective-permute-start | bytes 128 | tf_op jit(solution)/shard_map/ppermute | solution.py:162
  23.5 9.3 %collective-permute-start.8 = (bf16[5,256,128]{2,1,0:T(8,128)(2,1)S(1)}, bf16[5,256,128]{2,1,0:T(8,128)(2,1)S(1)}, u32[]{:S(2)}, u32[]{:S(2)}) collective-permute-start(bf16[5,256,128]{2,1,0:T(8,128)(2,1)S(1)} %collective-permute-done.2.v2), channel_id=1, source_target_pairs={{8,0},{12,4},{16,24},{20,28},{9,1},{13,5},{17,25},{21,29},{10,2},{... | collective-permute-start | bytes 983048 | tf_op jit(solution)/shard_map/ppermute | solution.py:148
  25.6 25.5 %collective-permute-start.10 = (bf16[5,256,128]{2,1,0:T(8,128)(2,1)S(1)}, bf16[5,256,128]{2,1,0:T(8,128)(2,1)S(1)}, u32[]{:S(2)}, u32[]{:S(2)}) collective-permute-start(bf16[5,256,128]{2,1,0:T(8,128)(2,1)S(1)} %get-tuple-element.93), channel_id=1, source_target_pairs={{0,16},{4,20},{8,24},{12,28},{16,0},{20,4},{24,8},{28,12},{1,17},{... | collective-permute-start | bytes 983048 | tf_op jit(solution)/shard_map/ppermute | solution.py:148
  35.0 17.2 %copy-start.6 = (s32[5]{0:T(128)S(1)}, s32[5]{0:T(128)}, u32[]{:S(2)}) copy-start(s32[5]{0:T(128)} %param.13) | copy-start | bytes 64
  35.0 6.6 %collective-permute-start.9 = (bf16[5,2,112,128]{3,2,1,0:T(8,128)(2,1)S(1)}, bf16[5,2,112,128]{3,2,1,0:T(8,128)(2,1)S(1)}, u32[]{:S(2)}, u32[]{:S(2)}) collective-permute-start(bf16[5,2,112,128]{3,2,1,0:T(8,128)(2,1)S(1)} %get-tuple-element.60), channel_id=1, source_target_pairs={{0,4},{4,0},{8,12},{12,8},{16,20},{20,16},{24,28},{28,24},{1,5},{5... | collective-permute-start | bytes 860168 | tf_op jit(solution)/shard_map/ppermute | solution.py:151
  35.5 35.6 %collective-permute-start.11 = (bf16[5,256,128]{2,1,0:T(8,128)(2,1)}, bf16[5,256,128]{2,1,0:T(8,128)(2,1)S(1)}, u32[]{:S(2)}, u32[]{:S(2)}) collective-permute-start(bf16[5,256,128]{2,1,0:T(8,128)(2,1)} %get-tuple-element.92), channel_id=1, source_target_pairs={{0,16},{4,20},{8,24},{12,28},{16,0},{20,4},{24,8},{28,12},{1,17},{... | collective-permute-start | bytes 983048 | tf_op jit(solution)/shard_map/ppermute | solution.py:148
  41.6 35.7 %collective-permute-start.13 = (bf16[10,256,128]{2,1,0:T(8,128)(2,1)S(1)}, bf16[10,256,128]{2,1,0:T(8,128)(2,1)S(1)}, u32[]{:S(2)}, u32[]{:S(2)}) collective-permute-start(bf16[10,256,128]{2,1,0:T(8,128)(2,1)S(1)} %copy-done.1), channel_id=1, source_target_pairs={{0,8},{4,12},{8,0},{12,4},{16,24},{20,28},{24,16},{28,20},{1,9},{5... | collective-permute-start | bytes 1966088 | tf_op jit(solution)/shard_map/ppermute | solution.py:148
  46.3 42.2 %collective-permute-start.16 = (bf16[10,256,128]{2,1,0:T(8,128)(2,1)S(1)}, bf16[10,256,128]{2,1,0:T(8,128)(2,1)S(1)}, u32[]{:S(2)}, u32[]{:S(2)}) collective-permute-start(bf16[10,256,128]{2,1,0:T(8,128)(2,1)S(1)} %copy-done.1), channel_id=1, source_target_pairs={{8,16},{12,20},{16,8},{20,12},{9,17},{13,21},{17,9},{21,13},{10,18... | collective-permute-start | bytes 1966088 | tf_op jit(solution)/shard_map/ppermute | solution.py:148
  52.2 14.5 %copy-start.4 = (s32[10]{0:T(128)S(1)}, s32[10]{0:T(128)}, u32[]{:S(2)}) copy-start(s32[10]{0:T(128)} %target_ref.1) | copy-start | bytes 124
  53.4 7.9 %collective-permute-start = (bf16[5,2,112,128]{3,2,1,0:T(8,128)(2,1)S(1)}, bf16[5,2,112,128]{3,2,1,0:T(8,128)(2,1)S(1)}, u32[]{:S(2)}, u32[]{:S(2)}) collective-permute-start(bf16[5,2,112,128]{3,2,1,0:T(8,128)(2,1)S(1)} %select_convert_fusion.2), channel_id=1, source_target_pairs={{0,2},{1,3},{2,0},{3,1},{4,6},{5,7},{6,4},{7,5},{8,10},{9,11},{10,... | collective-permute-start | bytes 860168 | tf_op jit(solution)/shard_map/while/body/ppermute | solution.py:162
  62.1 2.3 %collective-permute-start.1 = (bf16[10,2,112,128]{3,2,1,0:T(8,128)(2,1)}, bf16[10,2,112,128]{3,2,1,0:T(8,128)(2,1)}, u32[]{:S(2)}, u32[]{:S(2)}) collective-permute-start(bf16[10,2,112,128]{3,2,1,0:T(8,128)(2,1)} %pad_maximum_fusion.4), channel_id=1, source_target_pairs={{0,1},{1,0},{2,3},{3,2},{4,5},{5,4},{6,7},{7,6},{8,9},{9,8},{10,11... | collective-permute-start | bytes 1720328 | tf_op jit(solution)/shard_map/while/body/ppermute | solution.py:162
  69.7 7.4 %collective-permute-start.12 = (bf16[104,1024]{1,0:T(8,128)(2,1)S(1)}, bf16[104,1024]{1,0:T(8,128)(2,1)S(1)}, u32[]{:S(2)}, u32[]{:S(2)}) collective-permute-start(bf16[104,1024]{1,0:T(8,128)(2,1)S(1)} %get-tuple-element.69), channel_id=1, source_target_pairs={{0,4},{4,0},{8,12},{12,8},{16,20},{20,16},{24,28},{28,24},{1,5},{5... | collective-permute-start | bytes 638984 | tf_op jit(solution)/shard_map/ppermute | solution.py:151
  69.8 18.3 %collective-permute-start.17 = (bf16[5,256,128]{2,1,0:T(8,128)(2,1)S(1)}, bf16[5,256,128]{2,1,0:T(8,128)(2,1)S(1)}, u32[]{:S(2)}, u32[]{:S(2)}) collective-permute-start(bf16[5,256,128]{2,1,0:T(8,128)(2,1)S(1)} %collective-permute-done.10.refs_0_), channel_id=1, source_target_pairs={{8,0},{12,4},{16,24},{20,28},{9,1},{13,5},{17,25},{21,29},{10,2},{... | collective-permute-start | bytes 983048 | tf_op jit(solution)/shard_map/ppermute | solution.py:148
  71.1 17.4 %collective-permute-start.18 = (bf16[5,256,128]{2,1,0:T(8,128)(2,1)S(1)}, bf16[5,256,128]{2,1,0:T(8,128)(2,1)S(1)}, u32[]{:S(2)}, u32[]{:S(2)}) collective-permute-start(bf16[5,256,128]{2,1,0:T(8,128)(2,1)S(1)} %collective-permute-done.11.refs_1_), channel_id=1, source_target_pairs={{8,0},{12,4},{16,24},{20,28},{9,1},{13,5},{17,25},{21,29},{10,2},{... | collective-permute-start | bytes 983048 | tf_op jit(solution)/shard_map/ppermute | solution.py:148
  77.1 8.2 %collective-permute-start.14 = (bf16[104,1024]{1,0:T(8,128)(2,1)S(1)}, bf16[104,1024]{1,0:T(8,128)(2,1)S(1)}, u32[]{:S(2)}, u32[]{:S(2)}) collective-permute-start(bf16[104,1024]{1,0:T(8,128)(2,1)S(1)} %get-tuple-element.74), channel_id=1, source_target_pairs={{0,4},{4,0},{8,12},{12,8},{16,20},{20,16},{24,28},{28,24},{1,5},{5... | collective-permute-start | bytes 638984 | tf_op jit(solution)/shard_map/ppermute | solution.py:151
  78.7 9.3 %collective-permute-start.15 = (bf16[104,1024]{1,0:T(8,128)(2,1)S(1)}, bf16[104,1024]{1,0:T(8,128)(2,1)S(1)}, u32[]{:S(2)}, u32[]{:S(2)}) collective-permute-start(bf16[104,1024]{1,0:T(8,128)(2,1)S(1)} %get-tuple-element.76), channel_id=1, source_target_pairs={{0,4},{4,0},{8,12},{12,8},{16,20},{20,16},{24,28},{28,24},{1,5},{5... | collective-permute-start | bytes 638984 | tf_op jit(solution)/shard_map/ppermute | solution.py:151
  89.9 6.5 %collective-permute-start.19 = (bf16[104,1024]{1,0:T(8,128)(2,1)S(1)}, bf16[104,1024]{1,0:T(8,128)(2,1)S(1)}, u32[]{:S(2)}, u32[]{:S(2)}) collective-permute-start(bf16[104,1024]{1,0:T(8,128)(2,1)S(1)} %get-tuple-element.79), channel_id=1, source_target_pairs={{0,4},{4,0},{8,12},{12,8},{16,20},{20,16},{24,28},{28,24},{1,5},{5... | collective-permute-start | bytes 638984 | tf_op jit(solution)/shard_map/ppermute | solution.py:151

commit v4 on v3

--- a/solution.py
+++ b/solution.py
@@ -26,16 +26,21 @@
     )
 
 
-def pack_body(seg, pos_ref, x_ref, out_ref):
+def pack_body(seg, pos_ref, x_ref, *out_refs):
     half = 1 - pos_ref[0]
-    for piece in range(out_ref.shape[1] // seg):
+    pieces = out_refs[0].shape[1] // seg
+    for piece in range(pieces * len(out_refs)):
         start = pl.multiple_of((2 * piece + half) * seg, seg)
-        out_ref[:, piece * seg : (piece + 1) * seg] = x_ref[:, pl.ds(start, seg)]
-
-
-def compress_body(seg, pos_ref, source_ref, x_ref, xn_ref, v0, v1, v2, v3, v4, out_ref, send_ref):
+        place = piece % pieces * seg
+        out_refs[piece // pieces][:, place : place + seg] = x_ref[:, pl.ds(start, seg)]
+
+
+def compress_body(seg, pos_ref, source_ref, x_ref, xl_ref, xh_ref, *refs):
+    v0, v1, v2, v3, v4, out_ref, send_ref, xn_ref = refs
     half, mine = pos_ref[0], pos_ref[1]
     columns = x_ref.shape[0]
+    xn_ref[:, : xl_ref.shape[1]] = xl_ref[...]
+    xn_ref[:, xl_ref.shape[1] :] = xh_ref[...]
     out_ref[...] = jnp.zeros_like(out_ref)
 
     def run(shards):
@@ -113,18 +118,37 @@
         other_ref[:, span] = acc[target, 1 - half, :columns].astype(other_ref.dtype)
 
 
-def join_body(seg, clusters, pos_ref, *refs):
+def expand_own_body(seg, columns, pos_ref, rows_ref, u_ref, side_ref, out_ref, acc):
+    half = pos_ref[0]
+    clusters, sides, padded, depth = rows_ref.shape
+    rows = rows_ref[:, half].reshape(clusters * padded, depth)
+    for shard, place in ((u_ref, half), (side_ref, 1 - half)):
+        factor = jnp.concatenate([shard[slot] for slot in range(shard.shape[0])], axis=1)
+        product = lax.dot_general(
+            rows, factor, (((1,), (1,)), ((), ())), preferred_element_type=jnp.float32
+        )
+        acc[...] = product.reshape(clusters, padded, seg)
+        for target in range(clusters):
+            start = pl.multiple_of((2 * target + place) * seg, seg)
+            out_ref[:, pl.ds(start, seg)] = acc[target, :columns].astype(out_ref.dtype)
+
+
+def join_body(seg, clusters, pos_ref, first_ref, *refs):
     out_ref = refs[-1]
     half, mine = pos_ref[0], pos_ref[1]
-    for step in range(PLACES):
+    for target in range(clusters):
+        start = pl.multiple_of((target * PLACES + mine) * 2 * seg, 2 * seg)
+        span = slice(2 * target * seg, 2 * (target + 1) * seg)
+        out_ref[:, pl.ds(start, 2 * seg)] = first_ref[:, span]
+    for step in range(1, PLACES):
         place = jnp.bitwise_xor(mine, step)
         for target in range(clusters):
             span = slice(target * seg, (target + 1) * seg)
             base = (target * PLACES + place) * 2
             here = pl.multiple_of((base + half) * seg, seg)
             there = pl.multiple_of((base + 1 - half) * seg, seg)
-            out_ref[:, pl.ds(here, seg)] = refs[step][:, span]
-            out_ref[:, pl.ds(there, seg)] = refs[PLACES + step][:, span]
+            out_ref[:, pl.ds(here, seg)] = refs[step - 1][:, span]
+            out_ref[:, pl.ds(there, seg)] = refs[PLACES + step - 2][:, span]
 
 
 def after(value, *first):
@@ -158,9 +182,11 @@
 
     stages = [1 << bit for bit in reversed(range((owners - 1).bit_length()))]
 
+    def swapped(array, stage):
+        return lax.ppermute(array, "clus", [(p, p ^ stage) for p in range(owners)])
+
     def double(array, stage):
-        other = lax.ppermute(array, "clus", [(p, p ^ stage) for p in range(owners)])
-        return jnp.concatenate([array, other], axis=0)
+        return jnp.concatenate([array, swapped(array, stage)], axis=0)
 
     v_far, v_near, v_middle = (
         move(v_factors, far),
@@ -169,18 +195,19 @@
     )
     packed = call(
         functools.partial(pack_body, seg),
-        jax.ShapeDtypeStruct((columns, width // 2), incident.dtype),
+        [jax.ShapeDtypeStruct((columns, width // 4), incident.dtype)] * 2,
         [SMEM, VMEM],
         "pack",
         moved=3 * columns * width,
     )(position, incident)
-    x_other = across(packed)
+    x_other = [across(part) for part in packed]
     slots = block_slot
     for stage in stages:
         slots = double(slots, stage)
     v_far, slots = lax.optimization_barrier((v_far, slots))
     v_ends = move(v_far, ends)
-    u_first = after(u_factors, v_far)
+    u_first = after(u_factors, v_near, v_middle, v_ends)
+    u_side = across(after(u_factors, *x_other))
     u_far = [move(u_first[part], far) for part in (slice(0, early), slice(early, capacity))]
     u_ends = [move(part, ends) for part in u_far]
 
@@ -190,30 +217,29 @@
             jax.ShapeDtypeStruct((blocks, 2, padded, rank_max), jnp.float32),
             jax.ShapeDtypeStruct((blocks, 2, padded, rank_max), jnp.bfloat16),
         ],
-        [SMEM, SMEM] + [VMEM] * 7,
+        [SMEM, SMEM] + [VMEM] * 8,
         "compress",
         flops=4 * blocks * columns * seg * PLACES * rank_max,
         moved=3 * columns * width + 2 * PLACES * v_factors.size,
-    )(position, block_source, incident, x_other, v_factors, v_near, v_far, v_middle, v_ends)
+        scratch=[pltpu.VMEM((columns, width // 2), incident.dtype)],
+    )(position, block_source, incident, *x_other, v_factors, v_near, v_far, v_middle, v_ends)
     received = across(sent)
     u_next = after(u_factors, received)
     u_near, u_middle = move(u_next, near), move(u_next, middle)
 
-    def chain(_, unused):
-        rank_index = lax.broadcasted_iota(jnp.int32, (blocks, 1, 1, rank_max), 3)
-        rows = jnp.where(
-            rank_index < block_rank[:, None, None, None],
-            partial + received.astype(jnp.float32),
-            0.0,
-        ).astype(jnp.bfloat16)
-        for stage in stages:
-            rows = double(rows, stage)
-        return rows
-
-    rounds = 1 + jnp.minimum(me, 0)
-    gathered = lax.fori_loop(
-        0, rounds, chain, jnp.zeros((owners * blocks, 2, padded, rank_max), jnp.bfloat16)
-    )
+    rank_index = lax.broadcasted_iota(jnp.int32, (blocks, 1, 1, rank_max), 3)
+    rows = jnp.where(
+        rank_index < block_rank[:, None, None, None],
+        partial + received.astype(jnp.float32),
+        0.0,
+    ).astype(jnp.bfloat16)
+
+    rounds, gathered = 1 + jnp.minimum(me, 0), rows
+    for stage in stages:
+        other = lax.fori_loop(
+            0, rounds, lambda _, array, stage=stage: swapped(array, stage), gathered
+        )
+        gathered = jnp.concatenate([gathered, other], axis=0)
     wanted = owner * capacity + lax.broadcasted_iota(jnp.int32, (capacity, slots.shape[0]), 0)
     order = lax.broadcasted_iota(jnp.int32, (capacity, slots.shape[0]), 1)
     feeding = jnp.max(jnp.where(wanted == slots[None, :], order, -1), axis=1)
@@ -223,24 +249,30 @@
         [SMEM, SMEM, VMEM],
         "land",
         moved=2 * gathered.size * (1 + clusters),
-    )(feeding, slot_target, after(gathered, u_far[0]))
+    )(feeding, slot_target, gathered)
 
     chunk = jax.ShapeDtypeStruct((columns, clusters * seg), jnp.bfloat16)
     own_parts, other_parts = [None] * PLACES, [None] * PLACES
+    first = call(
+        functools.partial(expand_own_body, seg, columns),
+        jax.ShapeDtypeStruct((columns, 2 * clusters * seg), jnp.bfloat16),
+        [SMEM] + [VMEM] * 3,
+        "expand_own",
+        flops=4 * clusters * capacity * columns * seg * rank_max,
+        moved=4 * u_factors.size + 2 * slot_rows.size + 4 * columns * clusters * seg,
+        scratch=[pltpu.VMEM((clusters, padded, seg), jnp.float32)],
+    )(position, slot_rows, u_factors, u_side)
     arrivals = {
-        0: ([u_factors], [[0]]),
+        1: ([u_near], [[0]]),
         2: (u_far, [[0, 1]]),
-        1: ([u_near], [[0]]),
         3: ([u_middle, *u_ends], [[0], [1, 2]]),
     }
     finished = []
     for step, (shards, choices) in arrivals.items():
         if finished:
             slot_rows = after(slot_rows, own_parts[finished[-1]])
-        if len(finished) > 1:
-            slot_rows = after(slot_rows, other_parts[finished[-2]])
-        if len(finished) == PLACES - 1:
-            slot_rows = after(slot_rows, other_parts[finished[-1]])
+        if len(finished) == 2:
+            slot_rows = after(slot_rows, first, other_parts[finished[0]])
         own, other = call(
             functools.partial(expand_body, seg, columns, choices),
             [chunk, chunk],
@@ -255,10 +287,10 @@
     return call(
         functools.partial(join_body, seg, clusters),
         jax.ShapeDtypeStruct((columns, width), jnp.bfloat16),
-        [SMEM] + [VMEM] * (2 * PLACES),
+        [SMEM] + [VMEM] * (2 * PLACES - 1),
         "join",
         moved=4 * columns * width,
-    )(position, *own_parts, *other_parts)
+    )(position, first, *own_parts[1:], *other_parts[1:])
 
 
 def gathered_plan(

time: 98.6 us -> 91.5 us (0.928)
  the two profiles are of different devices: /device:TPU:0 before, /device:TPU:26 now
where the time goes in v4:
time: 91.5 us; the launch traced here: 91.2 us
  waiting for transfers between devices  53.9 us (59%)
  starting transfers between devices  19 us (21%)
  Pallas kernels  11.1 us (12%)
  other arithmetic  3.76 us (4%)
  local copies, waits for them, and re-layouts  3.22 us (4%)
    ppermute x10, waiting for transfers between devices, move(): lax.ppermute(array, 'rhs', [(2 * a + i, 2 * b + i) for a, b in pairs for...  28.6 us
    ppermute x7, waiting for transfers between devices, across(): return lax.ppermute(array, 'rhs', [(p, p ^ 1) for p in range(2 * PLACES)])  14.8 us
    ppermute x4, waiting for transfers between devices, swapped(): return lax.ppermute(array, 'clus', [(p, p ^ stage) for p in range(owners)])  10.4 us
    ppermute x10, starting transfers between devices, move(): lax.ppermute(array, 'rhs', [(2 * a + i, 2 * b + i) for a, b in pairs for...  9.05 us
    ppermute x7, starting transfers between devices, across(): return lax.ppermute(array, 'rhs', [(p, p ^ 1) for p in range(2 * PLACES)])  6.87 us
    pallas_call x3, Pallas kernels, paired(): call(functools.partial(expand_body, seg, columns, choices), [chunk, chunk...  4.17 us
    ppermute x4, starting transfers between devices, swapped(): return lax.ppermute(array, 'clus', [(p, p ^ stage) for p in range(owners)])  3.11 us
    concatenate x2, other arithmetic, paired(): gathered = jnp.concatenate([gathered, other], axis=0)  2.23 us
  transfers between devices with their start and end apart: 21, of which 15 were waited for; matrix products, arithmetic and copies ran while one was open for 6% of the time, Pallas kernels for 8%

profile of v4, /device:TPU:26, one launch (start us, length us, event | category | flops | bytes accessed | tf_op | source)
XLA Modules:
  0.0 91.2 jit_solution(7360901310403005332)
XLA Ops:
  0.9 1.5 %copy-done = bf16[104,8192]{1,0:T(8,128)(2,1)S(1)} copy-done((bf16[104,8192]{1,0:T(8,128)(2,1)S(1)}, bf16[104,8192]{1,0:T(8,128)(2,1)}, u32[]{:S(2)}) %copy-start) | copy-done | bytes 1703960
  3.3 1.8 %collective-permute-start.6 = (bf16[104,2048]{1,0:T(8,128)(2,1)S(1)}, bf16[104,2048]{1,0:T(8,128)(2,1)S(1)}, u32[]{:S(2)}, u32[]{:S(2)}) collective-permute-start(bf16[104,2048]{1,0:T(8,128)(2,1)S(1)} %get-tuple-element.61), channel_id=1, source_target_pairs={{0,4},{4,0},{8,12},{12,8},{16,20},{20,16},{24,28},{28,24},{1,5},{5... | collective-permute-start | bytes 1277960 | tf_op jit(solution)/shard_map/ppermute | solution.py:175
  5.1 1.5 %collective-permute-start.3 = (s32[5]{0:T(128)S(1)}, s32[5]{0:T(128)S(1)}, u32[]{:S(2)}, u32[]{:S(2)}) collective-permute-start(s32[5]{0:T(128)S(1)} %copy-done.7), channel_id=1, source_target_pairs={{0,2},{1,3},{2,0},{3,1},{4,6},{5,7},{6,4},{7,5},{8,10},{9,11},{10,... | collective-permute-start | bytes 68 | tf_op jit(solution)/shard_map/ppermute | solution.py:186
  6.6 2.0 %collective-permute-done.3 = s32[5]{0:T(128)S(1)} collective-permute-done((s32[5]{0:T(128)S(1)}, s32[5]{0:T(128)S(1)}, u32[]{:S(2)}, u32[]{:S(2)}) %collective-permute-start.3) | collective-permute-done | bytes 52 | tf_op jit(solution)/shard_map/ppermute | solution.py:186
  8.7 1.1 %collective-permute-done.4 = s32[10]{0:T(128)S(1)} collective-permute-done((s32[10]{0:T(128)S(1)}, s32[10]{0:T(128)S(1)}, u32[]{:S(2)}, u32[]{:S(2)}) %collective-permute-start.4) | collective-permute-done | bytes 72 | tf_op jit(solution)/shard_map/ppermute | solution.py:186
  10.7 6.8 %collective-permute-done.2.refs_2_ = bf16[5,256,128]{2,1,0:T(8,128)(2,1)S(1)} collective-permute-done((bf16[5,256,128]{2,1,0:T(8,128)(2,1)}, bf16[5,256,128]{2,1,0:T(8,128)(2,1)S(1)}, u32[]{:S(2)}, u32[]{:S(2)}) %collective-permute-start.2) | collective-permute-done | bytes 327712 | tf_op jit(solution)/shard_map/ppermute | solution.py:172
  17.6 1.3 %collective-permute-start.9 = (bf16[5,256,128]{2,1,0:T(8,128)(2,1)S(1)}, bf16[5,256,128]{2,1,0:T(8,128)(2,1)S(1)}, u32[]{:S(2)}, u32[]{:S(2)}) collective-permute-start(bf16[5,256,128]{2,1,0:T(8,128)(2,1)S(1)} %collective-permute-done.2.refs_2_), channel_id=1, source_target_pairs={{8,0},{12,4},{16,24},{20,28},{9,1},{13,5},{17,25},{21,29},{10,2},{... | collective-permute-start | bytes 983048 | tf_op jit(solution)/shard_map/ppermute | solution.py:172
  18.9 4.3 %collective-permute-done.6.xh_ref = bf16[104,2048]{1,0:T(8,128)(2,1)S(1)} collective-permute-done((bf16[104,2048]{1,0:T(8,128)(2,1)S(1)}, bf16[104,2048]{1,0:T(8,128)(2,1)S(1)}, u32[]{:S(2)}, u32[]{:S(2)}) %collective-permute-start.6) | collective-permute-done | bytes 426016 | tf_op jit(solution)/shard_map/ppermute | solution.py:175
  23.2 5.8 %collective-permute-done.9.refs_4_ = bf16[5,256,128]{2,1,0:T(8,128)(2,1)S(1)} collective-permute-done((bf16[5,256,128]{2,1,0:T(8,128)(2,1)S(1)}, bf16[5,256,128]{2,1,0:T(8,128)(2,1)S(1)}, u32[]{:S(2)}, u32[]{:S(2)}) %collective-permute-start.9) | collective-permute-done | bytes 327712 | tf_op jit(solution)/shard_map/ppermute | solution.py:172
  29.0 2.1 %compress.1 = (f32[5,2,112,128]{3,2,1,0:T(8,128)S(1)}, bf16[5,2,112,128]{3,2,1,0:T(8,128)(2,1)}) custom-call(s32[2]{0:T(128)S(1)} %pad_add_fusion.pos_ref, s32[5]{0:T(128)S(1)} %copy-done.3, bf16[104,8192]{1,0:T(8,128)(2,1)S(1)} %copy-done, bf16[104,2048]{1,0:T(8,128)(2,1)S(1)} %collective-permute-done.5.xl_ref, ...), custom_call_target="tpu_custom_call" | custom-call | flops 272629760 | bytes 3866624 | tf_op jit(solution)/shard_map/compress/pallas_call | solution.py:214
  31.8 1.5 %collective-permute-start.11 = (bf16[10,256,128]{2,1,0:T(8,128)(2,1)S(1)}, bf16[10,256,128]{2,1,0:T(8,128)(2,1)S(1)}, u32[]{:S(2)}, u32[]{:S(2)}) collective-permute-start(bf16[10,256,128]{2,1,0:T(8,128)(2,1)S(1)} %copy-done.1), channel_id=1, source_target_pairs={{0,4},{4,0},{8,12},{12,8},{16,20},{20,16},{24,28},{28,24},{1,5},{5... | collective-permute-start | bytes 1966088 | tf_op jit(solution)/shard_map/ppermute | solution.py:175
  34.1 2.9 %collective-permute-start.14 = (bf16[5,256,128]{2,1,0:T(8,128)(2,1)}, bf16[5,256,128]{2,1,0:T(8,128)(2,1)S(1)}, u32[]{:S(2)}, u32[]{:S(2)}) collective-permute-start(bf16[5,256,128]{2,1,0:T(8,128)(2,1)} %get-tuple-element.91), channel_id=1, source_target_pairs={{0,16},{4,20},{8,24},{12,28},{16,0},{20,4},{24,8},{28,12},{1,17},{... | collective-permute-start | bytes 983048 | tf_op jit(solution)/shard_map/ppermute | solution.py:172
  37.1 4.2 %collective-permute-done.10 = bf16[5,2,112,128]{3,2,1,0:T(8,128)(2,1)} collective-permute-done((bf16[5,2,112,128]{3,2,1,0:T(8,128)(2,1)}, bf16[5,2,112,128]{3,2,1,0:T(8,128)(2,1)}, u32[]{:S(2)}, u32[]{:S(2)}) %collective-permute-start.10) | collective-permute-done | bytes 286752 | tf_op jit(solution)/shard_map/ppermute | solution.py:175
  42.3 6.7 %while.20 = (s32[]{:T(128)}, bf16[5,2,112,128]{3,2,1,0:T(8,128)(2,1)S(1)}, s32[]{:T(128)}, s32[]{:T(128)}) while((s32[]{:T(128)}, bf16[5,2,112,128]{3,2,1,0:T(8,128)(2,1)S(1)}, s32[]{:T(128)}, s32[]{:T(128)}) %tuple.46), condition=%wide.region_2.3_spmd, body=%wide.region_1.2_spmd.sunk | while | flops 2 | bytes 1720413 | solution.py:239
  42.3 1.6 %collective-permute-start = (bf16[5,2,112,128]{3,2,1,0:T(8,128)(2,1)S(1)}, bf16[5,2,112,128]{3,2,1,0:T(8,128)(2,1)S(1)}, u32[]{:S(2)}, u32[]{:S(2)}) collective-permute-start(bf16[5,2,112,128]{3,2,1,0:T(8,128)(2,1)S(1)} %get-tuple-element.138), channel_id=1, source_target_pairs={{0,2},{1,3},{2,0},{3,1},{4,6},{5,7},{6,4},{7,5},{8,10},{9,11},{10,... | collective-permute-start | bytes 860168 | tf_op jit(solution)/shard_map/while/body/ppermute | solution.py:186
  43.9 5.1 %collective-permute-done = bf16[5,2,112,128]{3,2,1,0:T(8,128)(2,1)S(1)} collective-permute-done((bf16[5,2,112,128]{3,2,1,0:T(8,128)(2,1)S(1)}, bf16[5,2,112,128]{3,2,1,0:T(8,128)(2,1)S(1)}, u32[]{:S(2)}, u32[]{:S(2)}) %collective-permute-start) | collective-permute-done | bytes 286752 | tf_op jit(solution)/shard_map/while/body/ppermute | solution.py:186
  50.0 3.0 %while.21 = (s32[]{:T(128)}, bf16[10,2,112,128]{3,2,1,0:T(8,128)(2,1)}, s32[]{:T(128)}, s32[]{:T(128)}) while((s32[]{:T(128)}, bf16[10,2,112,128]{3,2,1,0:T(8,128)(2,1)}, s32[]{:T(128)}, s32[]{:T(128)}) %tuple.49), condition=%wide.region_4.5_spmd, body=%wide.region_3.4_spmd.sunk | while | flops 2 | bytes 3440733 | solution.py:239
  50.0 2.2 %collective-permute-done.1 = bf16[10,2,112,128]{3,2,1,0:T(8,128)(2,1)S(1)} collective-permute-done((bf16[10,2,112,128]{3,2,1,0:T(8,128)(2,1)}, bf16[10,2,112,128]{3,2,1,0:T(8,128)(2,1)S(1)}, u32[]{:S(2)}, u32[]{:S(2)}) %collective-permute-start.1) | collective-permute-done | bytes 573472 | tf_op jit(solution)/shard_map/while/body/ppermute | solution.py:186
  53.9 2.7 %collective-permute-done.13.refs_0_ = bf16[5,256,128]{2,1,0:T(8,128)(2,1)S(1)} collective-permute-done((bf16[5,256,128]{2,1,0:T(8,128)(2,1)}, bf16[5,256,128]{2,1,0:T(8,128)(2,1)S(1)}, u32[]{:S(2)}, u32[]{:S(2)}) %collective-permute-start.13) | collective-permute-done | bytes 327712 | tf_op jit(solution)/shard_map/ppermute | solution.py:172
  56.6 1.3 %collective-permute-start.17 = (bf16[5,256,128]{2,1,0:T(8,128)(2,1)S(1)}, bf16[5,256,128]{2,1,0:T(8,128)(2,1)S(1)}, u32[]{:S(2)}, u32[]{:S(2)}) collective-permute-start(bf16[5,256,128]{2,1,0:T(8,128)(2,1)S(1)} %collective-permute-done.13.refs_0_), channel_id=1, source_target_pairs={{8,0},{12,4},{16,24},{20,28},{9,1},{13,5},{17,25},{21,29},{10,2},{... | collective-permute-start | bytes 983048 | tf_op jit(solution)/shard_map/ppermute | solution.py:172
  57.9 5.7 %collective-permute-done.14.refs_1_ = bf16[5,256,128]{2,1,0:T(8,128)(2,1)S(1)} collective-permute-done((bf16[5,256,128]{2,1,0:T(8,128)(2,1)}, bf16[5,256,128]{2,1,0:T(8,128)(2,1)S(1)}, u32[]{:S(2)}, u32[]{:S(2)}) %collective-permute-start.14) | collective-permute-done | bytes 327712 | tf_op jit(solution)/shard_map/ppermute | solution.py:172
  63.5 1.3 %collective-permute-start.18 = (bf16[5,256,128]{2,1,0:T(8,128)(2,1)S(1)}, bf16[5,256,128]{2,1,0:T(8,128)(2,1)S(1)}, u32[]{:S(2)}, u32[]{:S(2)}) collective-permute-start(bf16[5,256,128]{2,1,0:T(8,128)(2,1)S(1)} %collective-permute-done.14.refs_1_), channel_id=1, source_target_pairs={{8,0},{12,4},{16,24},{20,28},{9,1},{13,5},{17,25},{21,29},{10,2},{... | collective-permute-start | bytes 983048 | tf_op jit(solution)/shard_map/ppermute | solution.py:172
  64.8 1.3 %pad_maximum_fusion.comp_ref = bf16[20,2,112,128]{3,2,1,0:T(8,128)(2,1)S(1)} fusion(bf16[10,2,112,128]{3,2,1,0:T(8,128)(2,1)} %get-tuple-element.66, bf16[5,2,112,128]{3,2,1,0:T(8,128)(2,1)} %copy-done.6, bf16[5,2,112,128]{3,2,1,0:T(8,128)(2,1)} %copy-done.5), kind=kLoop, calls=%fused_computation | loop fusion | flops 1146880 | bytes 2293760 | tf_op jit(solution)/shard_map/concatenate | solution.py:242
  67.1 5.3 %collective-permute-done.12.refs_0_ = bf16[10,256,128]{2,1,0:T(8,128)(2,1)S(1)} collective-permute-done((bf16[10,256,128]{2,1,0:T(8,128)(2,1)S(1)}, bf16[10,256,128]{2,1,0:T(8,128)(2,1)S(1)}, u32[]{:S(2)}, u32[]{:S(2)}) %collective-permute-start.12) | collective-permute-done | bytes 655392 | tf_op jit(solution)/shard_map/ppermute | solution.py:172
  72.4 1.4 %expand.3 = (bf16[104,1024]{1,0:T(8,128)(2,1)S(1)}, bf16[104,1024]{1,0:T(8,128)(2,1)S(1)}) custom-call(s32[2]{0:T(128)S(1)} %pad_add_fusion.pos_ref, bf16[4,2,112,1280]{3,2,1,0:T(8,128)(2,1)S(1)} %land.1.rows_ref, bf16[10,256,128]{2,1,0:T(8,128)(2,1)S(1)} %collective-permute-done.12.refs_0_), custom_call_target="tpu_custom_call" | custom-call | flops 545259520 | bytes 3375104 | tf_op jit(solution)/shard_map/expand/pallas_call | solution.py:276
  74.3 1.3 %expand_own.1.first_ref = bf16[104,2048]{1,0:T(8,128)(2,1)S(1)} custom-call(s32[2]{0:T(128)S(1)} %pad_add_fusion.pos_ref, bf16[4,2,112,1280]{3,2,1,0:T(8,128)(2,1)S(1)} %land.1.rows_ref, bf16[10,256,128]{2,1,0:T(8,128)(2,1)S(1)} %copy-done.1, bf16[10,256,128]{2,1,0:T(8,128)(2,1)S(1)} %collective-permute-done.11.side_ref), custom_call_target="tpu_custom_call" | custom-call | flops 545259520 | bytes 4030464 | tf_op jit(solution)/shard_map/expand_own/pallas_call | solution.py:256
  75.7 1.4 %expand.4 = (bf16[104,1024]{1,0:T(8,128)(2,1)S(1)}, bf16[104,1024]{1,0:T(8,128)(2,1)S(1)}) custom-call(s32[2]{0:T(128)S(1)} %pad_add_fusion.pos_ref, bf16[4,2,112,1280]{3,2,1,0:T(8,128)(2,1)S(1)} %land.1.rows_ref, bf16[5,256,128]{2,1,0:T(8,128)(2,1)S(1)} %collective-permute-done.13.refs_0_, bf16[5,256,128]{2,1,0:T(8,128)(2,1)S(1)} %collective-permute-done.14.refs_1_), custom_call_target="tpu_custom_call" | custom-call | flops 545259520 | bytes 3375104 | tf_op jit(solution)/shard_map/expand/pallas_call | solution.py:276
  77.1 1.6 %collective-permute-start.19 = (bf16[104,1024]{1,0:T(8,128)(2,1)S(1)}, bf16[104,1024]{1,0:T(8,128)(2,1)S(1)}, u32[]{:S(2)}, u32[]{:S(2)}) collective-permute-start(bf16[104,1024]{1,0:T(8,128)(2,1)S(1)} %get-tuple-element.77), channel_id=1, source_target_pairs={{0,4},{4,0},{8,12},{12,8},{16,20},{20,16},{24,28},{28,24},{1,5},{5... | collective-permute-start | bytes 638984 | tf_op jit(solution)/shard_map/ppermute | solution.py:175
  79.7 2.3 %collective-permute-done.18.refs_2_ = bf16[5,256,128]{2,1,0:T(8,128)(2,1)S(1)} collective-permute-done((bf16[5,256,128]{2,1,0:T(8,128)(2,1)S(1)}, bf16[5,256,128]{2,1,0:T(8,128)(2,1)S(1)}, u32[]{:S(2)}, u32[]{:S(2)}) %collective-permute-start.18) | collective-permute-done | bytes 327712 | tf_op jit(solution)/shard_map/ppermute | solution.py:172
  82.0 1.4 %expand.5 = (bf16[104,1024]{1,0:T(8,128)(2,1)S(1)}, bf16[104,1024]{1,0:T(8,128)(2,1)S(1)}) custom-call(s32[2]{0:T(128)S(1)} %pad_add_fusion.pos_ref, bf16[4,2,112,1280]{3,2,1,0:T(8,128)(2,1)S(1)} %land.1.rows_ref, bf16[10,256,128]{2,1,0:T(8,128)(2,1)S(1)} %collective-permute-done.16.refs_0_, bf16[5,256,128]{2,1,0:T(8,128)(2,1)S(1)} %collective-permute-done.17.refs_1_, ...), custom_call_target="tpu_custom_call" | custom-call | flops 545259520 | bytes 3375104 | tf_op jit(solution)/shard_map/expand/pallas_call | solution.py:276
  84.3 5.1 %collective-permute-done.20.refs_5_ = bf16[104,1024]{1,0:T(8,128)(2,1)S(1)} collective-permute-done((bf16[104,1024]{1,0:T(8,128)(2,1)S(1)}, bf16[104,1024]{1,0:T(8,128)(2,1)S(1)}, u32[]{:S(2)}, u32[]{:S(2)}) %collective-permute-start.20) | collective-permute-done | bytes 213024 | tf_op jit(solution)/shard_map/ppermute | solution.py:175
  89.3 1.9 %join.1 = bf16[104,8192]{1,0:T(8,128)(2,1)} custom-call(s32[2]{0:T(128)S(1)} %pad_add_fusion.pos_ref, bf16[104,2048]{1,0:T(8,128)(2,1)S(1)} %expand_own.1.first_ref, bf16[104,1024]{1,0:T(8,128)(2,1)S(1)} %get-tuple-element.69.refs_0_, bf16[104,1024]{1,0:T(8,128)(2,1)S(1)} %get-tuple-element.72.refs_1_, bf16[104,1024]{1,0:T(8,128)(2,1)S(1)} %get-tuple-element.76.refs_2_, ...), custom_call_target="tpu_custom_call" | custom-call | bytes 3407872 | tf_op jit(solution)/shard_map/join/pallas_call | solution.py:287
  (51 shorter events, 11.3 us)
Async XLA Ops:
  0.0 5.1 %copy-start.7 = (s32[5]{0:T(128)S(1)}, s32[5]{0:T(128)}, u32[]{:S(2)}) copy-start(s32[5]{0:T(128)} %param.16) | copy-start | bytes 64
  0.0 29.0 %copy-start.3 = (s32[5]{0:T(128)S(1)}, s32[5]{0:T(128)}, u32[]{:S(2)}) copy-start(s32[5]{0:T(128)} %source_ref.1) | copy-start | bytes 64
  0.0 17.6 %collective-permute-start.2 = (bf16[5,256,128]{2,1,0:T(8,128)(2,1)}, bf16[5,256,128]{2,1,0:T(8,128)(2,1)S(1)}, u32[]{:S(2)}, u32[]{:S(2)}) collective-permute-start(bf16[5,256,128]{2,1,0:T(8,128)(2,1)} %refs_0_.1), channel_id=1, source_target_pairs={{0,16},{4,20},{8,24},{12,28},{16,0},{20,4},{24,8},{28,12},{1,17},{... | collective-permute-start | bytes 983048 | tf_op jit(solution)/shard_map/ppermute | solution.py:172
  0.3 18.5 %collective-permute-start.7 = (bf16[5,256,128]{2,1,0:T(8,128)(2,1)}, bf16[5,256,128]{2,1,0:T(8,128)(2,1)S(1)}, u32[]{:S(2)}, u32[]{:S(2)}) collective-permute-start(bf16[5,256,128]{2,1,0:T(8,128)(2,1)} %refs_0_.1), channel_id=1, source_target_pairs={{0,8},{4,12},{8,0},{12,4},{16,24},{20,28},{24,16},{28,20},{1,9},{5... | collective-permute-start | bytes 983048 | tf_op jit(solution)/shard_map/ppermute | solution.py:172
  0.9 1.5 %copy-start = (bf16[104,8192]{1,0:T(8,128)(2,1)S(1)}, bf16[104,8192]{1,0:T(8,128)(2,1)}, u32[]{:S(2)}) copy-start(bf16[104,8192]{1,0:T(8,128)(2,1)} %x_ref.3) | copy-start | bytes 5111812
  2.3 7.6 %copy-start.2 = (bf16[5,256,128]{2,1,0:T(8,128)(2,1)S(1)}, bf16[5,256,128]{2,1,0:T(8,128)(2,1)}, u32[]{:S(2)}) copy-start(bf16[5,256,128]{2,1,0:T(8,128)(2,1)} %refs_0_.1) | copy-start | bytes 983044
  3.0 15.9 %collective-permute-start.5 = (bf16[104,2048]{1,0:T(8,128)(2,1)S(1)}, bf16[104,2048]{1,0:T(8,128)(2,1)S(1)}, u32[]{:S(2)}, u32[]{:S(2)}) collective-permute-start(bf16[104,2048]{1,0:T(8,128)(2,1)S(1)} %get-tuple-element.60), channel_id=1, source_target_pairs={{0,4},{4,0},{8,12},{12,8},{16,20},{20,16},{24,28},{28,24},{1,5},{5... | collective-permute-start | bytes 1277960 | tf_op jit(solution)/shard_map/ppermute | solution.py:175
  3.3 19.9 %collective-permute-start.6 = (bf16[104,2048]{1,0:T(8,128)(2,1)S(1)}, bf16[104,2048]{1,0:T(8,128)(2,1)S(1)}, u32[]{:S(2)}, u32[]{:S(2)}) collective-permute-start(bf16[104,2048]{1,0:T(8,128)(2,1)S(1)} %get-tuple-element.61), channel_id=1, source_target_pairs={{0,4},{4,0},{8,12},{12,8},{16,20},{20,16},{24,28},{28,24},{1,5},{5... | collective-permute-start | bytes 1277960 | tf_op jit(solution)/shard_map/ppermute | solution.py:175
  5.1 3.5 %collective-permute-start.3 = (s32[5]{0:T(128)S(1)}, s32[5]{0:T(128)S(1)}, u32[]{:S(2)}, u32[]{:S(2)}) collective-permute-start(s32[5]{0:T(128)S(1)} %copy-done.7), channel_id=1, source_target_pairs={{0,2},{1,3},{2,0},{3,1},{4,6},{5,7},{6,4},{7,5},{8,10},{9,11},{10,... | collective-permute-start | bytes 68 | tf_op jit(solution)/shard_map/ppermute | solution.py:186
  8.7 1.1 %collective-permute-start.4 = (s32[10]{0:T(128)S(1)}, s32[10]{0:T(128)S(1)}, u32[]{:S(2)}, u32[]{:S(2)}) collective-permute-start(s32[10]{0:T(128)S(1)} %pad_add_fusion.1), channel_id=1, source_target_pairs={{0,1},{1,0},{2,3},{3,2},{4,5},{5,4},{6,7},{7,6},{8,9},{9,8},{10,11... | collective-permute-start | bytes 128 | tf_op jit(solution)/shard_map/ppermute | solution.py:186
  9.9 21.8 %copy-start.8 = (s32[5]{0:T(128)S(1)}, s32[5]{0:T(128)}, u32[]{:S(2)}) copy-start(s32[5]{0:T(128)} %param.15) | copy-start | bytes 64
  9.9 21.9 %copy-start.1 = (bf16[10,256,128]{2,1,0:T(8,128)(2,1)S(1)}, bf16[10,256,128]{2,1,0:T(8,128)(2,1)}, u32[]{:S(2)}) copy-start(bf16[10,256,128]{2,1,0:T(8,128)(2,1)} %u_ref.1) | copy-start | bytes 1966084
  9.9 9.0 %collective-permute-start.8 = (bf16[5,256,128]{2,1,0:T(8,128)(2,1)S(1)}, bf16[5,256,128]{2,1,0:T(8,128)(2,1)S(1)}, u32[]{:S(2)}, u32[]{:S(2)}) collective-permute-start(bf16[5,256,128]{2,1,0:T(8,128)(2,1)S(1)} %copy-done.2), channel_id=1, source_target_pairs={{8,16},{12,20},{16,8},{20,12},{9,17},{13,21},{17,9},{21,13},{10,18... | collective-permute-start | bytes 983048 | tf_op jit(solution)/shard_map/ppermute | solution.py:172
  17.6 11.4 %collective-permute-start.9 = (bf16[5,256,128]{2,1,0:T(8,128)(2,1)S(1)}, bf16[5,256,128]{2,1,0:T(8,128)(2,1)S(1)}, u32[]{:S(2)}, u32[]{:S(2)}) collective-permute-start(bf16[5,256,128]{2,1,0:T(8,128)(2,1)S(1)} %collective-permute-done.2.refs_2_), channel_id=1, source_target_pairs={{8,0},{12,4},{16,24},{20,28},{9,1},{13,5},{17,25},{21,29},{10,2},{... | collective-permute-start | bytes 983048 | tf_op jit(solution)/shard_map/ppermute | solution.py:172
  31.1 10.1 %collective-permute-start.10 = (bf16[5,2,112,128]{3,2,1,0:T(8,128)(2,1)}, bf16[5,2,112,128]{3,2,1,0:T(8,128)(2,1)}, u32[]{:S(2)}, u32[]{:S(2)}) collective-permute-start(bf16[5,2,112,128]{3,2,1,0:T(8,128)(2,1)} %get-tuple-element.64), channel_id=1, source_target_pairs={{0,4},{4,0},{8,12},{12,8},{16,20},{20,16},{24,28},{28,24},{1,5},{5... | collective-permute-start | bytes 860168 | tf_op jit(solution)/shard_map/ppermute | solution.py:175
  31.8 42.6 %collective-permute-start.11 = (bf16[10,256,128]{2,1,0:T(8,128)(2,1)S(1)}, bf16[10,256,128]{2,1,0:T(8,128)(2,1)S(1)}, u32[]{:S(2)}, u32[]{:S(2)}) collective-permute-start(bf16[10,256,128]{2,1,0:T(8,128)(2,1)S(1)} %copy-done.1), channel_id=1, source_target_pairs={{0,4},{4,0},{8,12},{12,8},{16,20},{20,16},{24,28},{28,24},{1,5},{5... | collective-permute-start | bytes 1966088 | tf_op jit(solution)/shard_map/ppermute | solution.py:175
  34.1 22.4 %collective-permute-start.13 = (bf16[5,256,128]{2,1,0:T(8,128)(2,1)}, bf16[5,256,128]{2,1,0:T(8,128)(2,1)S(1)}, u32[]{:S(2)}, u32[]{:S(2)}) collective-permute-start(bf16[5,256,128]{2,1,0:T(8,128)(2,1)} %get-tuple-element.92), channel_id=1, source_target_pairs={{0,16},{4,20},{8,24},{12,28},{16,0},{20,4},{24,8},{28,12},{1,17},{... | collective-permute-start | bytes 983048 | tf_op jit(solution)/shard_map/ppermute | solution.py:172
  34.1 29.4 %collective-permute-start.14 = (bf16[5,256,128]{2,1,0:T(8,128)(2,1)}, bf16[5,256,128]{2,1,0:T(8,128)(2,1)S(1)}, u32[]{:S(2)}, u32[]{:S(2)}) collective-permute-start(bf16[5,256,128]{2,1,0:T(8,128)(2,1)} %get-tuple-element.91), channel_id=1, source_target_pairs={{0,16},{4,20},{8,24},{12,28},{16,0},{20,4},{24,8},{28,12},{1,17},{... | collective-permute-start | bytes 983048 | tf_op jit(solution)/shard_map/ppermute | solution.py:172
  41.2 31.2 %collective-permute-start.12 = (bf16[10,256,128]{2,1,0:T(8,128)(2,1)S(1)}, bf16[10,256,128]{2,1,0:T(8,128)(2,1)S(1)}, u32[]{:S(2)}, u32[]{:S(2)}) collective-permute-start(bf16[10,256,128]{2,1,0:T(8,128)(2,1)S(1)} %copy-done.1), channel_id=1, source_target_pairs={{0,8},{4,12},{8,0},{12,4},{16,24},{20,28},{24,16},{28,20},{1,9},{5... | collective-permute-start | bytes 1966088 | tf_op jit(solution)/shard_map/ppermute | solution.py:172
  42.3 7.7 %copy-start.5 = (bf16[5,2,112,128]{3,2,1,0:T(8,128)(2,1)}, bf16[5,2,112,128]{3,2,1,0:T(8,128)(2,1)S(1)}, u32[]{:S(2)}) copy-start(bf16[5,2,112,128]{3,2,1,0:T(8,128)(2,1)S(1)} %select_convert_fusion) | copy-start | bytes 860164
  42.3 6.7 %collective-permute-start = (bf16[5,2,112,128]{3,2,1,0:T(8,128)(2,1)S(1)}, bf16[5,2,112,128]{3,2,1,0:T(8,128)(2,1)S(1)}, u32[]{:S(2)}, u32[]{:S(2)}) collective-permute-start(bf16[5,2,112,128]{3,2,1,0:T(8,128)(2,1)S(1)} %get-tuple-element.138), channel_id=1, source_target_pairs={{0,2},{1,3},{2,0},{3,1},{4,6},{5,7},{6,4},{7,5},{8,10},{9,11},{10,... | collective-permute-start | bytes 860168 | tf_op jit(solution)/shard_map/while/body/ppermute | solution.py:186
  49.1 0.9 copy-start.6
  50.0 2.2 %collective-permute-start.1 = (bf16[10,2,112,128]{3,2,1,0:T(8,128)(2,1)}, bf16[10,2,112,128]{3,2,1,0:T(8,128)(2,1)S(1)}, u32[]{:S(2)}, u32[]{:S(2)}) collective-permute-start(bf16[10,2,112,128]{3,2,1,0:T(8,128)(2,1)} %get-tuple-element.150), channel_id=1, source_target_pairs={{0,1},{1,0},{2,3},{3,2},{4,5},{5,4},{6,7},{7,6},{8,9},{9,8},{10,11... | collective-permute-start | bytes 1720328 | tf_op jit(solution)/shard_map/while/body/ppermute | solution.py:186
  53.0 29.1 %collective-permute-start.16 = (bf16[10,256,128]{2,1,0:T(8,128)(2,1)S(1)}, bf16[10,256,128]{2,1,0:T(8,128)(2,1)S(1)}, u32[]{:S(2)}, u32[]{:S(2)}) collective-permute-start(bf16[10,256,128]{2,1,0:T(8,128)(2,1)S(1)} %copy-done.1), channel_id=1, source_target_pairs={{8,16},{12,20},{16,8},{20,12},{9,17},{13,21},{17,9},{21,13},{10,18... | collective-permute-start | bytes 1966088 | tf_op jit(solution)/shard_map/ppermute | solution.py:172
  56.6 23.1 %collective-permute-start.17 = (bf16[5,256,128]{2,1,0:T(8,128)(2,1)S(1)}, bf16[5,256,128]{2,1,0:T(8,128)(2,1)S(1)}, u32[]{:S(2)}, u32[]{:S(2)}) collective-permute-start(bf16[5,256,128]{2,1,0:T(8,128)(2,1)S(1)} %collective-permute-done.13.refs_0_), channel_id=1, source_target_pairs={{8,0},{12,4},{16,24},{20,28},{9,1},{13,5},{17,25},{21,29},{10,2},{... | collective-permute-start | bytes 983048 | tf_op jit(solution)/shard_map/ppermute | solution.py:172
  63.5 18.5 %collective-permute-start.18 = (bf16[5,256,128]{2,1,0:T(8,128)(2,1)S(1)}, bf16[5,256,128]{2,1,0:T(8,128)(2,1)S(1)}, u32[]{:S(2)}, u32[]{:S(2)}) collective-permute-start(bf16[5,256,128]{2,1,0:T(8,128)(2,1)S(1)} %collective-permute-done.14.refs_1_), channel_id=1, source_target_pairs={{8,0},{12,4},{16,24},{20,28},{9,1},{13,5},{17,25},{21,29},{10,2},{... | collective-permute-start | bytes 983048 | tf_op jit(solution)/shard_map/ppermute | solution.py:172
  64.8 1.4 %copy-start.4 = (s32[10]{0:T(128)S(1)}, s32[10]{0:T(128)}, u32[]{:S(2)}) copy-start(s32[10]{0:T(128)} %target_ref.1) | copy-start | bytes 124
  73.8 5.9 %collective-permute-start.15 = (bf16[104,1024]{1,0:T(8,128)(2,1)S(1)}, bf16[104,1024]{1,0:T(8,128)(2,1)S(1)}, u32[]{:S(2)}, u32[]{:S(2)}) collective-permute-start(bf16[104,1024]{1,0:T(8,128)(2,1)S(1)} %get-tuple-element.74), channel_id=1, source_target_pairs={{0,4},{4,0},{8,12},{12,8},{16,20},{20,16},{24,28},{28,24},{1,5},{5... | collective-permute-start | bytes 638984 | tf_op jit(solution)/shard_map/ppermute | solution.py:175
  77.1 7.2 %collective-permute-start.19 = (bf16[104,1024]{1,0:T(8,128)(2,1)S(1)}, bf16[104,1024]{1,0:T(8,128)(2,1)S(1)}, u32[]{:S(2)}, u32[]{:S(2)}) collective-permute-start(bf16[104,1024]{1,0:T(8,128)(2,1)S(1)} %get-tuple-element.77), channel_id=1, source_target_pairs={{0,4},{4,0},{8,12},{12,8},{16,20},{20,16},{24,28},{28,24},{1,5},{5... | collective-permute-start | bytes 638984 | tf_op jit(solution)/shard_map/ppermute | solution.py:175
  83.4 5.9 %collective-permute-start.20 = (bf16[104,1024]{1,0:T(8,128)(2,1)S(1)}, bf16[104,1024]{1,0:T(8,128)(2,1)S(1)}, u32[]{:S(2)}, u32[]{:S(2)}) collective-permute-start(bf16[104,1024]{1,0:T(8,128)(2,1)S(1)} %get-tuple-element.78), channel_id=1, source_target_pairs={{0,4},{4,0},{8,12},{12,8},{16,20},{20,16},{24,28},{28,24},{1,5},{5... | collective-permute-start | bytes 638984 | tf_op jit(solution)/shard_map/ppermute | solution.py:175

commit v5 on v4

--- a/solution.py
+++ b/solution.py
@@ -9,7 +9,7 @@
 
 VMEM = pl.BlockSpec(memory_space=pltpu.VMEM)
 SMEM = pl.BlockSpec(memory_space=pltpu.SMEM)
-LIMIT = 32 * 1024 * 1024
+LIMIT = 10 * 1024 * 1024
 
 
 def call(body, out_shape, in_specs, name, flops=0, moved=0, scratch=()):
@@ -27,12 +27,12 @@
 
 
 def pack_body(seg, pos_ref, x_ref, *out_refs):
-    half = 1 - pos_ref[0]
-    pieces = out_refs[0].shape[1] // seg
-    for piece in range(pieces * len(out_refs)):
-        start = pl.multiple_of((2 * piece + half) * seg, seg)
-        place = piece % pieces * seg
-        out_refs[piece // pieces][:, place : place + seg] = x_ref[:, pl.ds(start, seg)]
+    half, piece = 1 - pos_ref[0], 0
+    for out_ref in out_refs:
+        for place in range(0, out_ref.shape[1], seg):
+            start = pl.multiple_of((2 * piece + half) * seg, seg)
+            out_ref[:, place : place + seg] = x_ref[:, pl.ds(start, seg)]
+            piece += 1
 
 
 def compress_body(seg, pos_ref, source_ref, x_ref, xl_ref, xh_ref, *refs):
@@ -177,7 +177,6 @@
     far = [(p, p ^ 2) for p in range(PLACES)]
     near = [(p, p ^ 1) for p in range(PLACES)]
     middle = [(1, 2), (2, 1)]
-    early = capacity // 2
     ends = [(1, 0), (2, 3)]
 
     stages = [1 << bit for bit in reversed(range((owners - 1).bit_length()))]
@@ -195,7 +194,10 @@
     )
     packed = call(
         functools.partial(pack_body, seg),
-        [jax.ShapeDtypeStruct((columns, width // 4), incident.dtype)] * 2,
+        [
+            jax.ShapeDtypeStruct((columns, count * PLACES * seg), incident.dtype)
+            for count in (1, clusters - 1)
+        ],
         [SMEM, VMEM],
         "pack",
         moved=3 * columns * width,
@@ -204,12 +206,10 @@
     slots = block_slot
     for stage in stages:
         slots = double(slots, stage)
-    v_far, slots = lax.optimization_barrier((v_far, slots))
+    v_far, slots, x_low = lax.optimization_barrier((v_far, slots, x_other[0]))
     v_ends = move(v_far, ends)
     u_first = after(u_factors, v_near, v_middle, v_ends)
-    u_side = across(after(u_factors, *x_other))
-    u_far = [move(u_first[part], far) for part in (slice(0, early), slice(early, capacity))]
-    u_ends = [move(part, ends) for part in u_far]
+    u_far = move(u_first, far)
 
     partial, sent = call(
         functools.partial(compress_body, seg),
@@ -222,10 +222,10 @@
         flops=4 * blocks * columns * seg * PLACES * rank_max,
         moved=3 * columns * width + 2 * PLACES * v_factors.size,
         scratch=[pltpu.VMEM((columns, width // 2), incident.dtype)],
-    )(position, block_source, incident, *x_other, v_factors, v_near, v_far, v_middle, v_ends)
+    )(position, block_source, incident, x_low, x_other[1], v_factors, v_near, v_far, v_middle, v_ends)
     received = across(sent)
-    u_next = after(u_factors, received)
-    u_near, u_middle = move(u_next, near), move(u_next, middle)
+    u_side = across(after(u_factors, received))
+    u_near, u_middle = move(u_first, near), move(u_first, middle)
 
     rank_index = lax.broadcasted_iota(jnp.int32, (blocks, 1, 1, rank_max), 3)
     rows = jnp.where(
@@ -240,6 +240,7 @@
             0, rounds, lambda _, array, stage=stage: swapped(array, stage), gathered
         )
         gathered = jnp.concatenate([gathered, other], axis=0)
+    u_ends = move(after(u_far, gathered), ends)
     wanted = owner * capacity + lax.broadcasted_iota(jnp.int32, (capacity, slots.shape[0]), 0)
     order = lax.broadcasted_iota(jnp.int32, (capacity, slots.shape[0]), 1)
     feeding = jnp.max(jnp.where(wanted == slots[None, :], order, -1), axis=1)
@@ -264,8 +265,8 @@
     )(position, slot_rows, u_factors, u_side)
     arrivals = {
         1: ([u_near], [[0]]),
-        2: (u_far, [[0, 1]]),
-        3: ([u_middle, *u_ends], [[0], [1, 2]]),
+        2: ([u_far], [[0]]),
+        3: ([u_middle, u_ends], [[0], [1]]),
     }
     finished = []
     for step, (shards, choices) in arrivals.items():
@@ -355,6 +356,7 @@
         lax.axis_size("rhs") == 2 * PLACES
         and v_factors.shape[1] % 128 == 0
         and owners > 1
+        and incident.shape[1] > v_factors.shape[1] * 2 * PLACES
         and owners & (owners - 1) == 0
     )
     return (paired if fits else gathered_plan)(incident, v_factors, *rest)

time: 91.5 us -> 98.2 us (1.073)
  the two profiles are of different devices: /device:TPU:26 before, /device:TPU:0 now
where the time goes in v5:
time: 98.2 us; the launch traced here: 97.9 us
  waiting for transfers between devices  56.6 us (58%)
  starting transfers between devices  23.4 us (24%)
  Pallas kernels  11.7 us (12%)
  local copies, waits for them, and re-layouts  3.96 us (4%)
  other arithmetic  1.89 us (2%)
    ppermute x8, waiting for transfers between devices, move(): lax.ppermute(array, 'rhs', [(2 * a + i, 2 * b + i) for a, b in pairs for...  24.1 us
    ppermute x7, waiting for transfers between devices, across(): return lax.ppermute(array, 'rhs', [(p, p ^ 1) for p in range(2 * PLACES)])  22.3 us
    ppermute x8, starting transfers between devices, move(): lax.ppermute(array, 'rhs', [(2 * a + i, 2 * b + i) for a, b in pairs for...  12.4 us
    ppermute x4, waiting for transfers between devices, swapped(): return lax.ppermute(array, 'clus', [(p, p ^ stage) for p in range(owners)])  10.2 us
    ppermute x7, starting transfers between devices, across(): return lax.ppermute(array, 'rhs', [(p, p ^ 1) for p in range(2 * PLACES)])  7.95 us
    pallas_call x3, Pallas kernels, paired(): call(functools.partial(expand_body, seg, columns, choices), [chunk, chunk...  5.48 us
    unnamed x21, local copies, waits for them, and re-layouts  3.91 us
    ppermute x4, starting transfers between devices, swapped(): return lax.ppermute(array, 'clus', [(p, p ^ stage) for p in range(owners)])  3.04 us
  transfers between devices with their start and end apart: 19, of which 11 were waited for; matrix products, arithmetic and copies ran while one was open for 2% of the time, Pallas kernels for 9%

profile of v5, /device:TPU:0, one launch (start us, length us, event | category | flops | bytes accessed | tf_op | source)
XLA Modules:
  0.0 97.9 jit_solution(5586157929296935485)
XLA Ops:
  0.0 4.0 %collective-permute-start.2 = (bf16[5,256,128]{2,1,0:T(8,128)(2,1)}, bf16[5,256,128]{2,1,0:T(8,128)(2,1)S(1)}, u32[]{:S(2)}, u32[]{:S(2)}) collective-permute-start(bf16[5,256,128]{2,1,0:T(8,128)(2,1)} %refs_0_.1), channel_id=1, source_target_pairs={{0,16},{4,20},{8,24},{12,28},{16,0},{20,4},{24,8},{28,12},{1,17},{... | collective-permute-start | bytes 983048 | tf_op jit(solution)/shard_map/ppermute | solution.py:172
  4.1 1.5 %copy-done = bf16[104,8192]{1,0:T(8,128)(2,1)S(1)} copy-done((bf16[104,8192]{1,0:T(8,128)(2,1)S(1)}, bf16[104,8192]{1,0:T(8,128)(2,1)}, u32[]{:S(2)}) %copy-start) | copy-done | bytes 1703960
  6.2 1.6 %collective-permute-start.6 = (bf16[104,3072]{1,0:T(8,128)(2,1)S(1)}, bf16[104,3072]{1,0:T(8,128)(2,1)S(1)}, u32[]{:S(2)}, u32[]{:S(2)}) collective-permute-start(bf16[104,3072]{1,0:T(8,128)(2,1)S(1)} %get-tuple-element.63), channel_id=1, source_target_pairs={{0,4},{4,0},{8,12},{12,8},{16,20},{20,16},{24,28},{28,24},{1,5},{5... | collective-permute-start | bytes 1916936 | tf_op jit(solution)/shard_map/ppermute | solution.py:175
  7.8 1.6 %collective-permute-start.7 = (bf16[5,256,128]{2,1,0:T(8,128)(2,1)}, bf16[5,256,128]{2,1,0:T(8,128)(2,1)S(1)}, u32[]{:S(2)}, u32[]{:S(2)}) collective-permute-start(bf16[5,256,128]{2,1,0:T(8,128)(2,1)} %refs_0_.1), channel_id=1, source_target_pairs={{0,8},{4,12},{8,0},{12,4},{16,24},{20,28},{24,16},{28,20},{1,9},{5... | collective-permute-start | bytes 983048 | tf_op jit(solution)/shard_map/ppermute | solution.py:172
  9.9 1.5 %collective-permute-start.3 = (s32[5]{0:T(128)S(1)}, s32[5]{0:T(128)S(1)}, u32[]{:S(2)}, u32[]{:S(2)}) collective-permute-start(s32[5]{0:T(128)S(1)} %copy-done.8), channel_id=1, source_target_pairs={{0,2},{1,3},{2,0},{3,1},{4,6},{5,7},{6,4},{7,5},{8,10},{9,11},{10,... | collective-permute-start | bytes 68 | tf_op jit(solution)/shard_map/ppermute | solution.py:185
  11.4 2.0 %collective-permute-done.3 = s32[5]{0:T(128)S(1)} collective-permute-done((s32[5]{0:T(128)S(1)}, s32[5]{0:T(128)S(1)}, u32[]{:S(2)}, u32[]{:S(2)}) %collective-permute-start.3) | collective-permute-done | bytes 52 | tf_op jit(solution)/shard_map/ppermute | solution.py:185
  15.5 11.2 %collective-permute-done.5.xl_ref = bf16[104,1024]{1,0:T(8,128)(2,1)S(1)} collective-permute-done((bf16[104,1024]{1,0:T(8,128)(2,1)S(1)}, bf16[104,1024]{1,0:T(8,128)(2,1)S(1)}, u32[]{:S(2)}, u32[]{:S(2)}) %collective-permute-start.5) | collective-permute-done | bytes 213024 | tf_op jit(solution)/shard_map/ppermute | solution.py:175
  26.7 1.3 %collective-permute-start.9 = (bf16[5,256,128]{2,1,0:T(8,128)(2,1)S(1)}, bf16[5,256,128]{2,1,0:T(8,128)(2,1)S(1)}, u32[]{:S(2)}, u32[]{:S(2)}) collective-permute-start(bf16[5,256,128]{2,1,0:T(8,128)(2,1)S(1)} %collective-permute-done.2.refs_2_), channel_id=1, source_target_pairs={{8,0},{12,4},{16,24},{20,28},{9,1},{13,5},{17,25},{21,29},{10,2},{... | collective-permute-start | bytes 983048 | tf_op jit(solution)/shard_map/ppermute | solution.py:172
  28.0 8.8 %collective-permute-done.9.refs_4_ = bf16[5,256,128]{2,1,0:T(8,128)(2,1)S(1)} collective-permute-done((bf16[5,256,128]{2,1,0:T(8,128)(2,1)S(1)}, bf16[5,256,128]{2,1,0:T(8,128)(2,1)S(1)}, u32[]{:S(2)}, u32[]{:S(2)}) %collective-permute-start.9) | collective-permute-done | bytes 327712 | tf_op jit(solution)/shard_map/ppermute | solution.py:172
  37.8 1.4 %compress.1 = (f32[5,2,112,128]{3,2,1,0:T(8,128)S(1)}, bf16[5,2,112,128]{3,2,1,0:T(8,128)(2,1)S(1)}) custom-call(s32[2]{0:T(128)S(1)} %pad_add_fusion.pos_ref, s32[5]{0:T(128)S(1)} %copy-done.4, bf16[104,8192]{1,0:T(8,128)(2,1)S(1)} %copy-done.1, bf16[104,1024]{1,0:T(8,128)(2,1)S(1)} %collective-permute-done.5.xl_ref, ...), custom_call_target="tpu_custom_call" | custom-call | flops 272629760 | bytes 3866624 | tf_op jit(solution)/shard_map/compress/pallas_call | solution.py:214
  39.3 1.6 %collective-permute-start.10 = (bf16[5,2,112,128]{3,2,1,0:T(8,128)(2,1)S(1)}, bf16[5,2,112,128]{3,2,1,0:T(8,128)(2,1)S(1)}, u32[]{:S(2)}, u32[]{:S(2)}) collective-permute-start(bf16[5,2,112,128]{3,2,1,0:T(8,128)(2,1)S(1)} %get-tuple-element.66), channel_id=1, source_target_pairs={{0,4},{4,0},{8,12},{12,8},{16,20},{20,16},{24,28},{28,24},{1,5},{5... | collective-permute-start | bytes 860168 | tf_op jit(solution)/shard_map/ppermute | solution.py:175
  40.9 1.9 %collective-permute-start.12 = (bf16[10,256,128]{2,1,0:T(8,128)(2,1)S(1)}, bf16[10,256,128]{2,1,0:T(8,128)(2,1)}, u32[]{:S(2)}, u32[]{:S(2)}) collective-permute-start(bf16[10,256,128]{2,1,0:T(8,128)(2,1)S(1)} %copy-done.2), channel_id=1, source_target_pairs={{0,8},{4,12},{8,0},{12,4},{16,24},{20,28},{24,16},{28,20},{1,9},{5... | collective-permute-start | bytes 1966088 | tf_op jit(solution)/shard_map/ppermute | solution.py:172
  42.8 1.5 %collective-permute-start.15 = (bf16[10,256,128]{2,1,0:T(8,128)(2,1)S(1)}, bf16[10,256,128]{2,1,0:T(8,128)(2,1)}, u32[]{:S(2)}, u32[]{:S(2)}) collective-permute-start(bf16[10,256,128]{2,1,0:T(8,128)(2,1)S(1)} %copy-done.2), channel_id=1, source_target_pairs={{8,16},{12,20},{16,8},{20,12},{9,17},{13,21},{17,9},{21,13},{10,18... | collective-permute-start | bytes 1966088 | tf_op jit(solution)/shard_map/ppermute | solution.py:172
  44.4 2.2 %collective-permute-done.10 = bf16[5,2,112,128]{3,2,1,0:T(8,128)(2,1)S(1)} collective-permute-done((bf16[5,2,112,128]{3,2,1,0:T(8,128)(2,1)S(1)}, bf16[5,2,112,128]{3,2,1,0:T(8,128)(2,1)S(1)}, u32[]{:S(2)}, u32[]{:S(2)}) %collective-permute-start.10) | collective-permute-done | bytes 286752 | tf_op jit(solution)/shard_map/ppermute | solution.py:175
  46.7 1.6 %collective-permute-start.11 = (bf16[10,256,128]{2,1,0:T(8,128)(2,1)S(1)}, bf16[10,256,128]{2,1,0:T(8,128)(2,1)S(1)}, u32[]{:S(2)}, u32[]{:S(2)}) collective-permute-start(bf16[10,256,128]{2,1,0:T(8,128)(2,1)S(1)} %copy-done.2), channel_id=1, source_target_pairs={{0,4},{4,0},{8,12},{12,8},{16,20},{20,16},{24,28},{28,24},{1,5},{5... | collective-permute-start | bytes 1966088 | tf_op jit(solution)/shard_map/ppermute | solution.py:175
  48.2 6.7 %while.20 = (s32[]{:T(128)}, bf16[5,2,112,128]{3,2,1,0:T(8,128)(2,1)S(1)}, s32[]{:T(128)}, s32[]{:T(128)}) while((s32[]{:T(128)}, bf16[5,2,112,128]{3,2,1,0:T(8,128)(2,1)S(1)}, s32[]{:T(128)}, s32[]{:T(128)}) %tuple.45), condition=%wide.region_2.3_spmd, body=%wide.region_1.2_spmd.sunk | while | flops 2 | bytes 1720413 | solution.py:239
  48.2 1.5 %collective-permute-start = (bf16[5,2,112,128]{3,2,1,0:T(8,128)(2,1)S(1)}, bf16[5,2,112,128]{3,2,1,0:T(8,128)(2,1)S(1)}, u32[]{:S(2)}, u32[]{:S(2)}) collective-permute-start(bf16[5,2,112,128]{3,2,1,0:T(8,128)(2,1)S(1)} %get-tuple-element.138), channel_id=1, source_target_pairs={{0,2},{1,3},{2,0},{3,1},{4,6},{5,7},{6,4},{7,5},{8,10},{9,11},{10,... | collective-permute-start | bytes 860168 | tf_op jit(solution)/shard_map/while/body/ppermute | solution.py:185
  49.7 5.1 %collective-permute-done = bf16[5,2,112,128]{3,2,1,0:T(8,128)(2,1)S(1)} collective-permute-done((bf16[5,2,112,128]{3,2,1,0:T(8,128)(2,1)S(1)}, bf16[5,2,112,128]{3,2,1,0:T(8,128)(2,1)S(1)}, u32[]{:S(2)}, u32[]{:S(2)}) %collective-permute-start) | collective-permute-done | bytes 286752 | tf_op jit(solution)/shard_map/while/body/ppermute | solution.py:185
  55.6 2.0 %while.21 = (s32[]{:T(128)}, bf16[10,2,112,128]{3,2,1,0:T(8,128)(2,1)S(1)}, s32[]{:T(128)}, s32[]{:T(128)}) while((s32[]{:T(128)}, bf16[10,2,112,128]{3,2,1,0:T(8,128)(2,1)S(1)}, s32[]{:T(128)}, s32[]{:T(128)}) %tuple.48), condition=%wide.region_4.5_spmd, body=%wide.region_3.4_spmd.sunk | while | flops 2 | bytes 3440733 | solution.py:239
  55.6 2.0 %collective-permute-done.1 = bf16[10,2,112,128]{3,2,1,0:T(8,128)(2,1)S(1)} collective-permute-done((bf16[10,2,112,128]{3,2,1,0:T(8,128)(2,1)S(1)}, bf16[10,2,112,128]{3,2,1,0:T(8,128)(2,1)S(1)}, u32[]{:S(2)}, u32[]{:S(2)}) %collective-permute-start.1) | collective-permute-done | bytes 573472 | tf_op jit(solution)/shard_map/while/body/ppermute | solution.py:185
  58.4 1.3 %pad_maximum_fusion.comp_ref = bf16[20,2,112,128]{3,2,1,0:T(8,128)(2,1)S(1)} fusion(bf16[10,2,112,128]{3,2,1,0:T(8,128)(2,1)} %copy-done.7, bf16[5,2,112,128]{3,2,1,0:T(8,128)(2,1)} %copy-done.6, bf16[5,2,112,128]{3,2,1,0:T(8,128)(2,1)S(1)} %select_convert_fusion), kind=kLoop, calls=%fused_computation | loop fusion | flops 1146880 | bytes 2293760 | tf_op jit(solution)/shard_map/concatenate | solution.py:242
  59.7 9.3 %collective-permute-done.13.refs_0_ = bf16[10,256,128]{2,1,0:T(8,128)(2,1)S(1)} collective-permute-done((bf16[10,256,128]{2,1,0:T(8,128)(2,1)S(1)}, bf16[10,256,128]{2,1,0:T(8,128)(2,1)S(1)}, u32[]{:S(2)}, u32[]{:S(2)}) %collective-permute-start.13) | collective-permute-done | bytes 655392 | tf_op jit(solution)/shard_map/ppermute | solution.py:172
  69.0 1.3 %collective-permute-start.16 = (bf16[10,256,128]{2,1,0:T(8,128)(2,1)S(1)}, bf16[10,256,128]{2,1,0:T(8,128)(2,1)}, u32[]{:S(2)}, u32[]{:S(2)}) collective-permute-start(bf16[10,256,128]{2,1,0:T(8,128)(2,1)S(1)} %collective-permute-done.13.refs_0_), channel_id=1, source_target_pairs={{8,0},{12,4},{16,24},{20,28},{9,1},{13,5},{17,25},{21,29},{10,2},{... | collective-permute-start | bytes 1966088 | tf_op jit(solution)/shard_map/ppermute | solution.py:172
  71.4 1.9 %expand.3 = (bf16[104,1024]{1,0:T(8,128)(2,1)S(1)}, bf16[104,1024]{1,0:T(8,128)(2,1)S(1)}) custom-call(s32[2]{0:T(128)S(1)} %pad_add_fusion.pos_ref, bf16[4,2,112,1280]{3,2,1,0:T(8,128)(2,1)S(1)} %land.1.rows_ref, bf16[10,256,128]{2,1,0:T(8,128)(2,1)} %collective-permute-done.12.refs_0_), custom_call_target="tpu_custom_call" | custom-call | flops 545259520 | bytes 3375104 | tf_op jit(solution)/shard_map/expand/pallas_call | solution.py:277
  74.0 1.4 %expand.4 = (bf16[104,1024]{1,0:T(8,128)(2,1)S(1)}, bf16[104,1024]{1,0:T(8,128)(2,1)S(1)}) custom-call(s32[2]{0:T(128)S(1)} %pad_add_fusion.pos_ref, bf16[4,2,112,1280]{3,2,1,0:T(8,128)(2,1)S(1)} %land.1.rows_ref, bf16[10,256,128]{2,1,0:T(8,128)(2,1)S(1)} %collective-permute-done.13.refs_0_), custom_call_target="tpu_custom_call" | custom-call | flops 545259520 | bytes 3375104 | tf_op jit(solution)/shard_map/expand/pallas_call | solution.py:277
  75.4 1.6 %collective-permute-start.17 = (bf16[104,1024]{1,0:T(8,128)(2,1)S(1)}, bf16[104,1024]{1,0:T(8,128)(2,1)S(1)}, u32[]{:S(2)}, u32[]{:S(2)}) collective-permute-start(bf16[104,1024]{1,0:T(8,128)(2,1)S(1)} %get-tuple-element.79), channel_id=1, source_target_pairs={{0,4},{4,0},{8,12},{12,8},{16,20},{20,16},{24,28},{28,24},{1,5},{5... | collective-permute-start | bytes 638984 | tf_op jit(solution)/shard_map/ppermute | solution.py:175
  76.9 1.3 %expand_own.1.first_ref = bf16[104,2048]{1,0:T(8,128)(2,1)S(1)} custom-call(s32[2]{0:T(128)S(1)} %pad_add_fusion.pos_ref, bf16[4,2,112,1280]{3,2,1,0:T(8,128)(2,1)S(1)} %land.1.rows_ref, bf16[10,256,128]{2,1,0:T(8,128)(2,1)S(1)} %copy-done.2, bf16[10,256,128]{2,1,0:T(8,128)(2,1)S(1)} %collective-permute-done.11.side_ref), custom_call_target="tpu_custom_call" | custom-call | flops 545259520 | bytes 4030464 | tf_op jit(solution)/shard_map/expand_own/pallas_call | solution.py:257
  78.3 3.3 %collective-permute-done.14.refs_3_ = bf16[104,1024]{1,0:T(8,128)(2,1)S(1)} collective-permute-done((bf16[104,1024]{1,0:T(8,128)(2,1)S(1)}, bf16[104,1024]{1,0:T(8,128)(2,1)S(1)}, u32[]{:S(2)}, u32[]{:S(2)}) %collective-permute-start.14) | collective-permute-done | bytes 213024 | tf_op jit(solution)/shard_map/ppermute | solution.py:175
  81.6 6.0 %collective-permute-done.16.refs_1_ = bf16[10,256,128]{2,1,0:T(8,128)(2,1)} collective-permute-done((bf16[10,256,128]{2,1,0:T(8,128)(2,1)S(1)}, bf16[10,256,128]{2,1,0:T(8,128)(2,1)}, u32[]{:S(2)}, u32[]{:S(2)}) %collective-permute-start.16) | collective-permute-done | bytes 655392 | tf_op jit(solution)/shard_map/ppermute | solution.py:172
  87.5 2.1 %expand.5 = (bf16[104,1024]{1,0:T(8,128)(2,1)S(1)}, bf16[104,1024]{1,0:T(8,128)(2,1)S(1)}) custom-call(s32[2]{0:T(128)S(1)} %pad_add_fusion.pos_ref, bf16[4,2,112,1280]{3,2,1,0:T(8,128)(2,1)S(1)} %land.1.rows_ref, bf16[10,256,128]{2,1,0:T(8,128)(2,1)} %collective-permute-done.15.refs_0_, bf16[10,256,128]{2,1,0:T(8,128)(2,1)} %collective-permute-done.16.refs_1_), custom_call_target="tpu_custom_call" | custom-call | flops 545259520 | bytes 3375104 | tf_op jit(solution)/shard_map/expand/pallas_call | solution.py:277
  90.3 5.7 %collective-permute-done.18.refs_5_ = bf16[104,1024]{1,0:T(8,128)(2,1)S(1)} collective-permute-done((bf16[104,1024]{1,0:T(8,128)(2,1)S(1)}, bf16[104,1024]{1,0:T(8,128)(2,1)S(1)}, u32[]{:S(2)}, u32[]{:S(2)}) %collective-permute-start.18) | collective-permute-done | bytes 213024 | tf_op jit(solution)/shard_map/ppermute | solution.py:175
  96.0 1.9 %join.1 = bf16[104,8192]{1,0:T(8,128)(2,1)} custom-call(s32[2]{0:T(128)S(1)} %pad_add_fusion.pos_ref, bf16[104,2048]{1,0:T(8,128)(2,1)S(1)} %expand_own.1.first_ref, bf16[104,1024]{1,0:T(8,128)(2,1)S(1)} %get-tuple-element.71.refs_0_, bf16[104,1024]{1,0:T(8,128)(2,1)S(1)} %get-tuple-element.73.refs_1_, bf16[104,1024]{1,0:T(8,128)(2,1)S(1)} %get-tuple-element.78.refs_2_, ...), custom_call_target="tpu_custom_call" | custom-call | bytes 3407872 | tf_op jit(solution)/shard_map/join/pallas_call | solution.py:288
  (48 shorter events, 8.4 us)
Async XLA Ops:
  0.0 9.9 %copy-start.8 = (s32[5]{0:T(128)S(1)}, s32[5]{0:T(128)}, u32[]{:S(2)}) copy-start(s32[5]{0:T(128)} %param.16) | copy-start | bytes 64
  0.0 36.9 %copy-start.4 = (s32[5]{0:T(128)S(1)}, s32[5]{0:T(128)}, u32[]{:S(2)}) copy-start(s32[5]{0:T(128)} %source_ref.1) | copy-start | bytes 64
  0.0 26.7 %collective-permute-start.2 = (bf16[5,256,128]{2,1,0:T(8,128)(2,1)}, bf16[5,256,128]{2,1,0:T(8,128)(2,1)S(1)}, u32[]{:S(2)}, u32[]{:S(2)}) collective-permute-start(bf16[5,256,128]{2,1,0:T(8,128)(2,1)} %refs_0_.1), channel_id=1, source_target_pairs={{0,16},{4,20},{8,24},{12,28},{16,0},{20,4},{24,8},{28,12},{1,17},{... | collective-permute-start | bytes 983048 | tf_op jit(solution)/shard_map/ppermute | solution.py:172
  4.1 1.5 %copy-start = (bf16[104,8192]{1,0:T(8,128)(2,1)S(1)}, bf16[104,8192]{1,0:T(8,128)(2,1)}, u32[]{:S(2)}) copy-start(bf16[104,8192]{1,0:T(8,128)(2,1)} %x_ref.3) | copy-start | bytes 5111812
  5.6 31.3 %copy-start.1 = (bf16[104,8192]{1,0:T(8,128)(2,1)S(1)}, bf16[104,8192]{1,0:T(8,128)(2,1)}, u32[]{:S(2)}) copy-start(bf16[104,8192]{1,0:T(8,128)(2,1)} %x_ref.3) | copy-start | bytes 5111812
  6.2 21.8 %collective-permute-start.6 = (bf16[104,3072]{1,0:T(8,128)(2,1)S(1)}, bf16[104,3072]{1,0:T(8,128)(2,1)S(1)}, u32[]{:S(2)}, u32[]{:S(2)}) collective-permute-start(bf16[104,3072]{1,0:T(8,128)(2,1)S(1)} %get-tuple-element.63), channel_id=1, source_target_pairs={{0,4},{4,0},{8,12},{12,8},{16,20},{20,16},{24,28},{28,24},{1,5},{5... | collective-permute-start | bytes 1916936 | tf_op jit(solution)/shard_map/ppermute | solution.py:175
  7.8 20.2 %collective-permute-start.7 = (bf16[5,256,128]{2,1,0:T(8,128)(2,1)}, bf16[5,256,128]{2,1,0:T(8,128)(2,1)S(1)}, u32[]{:S(2)}, u32[]{:S(2)}) collective-permute-start(bf16[5,256,128]{2,1,0:T(8,128)(2,1)} %refs_0_.1), channel_id=1, source_target_pairs={{0,8},{4,12},{8,0},{12,4},{16,24},{20,28},{24,16},{28,20},{1,9},{5... | collective-permute-start | bytes 983048 | tf_op jit(solution)/shard_map/ppermute | solution.py:172
  9.4 17.3 %collective-permute-start.5 = (bf16[104,1024]{1,0:T(8,128)(2,1)S(1)}, bf16[104,1024]{1,0:T(8,128)(2,1)S(1)}, u32[]{:S(2)}, u32[]{:S(2)}) collective-permute-start(bf16[104,1024]{1,0:T(8,128)(2,1)S(1)} %get-tuple-element.60), channel_id=1, source_target_pairs={{0,4},{4,0},{8,12},{12,8},{16,20},{20,16},{24,28},{28,24},{1,5},{5... | collective-permute-start | bytes 638984 | tf_op jit(solution)/shard_map/ppermute | solution.py:175
  9.9 3.5 %collective-permute-start.3 = (s32[5]{0:T(128)S(1)}, s32[5]{0:T(128)S(1)}, u32[]{:S(2)}, u32[]{:S(2)}) collective-permute-start(s32[5]{0:T(128)S(1)} %copy-done.8), channel_id=1, source_target_pairs={{0,2},{1,3},{2,0},{3,1},{4,6},{5,7},{6,4},{7,5},{8,10},{9,11},{10,... | collective-permute-start | bytes 68 | tf_op jit(solution)/shard_map/ppermute | solution.py:185
  13.5 1.1 %collective-permute-start.4 = (s32[10]{0:T(128)S(1)}, s32[10]{0:T(128)S(1)}, u32[]{:S(2)}, u32[]{:S(2)}) collective-permute-start(s32[10]{0:T(128)S(1)} %pad_add_fusion.1), channel_id=1, source_target_pairs={{0,1},{1,0},{2,3},{3,2},{4,5},{5,4},{6,7},{7,6},{8,9},{9,8},{10,11... | collective-permute-start | bytes 128 | tf_op jit(solution)/shard_map/ppermute | solution.py:185
  14.6 26.2 %copy-start.9 = (s32[5]{0:T(128)S(1)}, s32[5]{0:T(128)}, u32[]{:S(2)}) copy-start(s32[5]{0:T(128)} %param.15) | copy-start | bytes 64
  14.7 26.1 %copy-start.2 = (bf16[10,256,128]{2,1,0:T(8,128)(2,1)S(1)}, bf16[10,256,128]{2,1,0:T(8,128)(2,1)}, u32[]{:S(2)}) copy-start(bf16[10,256,128]{2,1,0:T(8,128)(2,1)} %u_ref.1) | copy-start | bytes 1966084
  14.7 13.3 %collective-permute-start.8 = (bf16[5,256,128]{2,1,0:T(8,128)(2,1)}, bf16[5,256,128]{2,1,0:T(8,128)(2,1)S(1)}, u32[]{:S(2)}, u32[]{:S(2)}) collective-permute-start(bf16[5,256,128]{2,1,0:T(8,128)(2,1)} %refs_0_.1), channel_id=1, source_target_pairs={{8,16},{12,20},{16,8},{20,12},{9,17},{13,21},{17,9},{21,13},{10,18... | collective-permute-start | bytes 983048 | tf_op jit(solution)/shard_map/ppermute | solution.py:172
  26.7 10.1 %collective-permute-start.9 = (bf16[5,256,128]{2,1,0:T(8,128)(2,1)S(1)}, bf16[5,256,128]{2,1,0:T(8,128)(2,1)S(1)}, u32[]{:S(2)}, u32[]{:S(2)}) collective-permute-start(bf16[5,256,128]{2,1,0:T(8,128)(2,1)S(1)} %collective-permute-done.2.refs_2_), channel_id=1, source_target_pairs={{8,0},{12,4},{16,24},{20,28},{9,1},{13,5},{17,25},{21,29},{10,2},{... | collective-permute-start | bytes 983048 | tf_op jit(solution)/shard_map/ppermute | solution.py:172
  36.9 1.0 copy-start.3
  39.3 7.3 %collective-permute-start.10 = (bf16[5,2,112,128]{3,2,1,0:T(8,128)(2,1)S(1)}, bf16[5,2,112,128]{3,2,1,0:T(8,128)(2,1)S(1)}, u32[]{:S(2)}, u32[]{:S(2)}) collective-permute-start(bf16[5,2,112,128]{3,2,1,0:T(8,128)(2,1)S(1)} %get-tuple-element.66), channel_id=1, source_target_pairs={{0,4},{4,0},{8,12},{12,8},{16,20},{20,16},{24,28},{28,24},{1,5},{5... | collective-permute-start | bytes 860168 | tf_op jit(solution)/shard_map/ppermute | solution.py:175
  40.8 28.1 %collective-permute-start.13 = (bf16[10,256,128]{2,1,0:T(8,128)(2,1)S(1)}, bf16[10,256,128]{2,1,0:T(8,128)(2,1)S(1)}, u32[]{:S(2)}, u32[]{:S(2)}) collective-permute-start(bf16[10,256,128]{2,1,0:T(8,128)(2,1)S(1)} %copy-done.2), channel_id=1, source_target_pairs={{0,16},{4,20},{8,24},{12,28},{16,0},{20,4},{24,8},{28,12},{1,17},{... | collective-permute-start | bytes 1966088 | tf_op jit(solution)/shard_map/ppermute | solution.py:172
  40.9 30.5 %collective-permute-start.12 = (bf16[10,256,128]{2,1,0:T(8,128)(2,1)S(1)}, bf16[10,256,128]{2,1,0:T(8,128)(2,1)}, u32[]{:S(2)}, u32[]{:S(2)}) collective-permute-start(bf16[10,256,128]{2,1,0:T(8,128)(2,1)S(1)} %copy-done.2), channel_id=1, source_target_pairs={{0,8},{4,12},{8,0},{12,4},{16,24},{20,28},{24,16},{28,20},{1,9},{5... | collective-permute-start | bytes 1966088 | tf_op jit(solution)/shard_map/ppermute | solution.py:172
  42.8 38.7 %collective-permute-start.15 = (bf16[10,256,128]{2,1,0:T(8,128)(2,1)S(1)}, bf16[10,256,128]{2,1,0:T(8,128)(2,1)}, u32[]{:S(2)}, u32[]{:S(2)}) collective-permute-start(bf16[10,256,128]{2,1,0:T(8,128)(2,1)S(1)} %copy-done.2), channel_id=1, source_target_pairs={{8,16},{12,20},{16,8},{20,12},{9,17},{13,21},{17,9},{21,13},{10,18... | collective-permute-start | bytes 1966088 | tf_op jit(solution)/shard_map/ppermute | solution.py:172
  46.7 30.2 %collective-permute-start.11 = (bf16[10,256,128]{2,1,0:T(8,128)(2,1)S(1)}, bf16[10,256,128]{2,1,0:T(8,128)(2,1)S(1)}, u32[]{:S(2)}, u32[]{:S(2)}) collective-permute-start(bf16[10,256,128]{2,1,0:T(8,128)(2,1)S(1)} %copy-done.2), channel_id=1, source_target_pairs={{0,4},{4,0},{8,12},{12,8},{16,20},{20,16},{24,28},{28,24},{1,5},{5... | collective-permute-start | bytes 1966088 | tf_op jit(solution)/shard_map/ppermute | solution.py:175
  48.2 6.6 %collective-permute-start = (bf16[5,2,112,128]{3,2,1,0:T(8,128)(2,1)S(1)}, bf16[5,2,112,128]{3,2,1,0:T(8,128)(2,1)S(1)}, u32[]{:S(2)}, u32[]{:S(2)}) collective-permute-start(bf16[5,2,112,128]{3,2,1,0:T(8,128)(2,1)S(1)} %get-tuple-element.138), channel_id=1, source_target_pairs={{0,2},{1,3},{2,0},{3,1},{4,6},{5,7},{6,4},{7,5},{8,10},{9,11},{10,... | collective-permute-start | bytes 860168 | tf_op jit(solution)/shard_map/while/body/ppermute | solution.py:185
  54.9 0.7 copy-start.6
  55.6 2.0 %collective-permute-start.1 = (bf16[10,2,112,128]{3,2,1,0:T(8,128)(2,1)S(1)}, bf16[10,2,112,128]{3,2,1,0:T(8,128)(2,1)S(1)}, u32[]{:S(2)}, u32[]{:S(2)}) collective-permute-start(bf16[10,2,112,128]{3,2,1,0:T(8,128)(2,1)S(1)} %get-tuple-element.150), channel_id=1, source_target_pairs={{0,1},{1,0},{2,3},{3,2},{4,5},{5,4},{6,7},{7,6},{8,9},{9,8},{10,11... | collective-permute-start | bytes 1720328 | tf_op jit(solution)/shard_map/while/body/ppermute | solution.py:185
  57.6 0.8 copy-start.7
  58.4 12.0 %copy-start.5 = (s32[10]{0:T(128)S(1)}, s32[10]{0:T(128)}, u32[]{:S(2)}) copy-start(s32[10]{0:T(128)} %target_ref.1) | copy-start | bytes 124
  69.0 18.5 %collective-permute-start.16 = (bf16[10,256,128]{2,1,0:T(8,128)(2,1)S(1)}, bf16[10,256,128]{2,1,0:T(8,128)(2,1)}, u32[]{:S(2)}, u32[]{:S(2)}) collective-permute-start(bf16[10,256,128]{2,1,0:T(8,128)(2,1)S(1)} %collective-permute-done.13.refs_0_), channel_id=1, source_target_pairs={{8,0},{12,4},{16,24},{20,28},{9,1},{13,5},{17,25},{21,29},{10,2},{... | collective-permute-start | bytes 1966088 | tf_op jit(solution)/shard_map/ppermute | solution.py:172
  73.4 8.2 %collective-permute-start.14 = (bf16[104,1024]{1,0:T(8,128)(2,1)S(1)}, bf16[104,1024]{1,0:T(8,128)(2,1)S(1)}, u32[]{:S(2)}, u32[]{:S(2)}) collective-permute-start(bf16[104,1024]{1,0:T(8,128)(2,1)S(1)} %get-tuple-element.75), channel_id=1, source_target_pairs={{0,4},{4,0},{8,12},{12,8},{16,20},{20,16},{24,28},{28,24},{1,5},{5... | collective-permute-start | bytes 638984 | tf_op jit(solution)/shard_map/ppermute | solution.py:175
  75.4 14.9 %collective-permute-start.17 = (bf16[104,1024]{1,0:T(8,128)(2,1)S(1)}, bf16[104,1024]{1,0:T(8,128)(2,1)S(1)}, u32[]{:S(2)}, u32[]{:S(2)}) collective-permute-start(bf16[104,1024]{1,0:T(8,128)(2,1)S(1)} %get-tuple-element.79), channel_id=1, source_target_pairs={{0,4},{4,0},{8,12},{12,8},{16,20},{20,16},{24,28},{28,24},{1,5},{5... | collective-permute-start | bytes 638984 | tf_op jit(solution)/shard_map/ppermute | solution.py:175
  89.7 6.3 %collective-permute-start.18 = (bf16[104,1024]{1,0:T(8,128)(2,1)S(1)}, bf16[104,1024]{1,0:T(8,128)(2,1)S(1)}, u32[]{:S(2)}, u32[]{:S(2)}) collective-permute-start(bf16[104,1024]{1,0:T(8,128)(2,1)S(1)} %get-tuple-element.80), channel_id=1, source_target_pairs={{0,4},{4,0},{8,12},{12,8},{16,20},{20,16},{24,28},{28,24},{1,5},{5... | collective-permute-start | bytes 638984 | tf_op jit(solution)/shard_map/ppermute | solution.py:175
